TPU v7x, 128 devices: a whole 4x4x4 slice. The times are simulated.
128 devices in a mesh: seq: 32 (over x, y, core), kv: 4 (over z).
Axes of the slice: x: 4, y: 4, z: 4, core: 2. Of those that a mesh axis runs over, the one named last changes fastest.
Arguments:
- queries: bfloat16 [8192, 4096], P('seq', 'kv'), as said below
- keys: bfloat16 [8192, 1024], P('seq', 'kv'), as said below
- values: bfloat16 [8192, 1024], P('seq', 'kv'), may hold values from -6 to 6
- out_weight: bfloat16 [4096, 4096], P(None, 'kv'), may hold values from -0.09375 to 0.09375
- out_grad: bfloat16 [8192, 4096], P('seq', 'kv'), may hold values from -6 to 6
- doc_lengths: int32 [64], replicated, may hold values from 1 to 768, 8192 in all
Outputs:
- layer_out: bfloat16 [8192, 4096], P('seq', 'kv')
- query_grad: bfloat16 [8192, 4096], P('seq', 'kv')
- key_grad: bfloat16 [8192, 1024], P('seq', 'kv')
- value_grad: bfloat16 [8192, 1024], P('seq', 'kv')
- weight_grad: bfloat16 [4096, 4096], P('seq', 'kv')
Inputs may be any that keep to these rules, and one draw needn't show every extreme that they name: `queries`: every entry lies within -8 to 8. `keys`: every entry lies within -8 to 8. `doc_lengths`: the lengths sum to 8192; the longest document has exactly 768 tokens.
All inputs are finite; a program needn't handle non-finite values.
Results may differ from a plain program's by a relative error of at most 0.03.
Values may be sent and summed in bfloat16 or wider, within the bound.
No kernel may reach another device: no remote copies, remote signals or barrier semaphores. Data moves between devices by JAX's collectives and lax.ppermute only.
A program may use at most 128 MiB of HBM per device.

v0:
```python
import jax
import jax.numpy as jnp
from jax import lax
from jax.sharding import PartitionSpec as P

HEAD_SIZE = 128
REACH = 3


def shifted(block, axis, distance):
    devices = range(lax.axis_size(axis))
    route = [(i - distance, i) for i in devices if i - distance in devices]
    return lax.ppermute(block, axis, route)


def document_of(doc_lengths, positions):
    doc_ends = jnp.cumsum(doc_lengths)
    return jnp.sum((positions[:, None] >= doc_ends[None, :]).astype(jnp.int32), axis=1)


def probabilities(query_heads, key_heads, query_pos, key_pos, doc_lengths):
    scores = jnp.einsum(
        "igkd,jgd->gkij", query_heads, key_heads, preferred_element_type=jnp.float32
    ) * HEAD_SIZE ** (-0.5)
    same_doc = (
        document_of(doc_lengths, query_pos)[:, None] == document_of(doc_lengths, key_pos)[None, :]
    )
    allowed = same_doc & (key_pos[None, :] <= query_pos[:, None]) & (key_pos[None, :] >= 0)
    masked = jnp.where(allowed, scores, -1e30)
    row_max = jnp.max(masked, axis=-1, keepdims=True)
    row_sum = jnp.sum(jnp.exp(masked - row_max), axis=-1, keepdims=True)
    return jnp.exp(masked - (row_max + jnp.log(row_sum)))


def per_device(queries, keys, values, out_weight, out_grad, doc_lengths):
    tok_rows = queries.shape[0]
    key_span = (REACH + 1) * tok_rows
    groups = keys.shape[1] // HEAD_SIZE
    per_group = queries.shape[1] // HEAD_SIZE // groups
    first_row = lax.axis_index("seq") * tok_rows
    query_pos = first_row + jnp.arange(tok_rows, dtype=jnp.int32)
    key_pos = first_row - REACH * tok_rows + jnp.arange(key_span, dtype=jnp.int32)
    kv_pair = jnp.stack([keys, values])
    earlier = []
    moving = kv_pair
    for distance in range(REACH):
        moving = shifted(moving, "seq", 1)
        earlier.append(moving)
    kv_window = jnp.concatenate(earlier[::-1] + [kv_pair], axis=1)
    key_heads = kv_window[0].reshape(key_span, groups, HEAD_SIZE)
    value_heads = kv_window[1].reshape(key_span, groups, HEAD_SIZE)
    query_heads = queries.reshape(tok_rows, groups, per_group, HEAD_SIZE)
    exact_probs = probabilities(query_heads, key_heads, query_pos, key_pos, doc_lengths)
    rounded_probs = exact_probs.astype(jnp.bfloat16)
    attention = (
        jnp.einsum("gkij,jgd->igkd", rounded_probs, value_heads, preferred_element_type=jnp.float32)
        .reshape(tok_rows, -1)
        .astype(jnp.bfloat16)
    )
    partial_out = lax.dot_general(
        attention, out_weight, (((1,), (1,)), ((), ())), preferred_element_type=jnp.float32
    )
    layer_out = lax.psum_scatter(
        partial_out.astype(jnp.bfloat16), "kv", scatter_dimension=1, tiled=True
    )
    full_grad = lax.all_gather(out_grad, "kv", axis=1, tiled=True)
    attn_grad = jnp.dot(full_grad, out_weight, preferred_element_type=jnp.float32).astype(
        jnp.bfloat16
    )
    weight_grad = lax.psum_scatter(
        lax.dot_general(
            full_grad, attention, (((0,), (0,)), ((), ())), preferred_element_type=jnp.float32
        ).astype(jnp.bfloat16),
        "seq",
        scatter_dimension=0,
        tiled=True,
    )
    grad_heads = attn_grad.reshape(tok_rows, groups, per_group, HEAD_SIZE)
    attn_heads = attention.reshape(tok_rows, groups, per_group, HEAD_SIZE)
    row_dots = jnp.sum(
        grad_heads.astype(jnp.float32) * attn_heads.astype(jnp.float32), axis=-1
    ).transpose(1, 2, 0)
    prob_grads = jnp.einsum(
        "igkd,jgd->gkij", grad_heads, value_heads, preferred_element_type=jnp.float32
    )
    score_grads = (exact_probs * (prob_grads - row_dots[..., None]) * HEAD_SIZE ** (-0.5)).astype(
        jnp.bfloat16
    )
    query_grad = (
        jnp.einsum("gkij,jgd->igkd", score_grads, key_heads, preferred_element_type=jnp.float32)
        .reshape(tok_rows, -1)
        .astype(jnp.bfloat16)
    )
    key_terms = jnp.einsum(
        "gkij,igkd->jgd", score_grads, query_heads, preferred_element_type=jnp.float32
    ).reshape(key_span, -1)
    value_terms = jnp.einsum(
        "gkij,igkd->jgd", rounded_probs, grad_heads, preferred_element_type=jnp.float32
    ).reshape(key_span, -1)
    kv_terms = jnp.stack([key_terms, value_terms]).reshape(2, REACH + 1, tok_rows, -1)
    summed = kv_terms[:, 0]
    for distance in range(1, REACH + 1):
        summed = (
            shifted(summed.astype(jnp.bfloat16), "seq", -1).astype(summed.dtype)
            + kv_terms[:, distance]
        )
    key_grad = summed[0].astype(jnp.bfloat16)
    value_grad = summed[1].astype(jnp.bfloat16)
    return (layer_out, query_grad, key_grad, value_grad, weight_grad)


def solution(mesh):
    placed = (P("seq", "kv"), P("seq", "kv"), P("seq", "kv"), P(None, "kv"), P("seq", "kv"), P())
    return jax.shard_map(
        per_device,
        mesh=mesh,
        in_specs=placed,
        out_specs=(P("seq", "kv"), P("seq", "kv"), P("seq", "kv"), P("seq", "kv"), P("seq", "kv")),
        check_vma=False,
    )
```

profile of v0, /device:TPU:1, one launch (start us, length us, event | category | flops | bytes accessed | tf_op | source)
XLA Modules:
  0.0 199.9 jit_solution(5304707169145419572)
XLA Ops:
  10.0 4.6 %collective-permute-start = (bf16[2,256,256]{1,2,0:T(8,128)(2,1)S(1)}, bf16[2,256,256]{1,2,0:T(8,128)(2,1)S(1)}, u32[]{:S(2)}, u32[]{:S(2)}) collective-permute-start(bf16[2,256,256]{1,2,0:T(8,128)(2,1)S(1)} %pad_maximum_fusion.1), channel_id=1, source_target_pairs={{0,4},{4,8},{8,12},{12,16},{16,20},{20,24},{24,28},{28,32},{32,36}... | collective-permute-start | bytes 786440 | tf_op jit(solution)/shard_map/ppermute | solution.py:13
  14.6 3.3 %collective-permute-done = bf16[2,256,256]{1,2,0:T(8,128)(2,1)S(1)} collective-permute-done((bf16[2,256,256]{1,2,0:T(8,128)(2,1)S(1)}, bf16[2,256,256]{1,2,0:T(8,128)(2,1)S(1)}, u32[]{:S(2)}, u32[]{:S(2)}) %collective-permute-start) | collective-permute-done | bytes 262176 | tf_op jit(solution)/shard_map/ppermute | solution.py:13
  17.9 4.4 %collective-permute-start.1 = (bf16[2,256,256]{1,2,0:T(8,128)(2,1)S(1)}, bf16[2,256,256]{1,2,0:T(8,128)(2,1)S(1)}, u32[]{:S(2)}, u32[]{:S(2)}) collective-permute-start(bf16[2,256,256]{1,2,0:T(8,128)(2,1)S(1)} %collective-permute-done), channel_id=1, source_target_pairs={{0,4},{4,8},{8,12},{12,16},{16,20},{20,24},{24,28},{28,32},{32,36}... | collective-permute-start | bytes 786440 | tf_op jit(solution)/shard_map/ppermute | solution.py:13
  23.5 2.1 %collective-permute-done.1 = bf16[2,256,256]{1,2,0:T(8,128)(2,1)S(1)} collective-permute-done((bf16[2,256,256]{1,2,0:T(8,128)(2,1)S(1)}, bf16[2,256,256]{1,2,0:T(8,128)(2,1)S(1)}, u32[]{:S(2)}, u32[]{:S(2)}) %collective-permute-start.1) | collective-permute-done | bytes 262176 | tf_op jit(solution)/shard_map/ppermute | solution.py:13
  25.6 4.4 %collective-permute-start.2 = (bf16[2,256,256]{1,2,0:T(8,128)(2,1)S(1)}, bf16[2,256,256]{1,2,0:T(8,128)(2,1)S(1)}, u32[]{:S(2)}, u32[]{:S(2)}) collective-permute-start(bf16[2,256,256]{1,2,0:T(8,128)(2,1)S(1)} %collective-permute-done.1), channel_id=1, source_target_pairs={{0,4},{4,8},{8,12},{12,16},{16,20},{20,24},{24,28},{28,32},{32,36}... | collective-permute-start | bytes 786440 | tf_op jit(solution)/shard_map/ppermute | solution.py:13
  33.5 1.6 fusion.4
  35.1 3.2 %copy-done = f32[2,1024,256,4]{2,1,3,0:T(8,128)} copy-done((f32[2,1024,256,4]{2,1,3,0:T(8,128)}, f32[2,1024,256,4]{2,1,3,0:T(8,128)S(1)}, u32[]{:S(2)}) %copy-start) | copy-done | bytes 8388632
  38.3 1.8 exponential_reduce_fusion
  40.1 3.9 %all-gather.2.cloned.1.call-done = bf16[256,4096]{1,0:T(8,128)(2,1)} async-done(((bf16[256,1024]{1,0:T(8,128)(2,1)}), bf16[256,4096]{1,0:T(8,128)(2,1)}) %all-gather.2.cloned.1.call-update) | async-done | bytes 2097168 | tf_op jit(solution)/shard_map/all_gather | solution.py:66
  44.0 6.3 %convolution_convert_fusion.2 = bf16[256,1024]{1,0:T(8,128)(2,1)S(1)} fusion(bf16[256,4096]{1,0:T(8,128)(2,1)} %all-gather.2.cloned.1.call-done, bf16[4096,1024]{1,0:T(8,128)(2,1)} %param.9), kind=kOutput, calls=%fused_computation.17 | convolution fusion | flops 2147745792 | bytes 11010048 | tf_op jit(solution)/shard_map/dot_general | solution.py:67
  51.3 5.6 %multiply_reduce_fusion = (f32[256,2,4]{0,2,1:T(4,128)S(1)}, bf16[2,128,4,256]{3,1,2,0:T(8,128)(2,1)S(1)}) fusion(bf16[256,1024]{0,1:T(8,128)(2,1)S(1)} %copy.69, bf16[1024,2,128,1]{0,2,3,1:T(8,128)(2,1)S(1)} %bitcast.116, f32[2,1024,256,4]{2,1,3,0:T(8,128)} %copy-done, f32[2,4,256]{2,1,0:T(4,128)S(1)} %bitcast.122, pred[256,1024]{0,1:T(8,128)(4,1)S(1)} %and_and_fusion), kind=kOutput, calls=%fused_computation.20 | convolution fusion | flops 546568192 | bytes 10240000 | tf_op jit(solution)/shard_map/gkij,jgd->igkd/dot_general | solution.py:56
  57.8 7.2 %convolution_convert_fusion = bf16[256,4096]{1,0:T(8,128)(2,1)} fusion(bf16[256,1024]{0,1:T(8,128)(2,1)S(1)} %bitcast.118, bf16[4096,1024]{1,0:T(8,128)(2,1)} %param.9), kind=kOutput, calls=%fused_computation.10 | convolution fusion | flops 2148532224 | bytes 11010048 | tf_op jit(solution)/shard_map/dot_general | solution.py:60
  65.3 6.6 %convert_bitcast_fusion = bf16[4096,1024]{0,1:T(8,128)(2,1)} fusion(bf16[256,1024]{0,1:T(8,128)(2,1)} %bitcast.119, bf16[256,4096]{1,0:T(8,128)(2,1)S(1)} %copy-done.3), kind=kOutput, calls=%fused_computation.5 | convolution fusion | flops 2151677952 | bytes 11010048 | tf_op jit(solution)/shard_map/dot_general | solution.py:71
  71.9 11.5 %copy.96 = bf16[4096,1024]{1,0:T(8,128)(2,1)} copy(bf16[4096,1024]{0,1:T(8,128)(2,1)} %convert_bitcast_fusion) | data formatting | bytes 16777216
  84.6 5.3 %fusion.2 = bf16[2,4,256,1024]{2,3,1,0:T(8,128)(2,1)S(1)} fusion(f32[2,1024,256,4]{2,1,3,0:T(8,128)} %copy-done, f32[2,4,256]{2,1,0:T(4,128)S(1)} %bitcast.126, f32[2,4,256]{2,1,0:T(4,128)S(1)} %bitcast.123, pred[256,1024]{0,1:T(8,128)(4,1)S(1)} %and_and_fusion, bf16[1024,2,128,1]{0,2,3,1:T(8,128)(2,1)S(1)} %bitcast.117, ...), kind=kOutput, calls=%fused_computation.3 | convolution fusion | flops 551550976 | bytes 13910016 | tf_op jit(solution)/shard_map/igkd,jgd->gkij/dot_general | solution.py:83
  89.9 1.9 copy-done.1
  94.8 5.7 %convolution_bitcast_fusion = f32[1024,2,128]{0,2,1:T(8,128)S(1)} fusion(bf16[256,2,4,128]{0,3,2,1:T(8,128)(2,1)S(1)} %bitcast.115, f32[2,1024,256,4]{2,1,3,0:T(8,128)} %copy-done, f32[2,4,256]{2,1,0:T(4,128)S(1)} %bitcast.124, pred[256,1024]{0,1:T(8,128)(4,1)S(1)} %and_and_fusion), kind=kOutput, calls=%fused_computation.14 | convolution fusion | flops 545259520 | bytes 10231808 | tf_op jit(solution)/shard_map/gkij,igkd->jgd/dot_general | solution.py:97
  103.7 3.0 %collective-permute-start.3 = (bf16[2,256,256]{2,1,0:T(8,128)(2,1)S(1)}, bf16[2,256,256]{2,1,0:T(8,128)(2,1)S(1)}, u32[]{:S(2)}, u32[]{:S(2)}) collective-permute-start(bf16[2,256,256]{2,1,0:T(8,128)(2,1)S(1)} %fusion.16), channel_id=1, source_target_pairs={{4,0},{8,4},{12,8},{16,12},{20,16},{24,20},{28,24},{32,28},{36,32}... | collective-permute-start | bytes 786440 | tf_op jit(solution)/shard_map/ppermute | solution.py:13
  106.8 5.0 %collective-permute-done.3 = bf16[2,256,256]{2,1,0:T(8,128)(2,1)S(1)} collective-permute-done((bf16[2,256,256]{2,1,0:T(8,128)(2,1)S(1)}, bf16[2,256,256]{2,1,0:T(8,128)(2,1)S(1)}, u32[]{:S(2)}, u32[]{:S(2)}) %collective-permute-start.3) | collective-permute-done | bytes 262176 | tf_op jit(solution)/shard_map/ppermute | solution.py:13
  111.9 1.9 collective-permute-start.4
  113.8 5.8 %collective-permute-done.4 = bf16[2,256,256]{2,1,0:T(8,128)(2,1)S(1)} collective-permute-done((bf16[2,256,256]{2,1,0:T(8,128)(2,1)S(1)}, bf16[2,256,256]{2,1,0:T(8,128)(2,1)S(1)}, u32[]{:S(2)}, u32[]{:S(2)}) %collective-permute-start.4) | collective-permute-done | bytes 262176 | tf_op jit(solution)/shard_map/ppermute | solution.py:13
  120.3 1.9 collective-permute-start.5
  124.0 4.2 %collective-permute-done.5 = bf16[2,256,256]{2,1,0:T(8,128)(2,1)S(1)} collective-permute-done((bf16[2,256,256]{2,1,0:T(8,128)(2,1)}, bf16[2,256,256]{2,1,0:T(8,128)(2,1)S(1)}, u32[]{:S(2)}, u32[]{:S(2)}) %collective-permute-start.5) | collective-permute-done | bytes 262176 | tf_op jit(solution)/shard_map/ppermute | solution.py:13
  129.0 64.4 %reduce-scatter.7.cloned.1.call-done = bf16[128,1024]{1,0:T(8,128)(2,1)} async-done(((bf16[4096,1024]{1,0:T(8,128)(2,1)}), bf16[128,1024]{1,0:T(8,128)(2,1)}) %reduce-scatter.7.cloned.1.call-update) | async-done | bytes 262160
  (55 shorter events, 20.2 us)
Async XLA Ops:
  7.2 36.8 %all-gather.2.cloned.1.call-start = ((), (), s32[]{:S(2)}) async-start(), calls=%async_computation.3 | async-start | bytes 2621440 | tf_op jit(solution)/shard_map/all_gather | solution.py:66
  7.9 121.1 %reduce-scatter.5.cloned.1.call-start = ((), (), s32[]{:S(2)}) async-start(), calls=%async_computation.2 | async-start | bytes 2621440 | tf_op jit(solution)/shard_map/reduce_scatter | solution.py:63
  10.0 7.9 %collective-permute-start = (bf16[2,256,256]{1,2,0:T(8,128)(2,1)S(1)}, bf16[2,256,256]{1,2,0:T(8,128)(2,1)S(1)}, u32[]{:S(2)}, u32[]{:S(2)}) collective-permute-start(bf16[2,256,256]{1,2,0:T(8,128)(2,1)S(1)} %pad_maximum_fusion.1), channel_id=1, source_target_pairs={{0,4},{4,8},{8,12},{12,16},{16,20},{20,24},{24,28},{28,32},{32,36}... | collective-permute-start | bytes 786440 | tf_op jit(solution)/shard_map/ppermute | solution.py:13
  17.9 7.7 %collective-permute-start.1 = (bf16[2,256,256]{1,2,0:T(8,128)(2,1)S(1)}, bf16[2,256,256]{1,2,0:T(8,128)(2,1)S(1)}, u32[]{:S(2)}, u32[]{:S(2)}) collective-permute-start(bf16[2,256,256]{1,2,0:T(8,128)(2,1)S(1)} %collective-permute-done), channel_id=1, source_target_pairs={{0,4},{4,8},{8,12},{12,16},{16,20},{20,24},{24,28},{28,32},{32,36}... | collective-permute-start | bytes 786440 | tf_op jit(solution)/shard_map/ppermute | solution.py:13
  25.6 7.7 %collective-permute-start.2 = (bf16[2,256,256]{1,2,0:T(8,128)(2,1)S(1)}, bf16[2,256,256]{1,2,0:T(8,128)(2,1)S(1)}, u32[]{:S(2)}, u32[]{:S(2)}) collective-permute-start(bf16[2,256,256]{1,2,0:T(8,128)(2,1)S(1)} %collective-permute-done.1), channel_id=1, source_target_pairs={{0,4},{4,8},{8,12},{12,16},{16,20},{20,24},{24,28},{28,32},{32,36}... | collective-permute-start | bytes 786440 | tf_op jit(solution)/shard_map/ppermute | solution.py:13
  33.5 17.1 %copy-start.6 = (bf16[1,1024,256]{1,2,0:T(8,128)(2,1)}, bf16[1,1024,256]{1,2,0:T(8,128)(2,1)S(1)}, u32[]{:S(2)}) copy-start(bf16[1,1024,256]{1,2,0:T(8,128)(2,1)S(1)} %get-tuple-element.28) | copy-start | bytes 1572868
  35.1 3.2 %copy-start = (f32[2,1024,256,4]{2,1,3,0:T(8,128)}, f32[2,1024,256,4]{2,1,3,0:T(8,128)S(1)}, u32[]{:S(2)}) copy-start(f32[2,1024,256,4]{2,1,3,0:T(8,128)S(1)} %get-tuple-element.32) | copy-start | bytes 25165828
  50.5 0.8 copy-start.4
  57.0 0.8 copy-start.8
  57.0 8.3 %copy-start.3 = (bf16[256,4096]{1,0:T(8,128)(2,1)S(1)}, bf16[256,4096]{1,0:T(8,128)(2,1)}, u32[]{:S(2)}) copy-start(bf16[256,4096]{1,0:T(8,128)(2,1)} %all-gather.2.cloned.1.call-done) | copy-start | bytes 6291460
  65.1 128.3 %reduce-scatter.7.cloned.1.call-start = ((), (), s32[]{:S(2)}) async-start(), calls=%async_computation.4 | async-start | bytes 8650752
  83.4 1.1 copy-start.5
  83.4 1.2 copy-start.7
  89.9 1.9 copy-start.1
  103.5 18.7 %copy-start.2 = (bf16[2,4,256,1024]{2,3,1,0:T(8,128)(2,1)S(1)}, bf16[2,4,256,1024]{2,3,1,0:T(8,128)(2,1)}, u32[]{:S(2)}) copy-start(bf16[2,4,256,1024]{2,3,1,0:T(8,128)(2,1)} %copy-done.1) | copy-start | bytes 12582916
  103.7 8.1 %collective-permute-start.3 = (bf16[2,256,256]{2,1,0:T(8,128)(2,1)S(1)}, bf16[2,256,256]{2,1,0:T(8,128)(2,1)S(1)}, u32[]{:S(2)}, u32[]{:S(2)}) collective-permute-start(bf16[2,256,256]{2,1,0:T(8,128)(2,1)S(1)} %fusion.16), channel_id=1, source_target_pairs={{4,0},{8,4},{12,8},{16,12},{20,16},{24,20},{28,24},{32,28},{36,32}... | collective-permute-start | bytes 786440 | tf_op jit(solution)/shard_map/ppermute | solution.py:13
  111.9 7.7 %collective-permute-start.4 = (bf16[2,256,256]{2,1,0:T(8,128)(2,1)S(1)}, bf16[2,256,256]{2,1,0:T(8,128)(2,1)S(1)}, u32[]{:S(2)}, u32[]{:S(2)}) collective-permute-start(bf16[2,256,256]{2,1,0:T(8,128)(2,1)S(1)} %fusion.12), channel_id=1, source_target_pairs={{4,0},{8,4},{12,8},{16,12},{20,16},{24,20},{28,24},{32,28},{36,32}... | collective-permute-start | bytes 786440 | tf_op jit(solution)/shard_map/ppermute | solution.py:13
  120.3 7.9 %collective-permute-start.5 = (bf16[2,256,256]{2,1,0:T(8,128)(2,1)}, bf16[2,256,256]{2,1,0:T(8,128)(2,1)S(1)}, u32[]{:S(2)}, u32[]{:S(2)}) collective-permute-start(bf16[2,256,256]{2,1,0:T(8,128)(2,1)} %fusion.10), channel_id=1, source_target_pairs={{4,0},{8,4},{12,8},{16,12},{20,16},{24,20},{28,24},{32,28},{36,32}... | collective-permute-start | bytes 786440 | tf_op jit(solution)/shard_map/ppermute | solution.py:13
Sparse Core Ops, SparseCore 0:
  9.7 34.2 all-gather.1
  65.2 32.7 reduce-scatter.4
  102.7 90.5 reduce-scatter.6
where the time goes:
time: 202 us; the launch traced here: 200 us
  waiting for transfers between devices  90.3 us (45%)
  matrix products  40.4 us (20%)
  local copies, waits for them, and re-layouts  30.4 us (15%)
  starting transfers between devices  20.5 us (10%)
  between operations  14.1 us (7%)
  other arithmetic  4.27 us (2%)
    unnamed x4, waiting for transfers between devices  65.1 us
    unnamed x22, local copies, waits for them, and re-layouts  22.4 us
    ppermute x6, waiting for transfers between devices, shifted(): return lax.ppermute(block, axis, route)  21.3 us
    ppermute x6, starting transfers between devices, shifted(): return lax.ppermute(block, axis, route)  20.2 us
    dot_general x1, matrix products, per_device(): lax.dot_general(attention, out_weight, (((1,), (1,)), ((), ())), preferre...  7.22 us
    dot_general x1, matrix products, per_device(): lax.dot_general(full_grad, attention, (((0,), (0,)), ((), ())), preferred...  6.62 us
    dot_general x1, matrix products, per_device(): jnp.dot(full_grad, out_weight, preferred_element_type=jnp.float32)  6.34 us
    dot_general x1, matrix products, per_device(): jnp.einsum('gkij,igkd->jgd', rounded_probs, grad_heads, preferred_element...  5.73 us
  transfers between devices with their start and end apart: 9, of which 8 were waited for; matrix products, arithmetic and copies ran while one was open for 24% of the time, Pallas kernels for 0%

commit v1 on v0

v1 whole, which is shorter than its diff:
```python
import math

import jax
import jax.numpy as jnp
from jax import lax
from jax.experimental import pallas as pl
from jax.experimental.pallas import tpu as pltpu
from jax.sharding import PartitionSpec as P

BF = jnp.bfloat16
F32 = jnp.float32
HD = 128
TOK = 256
SIDE = 4
SCALE = HD**-0.5
EXP2_SCALE = SCALE * math.log2(math.e)
MASKED = -1e30
VMEM_LIMIT = 48 * 1024 * 1024
VM = pltpu.VMEM
SM = pltpu.SMEM


def dot_nn(a, b):
    return lax.dot_general(a, b, (((1,), (0,)), ((), ())), preferred_element_type=F32)


def dot_nt(a, b):
    return lax.dot_general(a, b, (((1,), (1,)), ((), ())), preferred_element_type=F32)


def seq_route(step):
    pairs = []
    for x in range(SIDE):
        for y in range(SIDE):
            for core in range(2):
                to = step(x, y, core)
                if to is not None:
                    pairs.append(((x * SIDE + y) * 2 + core, (to[0] * SIDE + to[1]) * 2 + to[2]))
    return pairs


def chip_step(x, y, core, chips, to_core):
    chip = x * SIDE + y + chips
    return (chip // SIDE, chip % SIDE, to_core) if 0 <= chip < SIDE * SIDE else None


SWAP = seq_route(lambda x, y, c: (x, y, 1 - c))
NEXT_CHIP = seq_route(lambda x, y, c: chip_step(x, y, c, 1, c))
MIXED = seq_route(lambda x, y, c: (x, y, 1) if c == 0 else chip_step(x, y, c, 2, 0))


def back(route):
    return [(b, a) for a, b in route]


def along(axis, d):
    if axis == "x":
        return seq_route(lambda x, y, c: ((x + d) % SIDE, y, c))
    return seq_route(lambda x, y, c: (x, (y + d) % SIDE, c))


def seq_send(v, route):
    return lax.ppermute(v, "seq", route)


def kv_send(v, d):
    return lax.ppermute(v, "kv", [(i, (i + d) % SIDE) for i in range(SIDE)])


def call(kernel, out_shape, n_in, scratch=(), smem_in=0, flops=0, transcendentals=0, moved=0):
    return pl.pallas_call(
        kernel,
        out_shape=out_shape,
        in_specs=[pl.BlockSpec(memory_space=SM)] * smem_in + [pl.BlockSpec(memory_space=VM)] * n_in,
        out_specs=jax.tree.map(lambda _: pl.BlockSpec(memory_space=VM), out_shape),
        scratch_shapes=list(scratch),
        compiler_params=pltpu.CompilerParams(vmem_limit_bytes=VMEM_LIMIT),
        cost_estimate=pl.CostEstimate(
            flops=flops, transcendentals=transcendentals, bytes_accessed=moved
        ),
    )


def split_kernel(info, g, k, v, mine, theirs, kv):
    core = info[0] % 2
    for y in range(SIDE):
        there = pl.ds(y * HD, HD)
        mine[:, there] = g[:, pl.ds(pl.multiple_of(y * 2 * HD + core * HD, HD), HD)]
        theirs[:, there] = g[:, pl.ds(pl.multiple_of(y * 2 * HD + (1 - core) * HD, HD), HD)]
    kv[:, : 2 * HD] = k[...]
    kv[:, 2 * HD :] = v[...]


def doc_starts(lengths, pos):
    def step(n, carry):
        end, start = carry
        end = end + lengths[n]
        return end, jnp.where(pos >= end, end, start)

    return lax.fori_loop(0, 64, step, (jnp.int32(0), jnp.zeros_like(pos)))[1]


def window(info, lengths, blocks):
    seq = info[0]
    core = seq % 2
    first = seq * TOK
    pos = first + lax.broadcasted_iota(jnp.int32, (1, TOK), 1)
    start = doc_starts(lengths, pos)
    own, chip_before, mixed, swapped = blocks
    mixed_at = jnp.where(core == 1, -1, -3)
    swapped_at = jnp.where(core == 1, -3, -1)
    out = []
    for ref, at in ((own, 0), (chip_before, -2), (mixed, mixed_at), (swapped, swapped_at)):
        key_pos = first + at * TOK + lax.broadcasted_iota(jnp.int32, (TOK, 1), 0)
        ok = (key_pos >= start) & (key_pos <= pos)
        out.append((ref, jnp.where(ok, 0.0, MASKED).astype(F32)))
    return out


def heads(ref, g):
    return jnp.concatenate([ref[:, pl.ds((4 * g + h) * HD, HD)] for h in range(4)], axis=0)


def fwd_kernel(info, lengths, q, own, chip_before, mixed, swapped, att, lse, scores, bias):
    for b, (_, mask) in enumerate(window(info, lengths, (own, chip_before, mixed, swapped))):
        bias[b] = mask
    refs = (own, chip_before, mixed, swapped)
    for g in range(2):
        qg = heads(q, g)
        top = jnp.full((1, 4 * TOK), MASKED, F32)
        for b, ref in enumerate(refs):
            s = dot_nt(ref[:, pl.ds(g * HD, HD)], qg) * EXP2_SCALE
            s = s + jnp.concatenate([bias[b]] * 4, axis=1)
            scores[b] = s
            top = jnp.maximum(top, jnp.max(s, axis=0, keepdims=True))
        total = jnp.zeros((1, 4 * TOK), F32)
        o = jnp.zeros((HD, 4 * TOK), F32)
        for b, ref in enumerate(refs):
            e = jnp.exp2(scores[b] - top)
            total = total + jnp.sum(e, axis=0, keepdims=True)
            o = o + dot_nn(ref[:, pl.ds((2 + g) * HD, HD)].T, e.astype(BF))
        lse[g : g + 1, :] = top + jnp.log2(total)
        o = (o / total).T
        for h in range(4):
            att[:, pl.ds((4 * g + h) * HD, HD)] = o[h * TOK : (h + 1) * TOK].astype(BF)


def bwd_kernel(
    info, lengths, q, own, chip_before, mixed, swapped, lse, att, grad_own, grad_other,
    dq, d_own, d_chip_before, d_mixed, d_swapped, bias, grad,
):
    for b, (_, mask) in enumerate(window(info, lengths, (own, chip_before, mixed, swapped))):
        bias[b] = mask
    grad[...] = (grad_own[...] + grad_other[...].astype(F32)).astype(BF)
    refs = (own, chip_before, mixed, swapped)
    outs = (d_own, d_chip_before, d_mixed, d_swapped)
    for g in range(2):
        qg = heads(q, g)
        og = heads(grad, g)
        ag = heads(att, g)
        dots = jnp.sum((og.astype(F32) * ag.astype(F32)).T, axis=0, keepdims=True)
        row_lse = lse[g : g + 1, :]
        dqt = jnp.zeros((HD, 4 * TOK), F32)
        for b, (ref, out) in enumerate(zip(refs, outs)):
            kb = ref[:, pl.ds(g * HD, HD)]
            vb = ref[:, pl.ds((2 + g) * HD, HD)]
            s = dot_nt(kb, qg) * EXP2_SCALE + jnp.concatenate([bias[b]] * 4, axis=1)
            p = jnp.exp2(s - row_lse)
            out[:, pl.ds((2 + g) * HD, HD)] = dot_nn(p.astype(BF), og).astype(out.dtype)
            ds = (p * (dot_nt(vb, og) - dots) * SCALE).astype(BF)
            out[:, pl.ds(g * HD, HD)] = dot_nn(ds, qg).astype(out.dtype)
            dqt = dqt + dot_nn(kb.T, ds)
        dqs = dqt.T
        for h in range(4):
            dq[:, pl.ds((4 * g + h) * HD, HD)] = dqs[h * TOK : (h + 1) * TOK].astype(BF)


def out_kernel(att, w, out):
    out[...] = dot_nt(att[...], w[...]).astype(BF)


def layer_out_terms(att, w):
    rows = 512
    return pl.pallas_call(
        out_kernel,
        grid=(w.shape[0] // rows,),
        in_specs=[
            pl.BlockSpec(att.shape, lambda i: (0, 0)),
            pl.BlockSpec((rows, w.shape[1]), lambda i: (i, 0)),
        ],
        out_specs=pl.BlockSpec((TOK, rows), lambda i: (0, i)),
        out_shape=jax.ShapeDtypeStruct((TOK, w.shape[0]), BF),
        compiler_params=pltpu.CompilerParams(vmem_limit_bytes=VMEM_LIMIT),
        cost_estimate=pl.CostEstimate(
            flops=2 * TOK * w.size, transcendentals=0, bytes_accessed=2 * w.size
        ),
    )(att, w)


def attn_grad_kernel(info, g0, gm, gp, g2a, g2b, w, own, other, total):
    j = pl.program_id(0)
    wb = w[...].reshape(4 * HD, w.shape[-1])

    @pl.when(j == 0)
    def _():
        total[...] = dot_nn(g0[...], wb)

    @pl.when(j == 1)
    def _():
        total[...] += dot_nn(gm[...], wb)

    @pl.when(j == 2)
    def _():
        total[...] += dot_nn(gp[...], wb)

    @pl.when(j == 3)
    def _():
        own[...] = total[:TOK] + dot_nn(g2a[...], wb)
        other[...] = (total[TOK:] + dot_nn(g2b[...], wb)).astype(BF)


def attn_grad_terms(info, parts, w):
    cols = w.shape[1]
    def w_at(j, info):
        rel = jnp.where(j == 1, 1, jnp.where(j == 2, 3, jnp.where(j == 3, 2, 0)))
        return ((info[1] + rel) % SIDE, info[0] % 2, 0, 0)

    whole = [pl.BlockSpec(p.shape, lambda j, info: (0, 0)) for p in parts]
    return pl.pallas_call(
        attn_grad_kernel,
        grid_spec=pltpu.PrefetchScalarGridSpec(
            num_scalar_prefetch=1,
            grid=(SIDE,),
            in_specs=whole + [pl.BlockSpec((SIDE, 1, HD, cols), w_at)],
            out_specs=[pl.BlockSpec((TOK, cols), lambda j, info: (0, 0))] * 2,
            scratch_shapes=[VM((2 * TOK, cols), F32)],
        ),
        out_shape=[
            jax.ShapeDtypeStruct((TOK, cols), F32),
            jax.ShapeDtypeStruct((TOK, cols), BF),
        ],
        compiler_params=pltpu.CompilerParams(vmem_limit_bytes=VMEM_LIMIT),
        cost_estimate=pl.CostEstimate(
            flops=2 * TOK * w.size, transcendentals=0, bytes_accessed=w.size
        ),
    )(info, *parts, w.reshape(SIDE * SIDE, 2, HD, cols))


def weight_kernel(info, g0, gm, gp, g2a, g2b, att, att_other, *rest):
    by_x, by_y, gt, a = rest[:4], rest[4:8], rest[8], rest[9]
    seq, z = info[0], info[1]
    y = (seq // 2) % SIDE
    x = seq // (2 * SIDE)
    a[:TOK] = att[...]
    a[TOK:] = att_other[...]
    gt[z] = g0[...].T
    gt[(z + 1) % SIDE] = gm[...].T
    gt[(z + 3) % SIDE] = gp[...].T
    gt[(z + 2) % SIDE, :, :TOK] = g2a[...].T
    gt[(z + 2) % SIDE, :, TOK:] = g2b[...].T
    half = a.shape[1] // 2
    for d in (1, 3, 2, 0):
        by_x[d][...] = dot_nn(gt[(x + d) % SIDE], a[:, :half]).astype(BF)
        rows = pl.ds(pl.multiple_of(((y + d) % SIDE) * HD, HD), HD)
        for k in range(SIDE):
            by_y[d][pl.ds(k * HD, HD), :] = dot_nn(gt[k, rows, :], a[:, half:]).astype(BF)


def weight_sum_kernel(info, *refs):
    from_x, from_y, to_y, to_x = refs[:4], refs[4:8], refs[8:12], refs[12:16]
    seq = info[0]
    y = (seq // 2) % SIDE
    x = seq // (2 * SIDE)
    for sources, outs, at in ((from_x, to_y, y), (from_y, to_x, x)):
        for d in (1, 3, 2, 0):
            rows = pl.ds(pl.multiple_of(((at + d) % SIDE) * HD, HD), HD)
            total = sources[0][rows, :].astype(F32)
            for s in sources[1:]:
                total = total + s[rows, :].astype(F32)
            outs[d][...] = total.astype(BF)


def sum_last_kernel(*refs):
    out = refs[8]
    half = out.shape[1] // 2
    for i in range(2):
        total = refs[4 * i][...].astype(F32)
        for s in refs[4 * i + 1 : 4 * i + 4]:
            total = total + s[...].astype(F32)
        out[:, i * half : (i + 1) * half] = total.astype(BF)


def weight_gradient(info, parts, att, att_other):
    cols = att.shape[1]
    half = cols // 2
    terms = call(
        weight_kernel,
        [jax.ShapeDtypeStruct((4 * HD, half), BF)] * 8,
        len(parts) + 2,
        scratch=[VM((SIDE, 4 * HD, 2 * TOK), BF), VM((2 * TOK, cols), BF)],
        smem_in=1,
        flops=2 * 2048 * 512 * cols,
        moved=7 * 2**20,
    )(info, *parts, att, att_other)
    by_x, by_y = terms[:4], terms[4:]
    from_x, from_y = [by_x[0], None, None, None], [by_y[0], None, None, None]
    for d in (1, 3, 2):
        from_x[d] = seq_send(by_x[d], along("x", d))
        from_y[d] = seq_send(by_y[d], along("y", d))
    sums = call(
        weight_sum_kernel,
        [jax.ShapeDtypeStruct((HD, half), BF)] * 8,
        8,
        smem_in=1,
        flops=4 * 2**20,
        moved=5 * 2**20,
    )(info, *from_x, *from_y)
    to_y, to_x = sums[:4], sums[4:]
    last_x, last_y = [to_x[0]], [to_y[0]]
    for d in (1, 3, 2):
        last_y.append(seq_send(to_y[d], along("y", d)))
        last_x.append(seq_send(to_x[d], along("x", d)))
    return call(
        sum_last_kernel, jax.ShapeDtypeStruct((HD, cols), BF), 8, flops=2**20, moved=5 * 2**18
    )(*last_y, *last_x)


def finish_kernel(own, chip_before, mixed, dk, dv):
    total = own[...] + chip_before[...].astype(F32) + mixed[...].astype(F32)
    dk[...] = total[:, : 2 * HD].astype(BF)
    dv[...] = total[:, 2 * HD :].astype(BF)


def per_device(queries, keys, values, out_weight, out_grad, doc_lengths):
    shape = jax.ShapeDtypeStruct
    info = jnp.stack([lax.axis_index("seq"), lax.axis_index("kv")]).astype(jnp.int32)
    cols = queries.shape[1]
    mine, theirs, kv = call(
        split_kernel, [shape((TOK, 4 * HD), BF)] * 3, 3, smem_in=1, moved=2 * 2**20
    )(info, out_grad, keys, values)

    chip_before = seq_send(kv, NEXT_CHIP)
    other_half = seq_send(theirs, SWAP)
    mixed = seq_send(kv, MIXED)
    swapped = seq_send(chip_before, SWAP)

    g0 = jnp.concatenate([mine, other_half], axis=0)
    gp = kv_send(g0, 1)
    gm = kv_send(g0, -1)
    g2a = kv_send(gp[:TOK], 1)
    g2b = kv_send(gm[TOK:], -1)
    parts = (g0, gm, gp, g2a, g2b)

    tile = 2 * TOK * 4 * TOK
    att, lse = call(
        fwd_kernel,
        [shape((TOK, cols), BF), shape((2, 4 * TOK), F32)],
        5,
        scratch=[VM((4, TOK, 4 * TOK), F32), VM((4, TOK, TOK), F32)],
        smem_in=2,
        flops=8 * tile * HD * 2,
        transcendentals=8 * tile,
        moved=2 * 2**20,
    )(info, doc_lengths, queries, kv, chip_before, mixed, swapped)

    att_other = seq_send(att, SWAP)
    layer_out = lax.psum_scatter(
        layer_out_terms(att, out_weight), "kv", scatter_dimension=1, tiled=True
    )

    weight_grad = weight_gradient(info, parts, att, att_other)

    grad_own, grad_to_other = attn_grad_terms(info, parts, out_weight)
    grad_other = seq_send(grad_to_other, SWAP)
    query_grad, d_own, d_chip_before, d_mixed, d_swapped = call(
        bwd_kernel,
        [
            shape((TOK, cols), BF),
            shape((TOK, 4 * HD), F32),
            shape((TOK, 4 * HD), F32),
            shape((TOK, 4 * HD), BF),
            shape((TOK, 4 * HD), BF),
        ],
        9,
        scratch=[VM((4, TOK, TOK), F32), VM((TOK, cols), BF)],
        smem_in=2,
        flops=8 * tile * HD * 5,
        transcendentals=8 * tile,
        moved=6 * 2**20,
    )(info, doc_lengths, queries, kv, chip_before, mixed, swapped, lse, att, grad_own, grad_other)
    from_mixed = seq_send(d_mixed, back(MIXED))
    from_swapped = seq_send(d_swapped, SWAP)
    from_chip = seq_send(
        (d_chip_before + from_swapped.astype(F32)).astype(BF), back(NEXT_CHIP)
    )
    key_grad, value_grad = call(
        finish_kernel, [shape((TOK, 2 * HD), BF)] * 2, 3, flops=2**20, moved=2**20
    )(d_own, from_chip, from_mixed)
    return (layer_out, query_grad, key_grad, value_grad, weight_grad)


def solution(mesh):
    placed = (P("seq", "kv"), P("seq", "kv"), P("seq", "kv"), P(None, "kv"), P("seq", "kv"), P())
    return jax.shard_map(
        per_device,
        mesh=mesh,
        in_specs=placed,
        out_specs=(P("seq", "kv"),) * 5,
        check_vma=False,
    )
```

time: 202 us -> 156 us (0.77)
  the two profiles are of different devices: /device:TPU:1 before, /device:TPU:6 now
where the time goes in v1:
time: 156 us; the launch traced here: 155 us
  waiting for transfers between devices  61.5 us (39%)
  starting transfers between devices  38.6 us (25%)
  Pallas kernels  33.9 us (22%)
  between operations  14.2 us (9%)
  local copies, waits for them, and re-layouts  6.49 us (4%)
    ppermute x21, waiting for transfers between devices, seq_send(): return lax.ppermute(v, 'seq', route)  31.8 us
    ppermute x21, starting transfers between devices, seq_send(): return lax.ppermute(v, 'seq', route)  30.1 us
    ppermute x4, waiting for transfers between devices, kv_send(): return lax.ppermute(v, 'kv', [(i, (i + d) % SIDE) for i in range(SIDE)])  29.6 us
    pallas_call x1, Pallas kernels, layer_out_terms(): pl.pallas_call(out_kernel, grid=(w.shape[0] // rows,), in_specs=[pl.Block...  8.91 us
    ppermute x4, starting transfers between devices, kv_send(): return lax.ppermute(v, 'kv', [(i, (i + d) % SIDE) for i in range(SIDE)])  8.49 us
    pallas_call x1, Pallas kernels, per_device(): call(bwd_kernel, [shape((TOK, cols), BF), shape((TOK, 4 * HD), F32), shap...  7.38 us
    unnamed x23, local copies, waits for them, and re-layouts  6.44 us
    pallas_call x1, Pallas kernels, attn_grad_terms(): pl.pallas_call(attn_grad_kernel, grid_spec=pltpu.PrefetchScalarGridSpec(n...  5.57 us
  transfers between devices with their start and end apart: 26, of which 14 were waited for; matrix products, arithmetic and copies ran while one was open for 0% of the time, Pallas kernels for 13%

profile of v1, /device:TPU:6, one launch (start us, length us, event | category | flops | bytes accessed | tf_op | source)
XLA Modules:
  0.0 154.9 jit_solution(1239960003369030004)
XLA Ops:
  10.8 3.5 %collective-permute-start = (bf16[256,512]{1,0:T(8,128)(2,1)S(1)}, bf16[256,512]{1,0:T(8,128)(2,1)S(1)}, u32[]{:S(2)}, u32[]{:S(2)}) collective-permute-start(bf16[256,512]{1,0:T(8,128)(2,1)S(1)} %get-tuple-element.35.own), channel_id=1, source_target_pairs={{0,8},{4,12},{8,16},{12,20},{16,24},{20,28},{24,32},{28,36},{32,40... | collective-permute-start | bytes 786440 | tf_op jit(solution)/shard_map/ppermute | solution.py:63
  14.3 1.9 %collective-permute-start.1 = (bf16[256,512]{1,0:T(8,128)(2,1)S(1)}, bf16[256,512]{1,0:T(8,128)(2,1)S(1)}, u32[]{:S(2)}, u32[]{:S(2)}) collective-permute-start(bf16[256,512]{1,0:T(8,128)(2,1)S(1)} %get-tuple-element.35.own), channel_id=1, source_target_pairs={{0,4},{4,16},{8,12},{12,24},{16,20},{20,32},{24,28},{28,40},{32,36... | collective-permute-start | bytes 786440 | tf_op jit(solution)/shard_map/ppermute | solution.py:63
  16.3 8.1 %collective-permute-done.chip_before = bf16[256,512]{1,0:T(8,128)(2,1)S(1)} collective-permute-done((bf16[256,512]{1,0:T(8,128)(2,1)S(1)}, bf16[256,512]{1,0:T(8,128)(2,1)S(1)}, u32[]{:S(2)}, u32[]{:S(2)}) %collective-permute-start) | collective-permute-done | bytes 262176 | tf_op jit(solution)/shard_map/ppermute | solution.py:63
  27.6 4.4 %shard_map.102 = (bf16[256,1024]{1,0:T(8,128)(2,1)S(1)}, f32[2,1024]{1,0:T(2,128)S(1)}) custom-call(s32[2]{0:T(128)S(1)} %pad_add_fusion.info, s32[64]{0:T(128)S(1)} %copy-done.8, bf16[256,1024]{1,0:T(8,128)(2,1)S(1)} %copy-done.6, bf16[256,512]{1,0:T(8,128)(2,1)S(1)} %get-tuple-element.35.own, bf16[256,512]{1,0:T(8,128)(2,1)S(1)} %collective-permute-done.chip_before, ...), custom_call_target="tpu_custom_call" | custom-call | flops 1073741824 | bytes 2097152 | tf_op jit(solution)/shard_map/pallas_call | solution.py:355
  32.0 8.9 %shard_map.103 = bf16[256,4096]{1,0:T(8,128)(2,1)} custom-call(bf16[256,1024]{1,0:T(8,128)(2,1)S(1)} %get-tuple-element.36.att, bf16[4096,1024]{1,0:T(8,128)(2,1)} %w.1), custom_call_target="tpu_custom_call" | custom-call | flops 2147483648 | bytes 8388608 | tf_op jit(solution)/shard_map/pallas_call | solution.py:184
  42.6 2.0 %collective-permute-start.5 = (bf16[512,512]{1,0:T(8,128)(2,1)S(1)}, bf16[512,512]{1,0:T(8,128)(2,1)S(1)}, u32[]{:S(2)}, u32[]{:S(2)}) collective-permute-start(bf16[512,512]{1,0:T(8,128)(2,1)S(1)} %constant_dynamic-update-slice_fusion.g0), channel_id=1, source_target_pairs={{0,1},{1,2},{2,3},{3,0},{4,5},{5,6},{6,7},{7,4},{8,9},{9,10},{10,1... | collective-permute-start | bytes 1572872 | tf_op jit(solution)/shard_map/ppermute | solution.py:67
  44.6 2.2 %collective-permute-start.4 = (bf16[512,512]{1,0:T(8,128)(2,1)S(1)}, bf16[512,512]{1,0:T(8,128)(2,1)S(1)}, u32[]{:S(2)}, u32[]{:S(2)}) collective-permute-start(bf16[512,512]{1,0:T(8,128)(2,1)S(1)} %constant_dynamic-update-slice_fusion.g0), channel_id=1, source_target_pairs={{0,3},{1,0},{2,1},{3,2},{4,7},{5,4},{6,5},{7,6},{8,11},{9,8},{10,9... | collective-permute-start | bytes 1572872 | tf_op jit(solution)/shard_map/ppermute | solution.py:67
  46.8 16.8 %collective-permute-done.5.gp = bf16[512,512]{1,0:T(8,128)(2,1)S(1)} collective-permute-done((bf16[512,512]{1,0:T(8,128)(2,1)S(1)}, bf16[512,512]{1,0:T(8,128)(2,1)S(1)}, u32[]{:S(2)}, u32[]{:S(2)}) %collective-permute-start.5) | collective-permute-done | bytes 524320 | tf_op jit(solution)/shard_map/ppermute | solution.py:67
  66.0 3.8 %collective-permute-start.7 = (bf16[256,512]{1,0:T(8,128)(2,1)S(1)}, bf16[256,512]{1,0:T(8,128)(2,1)S(1)}, u32[]{:S(2)}, u32[]{:S(2)}) collective-permute-start(bf16[256,512]{1,0:T(8,128)(2,1)S(1)} %slice.9), channel_id=1, source_target_pairs={{0,3},{1,0},{2,1},{3,2},{4,7},{5,4},{6,5},{7,6},{8,11},{9,8},{10,9... | collective-permute-start | bytes 786440 | tf_op jit(solution)/shard_map/ppermute | solution.py:67
  69.8 9.4 %collective-permute-done.6.g2a = bf16[256,512]{1,0:T(8,128)(2,1)S(1)} collective-permute-done((bf16[256,512]{1,0:T(8,128)(2,1)S(1)}, bf16[256,512]{1,0:T(8,128)(2,1)S(1)}, u32[]{:S(2)}, u32[]{:S(2)}) %collective-permute-start.6) | collective-permute-done | bytes 262176 | tf_op jit(solution)/shard_map/ppermute | solution.py:67
  80.8 5.6 %shard_map.104 = (f32[256,1024]{1,0:T(8,128)S(1)}, bf16[256,1024]{1,0:T(8,128)(2,1)S(1)}) custom-call(s32[2]{0:T(128)S(1)} %pad_add_fusion.info, bf16[512,512]{1,0:T(8,128)(2,1)S(1)} %constant_dynamic-update-slice_fusion.g0, bf16[512,512]{1,0:T(8,128)(2,1)S(1)} %collective-permute-done.4.gm, bf16[512,512]{1,0:T(8,128)(2,1)S(1)} %collective-permute-done.5.gp, ...), custom_call_target="tpu_custom_call" | custom-call | flops 2147483648 | bytes 4194304 | tf_op jit(solution)/shard_map/pallas_call | solution.py:229
  87.3 4.3 %shard_map.107 = (bf16[512,512]{1,0:T(8,128)(2,1)S(1)}, bf16[512,512]{1,0:T(8,128)(2,1)S(1)}, bf16[512,512]{1,0:T(8,128)(2,1)S(1)}, bf16[512,512]{1,0:T(8,128)(2...) custom-call(s32[2]{0:T(128)S(1)} %pad_add_fusion.info, ...), custom_call_target="tpu_custom_call" | custom-call | flops 2147483648 | bytes 7340032 | tf_op jit(solution)/shard_map/pallas_call | solution.py:296
  91.7 2.9 %collective-permute-start.14 = (bf16[512,512]{1,0:T(8,128)(2,1)S(1)}, bf16[512,512]{1,0:T(8,128)(2,1)S(1)}, u32[]{:S(2)}, u32[]{:S(2)}) collective-permute-start(bf16[512,512]{1,0:T(8,128)(2,1)S(1)} %get-tuple-element.51), channel_id=1, source_target_pairs={{0,64},{4,68},{8,72},{12,76},{16,80},{20,84},{24,88},{28,92},{32,9... | collective-permute-start | bytes 1572872 | tf_op jit(solution)/shard_map/ppermute | solution.py:63
  94.8 3.4 %collective-permute-start.17 = (bf16[512,512]{1,0:T(8,128)(2,1)S(1)}, bf16[512,512]{1,0:T(8,128)(2,1)S(1)}, u32[]{:S(2)}, u32[]{:S(2)}) collective-permute-start(bf16[512,512]{1,0:T(8,128)(2,1)S(1)} %get-tuple-element.55), channel_id=1, source_target_pairs={{0,16},{4,20},{8,24},{12,28},{16,0},{20,4},{24,8},{28,12},{32,48},... | collective-permute-start | bytes 1572872 | tf_op jit(solution)/shard_map/ppermute | solution.py:63
  98.2 8.2 %collective-permute-done.13.refs_1_ = bf16[512,512]{1,0:T(8,128)(2,1)S(1)} collective-permute-done((bf16[512,512]{1,0:T(8,128)(2,1)S(1)}, bf16[512,512]{1,0:T(8,128)(2,1)S(1)}, u32[]{:S(2)}, u32[]{:S(2)}) %collective-permute-start.13) | collective-permute-done | bytes 524320 | tf_op jit(solution)/shard_map/ppermute | solution.py:63
  106.4 2.2 %collective-permute-start.18 = (bf16[512,512]{1,0:T(8,128)(2,1)S(1)}, bf16[512,512]{1,0:T(8,128)(2,1)S(1)}, u32[]{:S(2)}, u32[]{:S(2)}) collective-permute-start(bf16[512,512]{1,0:T(8,128)(2,1)S(1)} %get-tuple-element.56), channel_id=1, source_target_pairs={{0,24},{4,28},{8,0},{12,4},{16,8},{20,12},{24,16},{28,20},{32,56},... | collective-permute-start | bytes 1572872 | tf_op jit(solution)/shard_map/ppermute | solution.py:63
  109.6 7.4 %shard_map.105 = (bf16[256,1024]{1,0:T(8,128)(2,1)}, f32[256,512]{1,0:T(8,128)S(1)}, f32[256,512]{1,0:T(8,128)S(1)}, bf16[256,512]{1,0:T(8,128)(2,1)S(1)}, bf16[256,512]{1,0:T(8,128)(2,1)S(1)}) custom-call(s32[2]{0:T(128)S(1)} %pad_add_fusion.info, s32[64]{0:T(128)S(1)} %copy-done.9, bf16[256,1024]{1,0:T(8,128)(2,1)S(1)} %copy-done.7, ...), custom_call_target="tpu_custom_call" | custom-call | flops 2684354560 | bytes 6291456 | tf_op jit(solution)/shard_map/pallas_call | solution.py:375
  117.0 2.0 %collective-permute-done.15.refs_3_ = bf16[512,512]{1,0:T(8,128)(2,1)S(1)} collective-permute-done((bf16[512,512]{1,0:T(8,128)(2,1)S(1)}, bf16[512,512]{1,0:T(8,128)(2,1)S(1)}, u32[]{:S(2)}, u32[]{:S(2)}) %collective-permute-start.15) | collective-permute-done | bytes 524320 | tf_op jit(solution)/shard_map/ppermute | solution.py:63
  119.0 3.5 %collective-permute-start.11 = (bf16[256,512]{1,0:T(8,128)(2,1)S(1)}, bf16[256,512]{1,0:T(8,128)(2,1)S(1)}, u32[]{:S(2)}, u32[]{:S(2)}) collective-permute-start(bf16[256,512]{1,0:T(8,128)(2,1)S(1)} %get-tuple-element.46), channel_id=1, source_target_pairs={{4,0},{16,4},{12,8},{24,12},{20,16},{32,20},{28,24},{40,28},{36,32... | collective-permute-start | bytes 786440 | tf_op jit(solution)/shard_map/ppermute | solution.py:63
  124.4 2.5 %collective-permute-start.20 = (bf16[128,512]{1,0:T(8,128)(2,1)S(1)}, bf16[128,512]{1,0:T(8,128)(2,1)S(1)}, u32[]{:S(2)}, u32[]{:S(2)}) collective-permute-start(bf16[128,512]{1,0:T(8,128)(2,1)S(1)} %get-tuple-element.59), channel_id=1, source_target_pairs={{0,24},{4,28},{8,0},{12,4},{16,8},{20,12},{24,16},{28,20},{32,56},... | collective-permute-start | bytes 393224 | tf_op jit(solution)/shard_map/ppermute | solution.py:63
  127.3 4.1 %collective-permute-start.10 = (bf16[256,512]{1,0:T(8,128)(2,1)S(1)}, bf16[256,512]{1,0:T(8,128)(2,1)S(1)}, u32[]{:S(2)}, u32[]{:S(2)}) collective-permute-start(bf16[256,512]{1,0:T(8,128)(2,1)S(1)} %add_convert_fusion), channel_id=1, source_target_pairs={{8,0},{12,4},{16,8},{20,12},{24,16},{28,20},{32,24},{36,28},{40,32... | collective-permute-start | bytes 786440 | tf_op jit(solution)/shard_map/ppermute | solution.py:63
  134.6 2.2 %collective-permute-start.24 = (bf16[128,512]{1,0:T(8,128)(2,1)S(1)}, bf16[128,512]{1,0:T(8,128)(2,1)S(1)}, u32[]{:S(2)}, u32[]{:S(2)}) collective-permute-start(bf16[128,512]{1,0:T(8,128)(2,1)S(1)} %get-tuple-element.64), channel_id=1, source_target_pairs={{0,64},{4,68},{8,72},{12,76},{16,80},{20,84},{24,88},{28,92},{32,9... | collective-permute-start | bytes 393224 | tf_op jit(solution)/shard_map/ppermute | solution.py:63
  138.7 3.3 %collective-permute-done.23.refs_6_ = bf16[128,512]{1,0:T(8,128)(2,1)S(1)} collective-permute-done((bf16[128,512]{1,0:T(8,128)(2,1)S(1)}, bf16[128,512]{1,0:T(8,128)(2,1)S(1)}, u32[]{:S(2)}, u32[]{:S(2)}) %collective-permute-start.23) | collective-permute-done | bytes 131104 | tf_op jit(solution)/shard_map/ppermute | solution.py:63
  141.9 4.5 %collective-permute-done.24.refs_7_ = bf16[128,512]{1,0:T(8,128)(2,1)S(1)} collective-permute-done((bf16[128,512]{1,0:T(8,128)(2,1)S(1)}, bf16[128,512]{1,0:T(8,128)(2,1)S(1)}, u32[]{:S(2)}, u32[]{:S(2)}) %collective-permute-start.24) | collective-permute-done | bytes 131104 | tf_op jit(solution)/shard_map/ppermute | solution.py:63
  (66 shorter events, 23.8 us)
Async XLA Ops:
  7.2 140.8 %reduce-scatter.2.cloned.1.call-start = ((), (), s32[]{:S(2)}) async-start(), calls=%async_computation.1 | async-start | bytes 2621440 | tf_op jit(solution)/shard_map/reduce_scatter | solution.py:367
  10.8 13.5 %collective-permute-start = (bf16[256,512]{1,0:T(8,128)(2,1)S(1)}, bf16[256,512]{1,0:T(8,128)(2,1)S(1)}, u32[]{:S(2)}, u32[]{:S(2)}) collective-permute-start(bf16[256,512]{1,0:T(8,128)(2,1)S(1)} %get-tuple-element.35.own), channel_id=1, source_target_pairs={{0,8},{4,12},{8,16},{12,20},{16,24},{20,28},{24,32},{28,36},{32,40... | collective-permute-start | bytes 786440 | tf_op jit(solution)/shard_map/ppermute | solution.py:63
  14.3 11.4 %collective-permute-start.1 = (bf16[256,512]{1,0:T(8,128)(2,1)S(1)}, bf16[256,512]{1,0:T(8,128)(2,1)S(1)}, u32[]{:S(2)}, u32[]{:S(2)}) collective-permute-start(bf16[256,512]{1,0:T(8,128)(2,1)S(1)} %get-tuple-element.35.own), channel_id=1, source_target_pairs={{0,4},{4,16},{8,12},{12,24},{16,20},{20,32},{24,28},{28,40},{32,36... | collective-permute-start | bytes 786440 | tf_op jit(solution)/shard_map/ppermute | solution.py:63
  42.6 21.0 %collective-permute-start.5 = (bf16[512,512]{1,0:T(8,128)(2,1)S(1)}, bf16[512,512]{1,0:T(8,128)(2,1)S(1)}, u32[]{:S(2)}, u32[]{:S(2)}) collective-permute-start(bf16[512,512]{1,0:T(8,128)(2,1)S(1)} %constant_dynamic-update-slice_fusion.g0), channel_id=1, source_target_pairs={{0,1},{1,2},{2,3},{3,0},{4,5},{5,6},{6,7},{7,4},{8,9},{9,10},{10,1... | collective-permute-start | bytes 1572872 | tf_op jit(solution)/shard_map/ppermute | solution.py:67
  44.6 21.4 %collective-permute-start.4 = (bf16[512,512]{1,0:T(8,128)(2,1)S(1)}, bf16[512,512]{1,0:T(8,128)(2,1)S(1)}, u32[]{:S(2)}, u32[]{:S(2)}) collective-permute-start(bf16[512,512]{1,0:T(8,128)(2,1)S(1)} %constant_dynamic-update-slice_fusion.g0), channel_id=1, source_target_pairs={{0,3},{1,0},{2,1},{3,2},{4,7},{5,4},{6,5},{7,6},{8,11},{9,8},{10,9... | collective-permute-start | bytes 1572872 | tf_op jit(solution)/shard_map/ppermute | solution.py:67
  46.8 39.6 %collective-permute-start.12 = (bf16[256,1024]{1,0:T(8,128)(2,1)S(1)}, bf16[256,1024]{1,0:T(8,128)(2,1)S(1)}, u32[]{:S(2)}, u32[]{:S(2)}) collective-permute-start(bf16[256,1024]{1,0:T(8,128)(2,1)S(1)} %get-tuple-element.36.att), channel_id=1, source_target_pairs={{0,4},{4,0},{8,12},{12,8},{16,20},{20,16},{24,28},{28,24},{32,36},... | collective-permute-start | bytes 1572872 | tf_op jit(solution)/shard_map/ppermute | solution.py:63
  63.7 15.5 %collective-permute-start.6 = (bf16[256,512]{1,0:T(8,128)(2,1)S(1)}, bf16[256,512]{1,0:T(8,128)(2,1)S(1)}, u32[]{:S(2)}, u32[]{:S(2)}) collective-permute-start(bf16[256,512]{1,0:T(8,128)(2,1)S(1)} %slice.8), channel_id=1, source_target_pairs={{0,1},{1,2},{2,3},{3,0},{4,5},{5,6},{6,7},{7,4},{8,9},{9,10},{10,1... | collective-permute-start | bytes 786440 | tf_op jit(solution)/shard_map/ppermute | solution.py:67
  66.0 14.7 %collective-permute-start.7 = (bf16[256,512]{1,0:T(8,128)(2,1)S(1)}, bf16[256,512]{1,0:T(8,128)(2,1)S(1)}, u32[]{:S(2)}, u32[]{:S(2)}) collective-permute-start(bf16[256,512]{1,0:T(8,128)(2,1)S(1)} %slice.9), channel_id=1, source_target_pairs={{0,3},{1,0},{2,1},{3,2},{4,7},{5,4},{6,5},{7,6},{8,11},{9,8},{10,9... | collective-permute-start | bytes 786440 | tf_op jit(solution)/shard_map/ppermute | solution.py:67
  86.4 8.5 %collective-permute-start.8 = (bf16[256,1024]{1,0:T(8,128)(2,1)S(1)}, bf16[256,1024]{1,0:T(8,128)(2,1)S(1)}, u32[]{:S(2)}, u32[]{:S(2)}) collective-permute-start(bf16[256,1024]{1,0:T(8,128)(2,1)S(1)} %get-tuple-element.41), channel_id=1, source_target_pairs={{0,4},{4,0},{8,12},{12,8},{16,20},{20,16},{24,28},{28,24},{32,36},... | collective-permute-start | bytes 1572872 | tf_op jit(solution)/shard_map/ppermute | solution.py:63
  91.6 14.8 %collective-permute-start.13 = (bf16[512,512]{1,0:T(8,128)(2,1)S(1)}, bf16[512,512]{1,0:T(8,128)(2,1)S(1)}, u32[]{:S(2)}, u32[]{:S(2)}) collective-permute-start(bf16[512,512]{1,0:T(8,128)(2,1)S(1)} %get-tuple-element.50), channel_id=1, source_target_pairs={{0,32},{4,36},{8,40},{12,44},{16,48},{20,52},{24,56},{28,60},{32,6... | collective-permute-start | bytes 1572872 | tf_op jit(solution)/shard_map/ppermute | solution.py:63
  91.7 25.3 %collective-permute-start.14 = (bf16[512,512]{1,0:T(8,128)(2,1)S(1)}, bf16[512,512]{1,0:T(8,128)(2,1)S(1)}, u32[]{:S(2)}, u32[]{:S(2)}) collective-permute-start(bf16[512,512]{1,0:T(8,128)(2,1)S(1)} %get-tuple-element.51), channel_id=1, source_target_pairs={{0,64},{4,68},{8,72},{12,76},{16,80},{20,84},{24,88},{28,92},{32,9... | collective-permute-start | bytes 1572872 | tf_op jit(solution)/shard_map/ppermute | solution.py:63
  94.5 24.4 %collective-permute-start.15 = (bf16[512,512]{1,0:T(8,128)(2,1)S(1)}, bf16[512,512]{1,0:T(8,128)(2,1)S(1)}, u32[]{:S(2)}, u32[]{:S(2)}) collective-permute-start(bf16[512,512]{1,0:T(8,128)(2,1)S(1)} %get-tuple-element.52), channel_id=1, source_target_pairs={{0,96},{4,100},{8,104},{12,108},{16,112},{20,116},{24,120},{28,124... | collective-permute-start | bytes 1572872 | tf_op jit(solution)/shard_map/ppermute | solution.py:63
  94.5 27.9 %collective-permute-start.16 = (bf16[512,512]{1,0:T(8,128)(2,1)S(1)}, bf16[512,512]{1,0:T(8,128)(2,1)S(1)}, u32[]{:S(2)}, u32[]{:S(2)}) collective-permute-start(bf16[512,512]{1,0:T(8,128)(2,1)S(1)} %get-tuple-element.54), channel_id=1, source_target_pairs={{0,8},{4,12},{8,16},{12,20},{16,24},{20,28},{24,0},{28,4},{32,40},... | collective-permute-start | bytes 1572872 | tf_op jit(solution)/shard_map/ppermute | solution.py:63
  94.8 27.6 %collective-permute-start.17 = (bf16[512,512]{1,0:T(8,128)(2,1)S(1)}, bf16[512,512]{1,0:T(8,128)(2,1)S(1)}, u32[]{:S(2)}, u32[]{:S(2)}) collective-permute-start(bf16[512,512]{1,0:T(8,128)(2,1)S(1)} %get-tuple-element.55), channel_id=1, source_target_pairs={{0,16},{4,20},{8,24},{12,28},{16,0},{20,4},{24,8},{28,12},{32,48},... | collective-permute-start | bytes 1572872 | tf_op jit(solution)/shard_map/ppermute | solution.py:63
  106.4 16.1 %collective-permute-start.18 = (bf16[512,512]{1,0:T(8,128)(2,1)S(1)}, bf16[512,512]{1,0:T(8,128)(2,1)S(1)}, u32[]{:S(2)}, u32[]{:S(2)}) collective-permute-start(bf16[512,512]{1,0:T(8,128)(2,1)S(1)} %get-tuple-element.56), channel_id=1, source_target_pairs={{0,24},{4,28},{8,0},{12,4},{16,8},{20,12},{24,16},{28,20},{32,56},... | collective-permute-start | bytes 1572872 | tf_op jit(solution)/shard_map/ppermute | solution.py:63
  117.0 10.2 %collective-permute-start.9 = (bf16[256,512]{1,0:T(8,128)(2,1)S(1)}, bf16[256,512]{1,0:T(8,128)(2,1)S(1)}, u32[]{:S(2)}, u32[]{:S(2)}) collective-permute-start(bf16[256,512]{1,0:T(8,128)(2,1)S(1)} %get-tuple-element.45), channel_id=1, source_target_pairs={{0,4},{4,0},{8,12},{12,8},{16,20},{20,16},{24,28},{28,24},{32,36},... | collective-permute-start | bytes 786440 | tf_op jit(solution)/shard_map/ppermute | solution.py:63
  119.0 28.3 %collective-permute-start.11 = (bf16[256,512]{1,0:T(8,128)(2,1)S(1)}, bf16[256,512]{1,0:T(8,128)(2,1)S(1)}, u32[]{:S(2)}, u32[]{:S(2)}) collective-permute-start(bf16[256,512]{1,0:T(8,128)(2,1)S(1)} %get-tuple-element.46), channel_id=1, source_target_pairs={{4,0},{16,4},{12,8},{24,12},{20,16},{32,20},{28,24},{40,28},{36,32... | collective-permute-start | bytes 786440 | tf_op jit(solution)/shard_map/ppermute | solution.py:63
  123.6 9.0 %collective-permute-start.19 = (bf16[128,512]{1,0:T(8,128)(2,1)S(1)}, bf16[128,512]{1,0:T(8,128)(2,1)S(1)}, u32[]{:S(2)}, u32[]{:S(2)}) collective-permute-start(bf16[128,512]{1,0:T(8,128)(2,1)S(1)} %get-tuple-element.58), channel_id=1, source_target_pairs={{0,8},{4,12},{8,16},{12,20},{16,24},{20,28},{24,0},{28,4},{32,40},... | collective-permute-start | bytes 393224 | tf_op jit(solution)/shard_map/ppermute | solution.py:63
  124.4 8.8 %collective-permute-start.20 = (bf16[128,512]{1,0:T(8,128)(2,1)S(1)}, bf16[128,512]{1,0:T(8,128)(2,1)S(1)}, u32[]{:S(2)}, u32[]{:S(2)}) collective-permute-start(bf16[128,512]{1,0:T(8,128)(2,1)S(1)} %get-tuple-element.59), channel_id=1, source_target_pairs={{0,24},{4,28},{8,0},{12,4},{16,8},{20,12},{24,16},{28,20},{32,56},... | collective-permute-start | bytes 393224 | tf_op jit(solution)/shard_map/ppermute | solution.py:63
  126.9 7.7 %collective-permute-start.21 = (bf16[128,512]{1,0:T(8,128)(2,1)S(1)}, bf16[128,512]{1,0:T(8,128)(2,1)S(1)}, u32[]{:S(2)}, u32[]{:S(2)}) collective-permute-start(bf16[128,512]{1,0:T(8,128)(2,1)S(1)} %get-tuple-element.60), channel_id=1, source_target_pairs={{0,16},{4,20},{8,24},{12,28},{16,0},{20,4},{24,8},{28,12},{32,48},... | collective-permute-start | bytes 393224 | tf_op jit(solution)/shard_map/ppermute | solution.py:63
  127.3 19.9 %collective-permute-start.10 = (bf16[256,512]{1,0:T(8,128)(2,1)S(1)}, bf16[256,512]{1,0:T(8,128)(2,1)S(1)}, u32[]{:S(2)}, u32[]{:S(2)}) collective-permute-start(bf16[256,512]{1,0:T(8,128)(2,1)S(1)} %add_convert_fusion), channel_id=1, source_target_pairs={{8,0},{12,4},{16,8},{20,12},{24,16},{28,20},{32,24},{36,28},{40,32... | collective-permute-start | bytes 786440 | tf_op jit(solution)/shard_map/ppermute | solution.py:63
  132.6 6.1 %collective-permute-start.22 = (bf16[128,512]{1,0:T(8,128)(2,1)S(1)}, bf16[128,512]{1,0:T(8,128)(2,1)S(1)}, u32[]{:S(2)}, u32[]{:S(2)}) collective-permute-start(bf16[128,512]{1,0:T(8,128)(2,1)S(1)} %get-tuple-element.62), channel_id=1, source_target_pairs={{0,32},{4,36},{8,40},{12,44},{16,48},{20,52},{24,56},{28,60},{32,6... | collective-permute-start | bytes 393224 | tf_op jit(solution)/shard_map/ppermute | solution.py:63
  133.2 8.7 %collective-permute-start.23 = (bf16[128,512]{1,0:T(8,128)(2,1)S(1)}, bf16[128,512]{1,0:T(8,128)(2,1)S(1)}, u32[]{:S(2)}, u32[]{:S(2)}) collective-permute-start(bf16[128,512]{1,0:T(8,128)(2,1)S(1)} %get-tuple-element.63), channel_id=1, source_target_pairs={{0,96},{4,100},{8,104},{12,108},{16,112},{20,116},{24,120},{28,124... | collective-permute-start | bytes 393224 | tf_op jit(solution)/shard_map/ppermute | solution.py:63
  134.6 11.8 %collective-permute-start.24 = (bf16[128,512]{1,0:T(8,128)(2,1)S(1)}, bf16[128,512]{1,0:T(8,128)(2,1)S(1)}, u32[]{:S(2)}, u32[]{:S(2)}) collective-permute-start(bf16[128,512]{1,0:T(8,128)(2,1)S(1)} %get-tuple-element.64), channel_id=1, source_target_pairs={{0,64},{4,68},{8,72},{12,76},{16,80},{20,84},{24,88},{28,92},{32,9... | collective-permute-start | bytes 393224 | tf_op jit(solution)/shard_map/ppermute | solution.py:63
  (13 other events, 142.3 us)
Sparse Core Ops, SparseCore 0:
  41.1 41.3 reduce-scatter.1

commit v2 on v1

v2 whole, which is shorter than its diff:
```python
import math

import jax
import jax.numpy as jnp
from jax import lax
from jax.experimental import pallas as pl
from jax.experimental.pallas import tpu as pltpu
from jax.sharding import PartitionSpec as P

BF = jnp.bfloat16
F32 = jnp.float32
HD = 128
TOK = 256
SIDE = 4
SCALE = HD**-0.5
EXP2_SCALE = SCALE * math.log2(math.e)
MASKED = -1e30
VMEM_LIMIT = 24 * 1024 * 1024
VM = pltpu.VMEM
SM = pltpu.SMEM


def dot_nn(a, b):
    return lax.dot_general(a, b, (((1,), (0,)), ((), ())), preferred_element_type=F32)


def dot_nt(a, b):
    return lax.dot_general(a, b, (((1,), (1,)), ((), ())), preferred_element_type=F32)


def seq_route(step):
    pairs = []
    for x in range(SIDE):
        for y in range(SIDE):
            for core in range(2):
                to = step(x, y, core)
                if to is not None:
                    pairs.append(((x * SIDE + y) * 2 + core, (to[0] * SIDE + to[1]) * 2 + to[2]))
    return pairs


def chip_step(x, y, core, chips, to_core):
    chip = x * SIDE + y + chips
    return (chip // SIDE, chip % SIDE, to_core) if 0 <= chip < SIDE * SIDE else None


SWAP = seq_route(lambda x, y, c: (x, y, 1 - c))
NEXT_CHIP = seq_route(lambda x, y, c: chip_step(x, y, c, 1, c))
MIXED = seq_route(lambda x, y, c: (x, y, 1) if c == 0 else chip_step(x, y, c, 2, 0))


def back(route):
    return [(b, a) for a, b in route]


def toward(core):
    return 1 - 2 * core


def along(axis, step):
    if axis == "x":
        return seq_route(lambda x, y, c: ((x + step(c)) % SIDE, y, c))
    return seq_route(lambda x, y, c: (x, (y + step(c)) % SIDE, c))


def same(core):
    return toward(core)


def opposite(core):
    return -toward(core)


def across(core):
    return 2


def seq_send(v, route):
    return lax.ppermute(v, "seq", route)


def kv_send(v, step):
    pairs = []
    for seq in range(2 * SIDE * SIDE):
        for z in range(SIDE):
            pairs.append((seq * SIDE + z, seq * SIDE + (z + step(seq % 2)) % SIDE))
    return lax.ppermute(v, ("seq", "kv"), pairs)


def call(kernel, out_shape, n_in, scratch=(), smem_in=0, flops=1000, transcendentals=0, moved=1000):
    return pl.pallas_call(
        kernel,
        out_shape=out_shape,
        in_specs=[pl.BlockSpec(memory_space=SM)] * smem_in + [pl.BlockSpec(memory_space=VM)] * n_in,
        out_specs=jax.tree.map(lambda _: pl.BlockSpec(memory_space=VM), out_shape),
        scratch_shapes=list(scratch),
        compiler_params=pltpu.CompilerParams(vmem_limit_bytes=VMEM_LIMIT),
        cost_estimate=pl.CostEstimate(
            flops=flops, transcendentals=transcendentals, bytes_accessed=moved
        ),
    )


def doc_starts(lengths, pos):
    def step(n, carry):
        end, start = carry
        end = end + lengths[n]
        return end, jnp.where(pos >= end, end, start)

    return lax.fori_loop(0, 64, step, (jnp.int32(0), jnp.zeros_like(pos)))[1]


def window(info, lengths, blocks):
    seq = info[0]
    core = seq % 2
    first = seq * TOK
    pos = first + lax.broadcasted_iota(jnp.int32, (1, TOK), 1)
    start = doc_starts(lengths, pos)
    own, chip_before, mixed, swapped = blocks
    mixed_at = jnp.where(core == 1, -1, -3)
    swapped_at = jnp.where(core == 1, -3, -1)
    out = []
    for ref, at in ((own, 0), (chip_before, -2), (mixed, mixed_at), (swapped, swapped_at)):
        key_pos = first + at * TOK + lax.broadcasted_iota(jnp.int32, (TOK, 1), 0)
        ok = (key_pos >= start) & (key_pos <= pos)
        out.append((ref, jnp.where(ok, 0.0, MASKED).astype(F32)))
    return out


def heads(ref, g):
    return jnp.concatenate([ref[:, pl.ds((4 * g + h) * HD, HD)] for h in range(4)], axis=0)


def fwd_kernel(info, lengths, q, own, chip_before, mixed, swapped, att, lse, scores, bias):
    for b, (_, mask) in enumerate(window(info, lengths, (own, chip_before, mixed, swapped))):
        bias[b] = mask
    refs = (own, chip_before, mixed, swapped)
    for g in range(2):
        qg = heads(q, g)
        top = jnp.full((1, 4 * TOK), MASKED, F32)
        for b, ref in enumerate(refs):
            s = dot_nt(ref[:, pl.ds(g * HD, HD)], qg) * EXP2_SCALE
            s = s + jnp.concatenate([bias[b]] * 4, axis=1)
            scores[b] = s
            top = jnp.maximum(top, jnp.max(s, axis=0, keepdims=True))
        total = jnp.zeros((1, 4 * TOK), F32)
        o = jnp.zeros((HD, 4 * TOK), F32)
        for b, ref in enumerate(refs):
            e = jnp.exp2(scores[b] - top)
            total = total + jnp.sum(e, axis=0, keepdims=True)
            o = o + dot_nn(ref[:, pl.ds((2 + g) * HD, HD)].T, e.astype(BF))
        lse[g : g + 1, :] = top + jnp.log2(total)
        o = (o / total).T
        for h in range(4):
            att[:, pl.ds((4 * g + h) * HD, HD)] = o[h * TOK : (h + 1) * TOK].astype(BF)


def bwd_kernel(
    info, lengths, q, own, chip_before, mixed, swapped, lse, att, attn_grad,
    dq, d_own, d_chip_before, d_mixed, d_swapped, bias,
):
    for b, (_, mask) in enumerate(window(info, lengths, (own, chip_before, mixed, swapped))):
        bias[b] = mask
    refs = (own, chip_before, mixed, swapped)
    outs = (d_own, d_chip_before, d_mixed, d_swapped)
    for g in range(2):
        qg = heads(q, g)
        og = heads(attn_grad, g)
        ag = heads(att, g)
        dots = jnp.sum((og.astype(F32) * ag.astype(F32)).T, axis=0, keepdims=True)
        row_lse = lse[g : g + 1, :]
        dqt = jnp.zeros((HD, 4 * TOK), F32)
        for b, (ref, out) in enumerate(zip(refs, outs)):
            kb = ref[:, pl.ds(g * HD, HD)]
            vb = ref[:, pl.ds((2 + g) * HD, HD)]
            s = dot_nt(kb, qg) * EXP2_SCALE + jnp.concatenate([bias[b]] * 4, axis=1)
            p = jnp.exp2(s - row_lse)
            out[:, pl.ds((2 + g) * HD, HD)] = dot_nn(p.astype(BF), og).astype(out.dtype)
            ds = (p * (dot_nt(vb, og) - dots) * SCALE).astype(BF)
            out[:, pl.ds(g * HD, HD)] = dot_nn(ds, qg).astype(out.dtype)
            dqt = dqt + dot_nn(kb.T, ds)
        dqs = dqt.T
        for h in range(4):
            dq[:, pl.ds((4 * g + h) * HD, HD)] = dqs[h * TOK : (h + 1) * TOK].astype(BF)


def finish_kernel(own, chip_before, mixed, dk, dv):
    total = own[...] + chip_before[...].astype(F32) + mixed[...].astype(F32)
    dk[...] = total[:, : 2 * HD].astype(BF)
    dv[...] = total[:, 2 * HD :].astype(BF)


def chunk(ref, at, size):
    return ref[pl.ds(pl.multiple_of((at % SIDE) * size, size), size), :]


def out_first_kernel(info, att, w, across_out, opposite_out):
    z, way = info[1], 1 - 2 * (info[0] % 2)
    rows = w.shape[0] // SIDE
    across_out[...] = dot_nt(att[...], chunk(w, z + 2, rows)).astype(BF)
    opposite_out[...] = dot_nt(att[...], chunk(w, z + SIDE - way, rows)).astype(BF)


def out_second_kernel(info, att, w, relayed, same_out, own):
    z, way = info[1], 1 - 2 * (info[0] % 2)
    rows = w.shape[0] // SIDE
    same = dot_nt(att[...], chunk(w, z + SIDE + way, rows)) + relayed[...].astype(F32)
    same_out[...] = same.astype(BF)
    own[...] = dot_nt(att[...], chunk(w, z, rows))


def attn_grad_kernel(info, g, first, second, third, w, out):
    z, way = info[1], 1 - 2 * (info[0] % 2)
    rows = w.shape[0] // SIDE
    total = dot_nn(g[...], chunk(w, z, rows))
    total = total + dot_nn(first[...], chunk(w, z + SIDE - way, rows))
    total = total + dot_nn(second[...], chunk(w, z + SIDE + way, rows))
    total = total + dot_nn(third[...], chunk(w, z + 2, rows))
    out[...] = total.astype(BF)


def place(info):
    seq = info[0]
    core = seq % 2
    return seq // (2 * SIDE), (seq // 2) % SIDE, info[1], core, 1 - 2 * core


def weight_terms(gt, a, k, by_x):
    half = a.shape[1] // 2
    if by_x:
        return dot_nn(gt[k % SIDE], a[:, :half])
    rows = pl.ds(pl.multiple_of((k % SIDE) * HD, HD), HD)
    lhs = jnp.concatenate([gt[x, rows, :] for x in range(SIDE)], axis=0)
    return dot_nn(lhs, a[:, half:])


def weight_across_kernel(info, *refs):
    here, there, att, att_there, gt, a, x_out, y_out = refs[:4], refs[4:8], *refs[8:]
    x, y, z, core, way = place(info)
    a[:TOK] = att[...]
    a[TOK:] = att_there[...]
    for t, sources, w in ((0, here, way), (1, there, -way)):
        for source, at in zip(sources, (z, z + SIDE - w, z + SIDE + w, z + 2)):
            for k in range(SIDE):
                columns = pl.ds(pl.multiple_of(k * 2 * HD + core * HD, HD), HD)
                gt[at % SIDE, k * HD : (k + 1) * HD, t * TOK : (t + 1) * TOK] = source[:, columns].T
    x_out[...] = weight_terms(gt, a, x + 2, True).astype(BF)
    y_out[...] = weight_terms(gt, a, y + 2, False).astype(BF)


def weight_opposite_kernel(info, gt, a, x_out, y_out):
    x, y, z, core, way = place(info)
    x_out[...] = weight_terms(gt, a, x + SIDE - way, True).astype(BF)
    y_out[...] = weight_terms(gt, a, y + SIDE - way, False).astype(BF)


def weight_same_kernel(info, gt, a, x_relayed, y_relayed, x_out, y_out, x_own, y_own):
    x, y, z, core, way = place(info)
    x_same = weight_terms(gt, a, x + SIDE + way, True) + x_relayed[...].astype(F32)
    x_out[...] = x_same.astype(BF)
    y_same = weight_terms(gt, a, y + SIDE + way, False) + y_relayed[...].astype(F32)
    y_out[...] = y_same.astype(BF)
    x_own[...] = weight_terms(gt, a, x, True)
    y_own[...] = weight_terms(gt, a, y, False)


def weight_sum_kernel(info, *refs):
    x, y, z, core, way = place(info)
    for sources, outs, at in ((refs[:3], refs[6:10], y), (refs[3:6], refs[10:14], x)):
        for out, to in zip(outs, (at + SIDE + way, at + SIDE - way, at + 2, at)):
            total = chunk(sources[0], to, HD)
            for s in sources[1:]:
                total = total + chunk(s, to, HD).astype(F32)
            out[...] = total.astype(out.dtype)


def sum_last_kernel(*refs):
    out = refs[8]
    half = out.shape[1] // 2
    for i in range(2):
        total = refs[4 * i][...]
        for s in refs[4 * i + 1 : 4 * i + 4]:
            total = total + s[...].astype(F32)
        out[:, i * half : (i + 1) * half] = total.astype(BF)


def weight_gradient(info, here, there, att, att_there):
    cols = att.shape[1]
    half = cols // 2
    piece = jax.ShapeDtypeStruct((4 * HD, half), BF)
    piece32 = jax.ShapeDtypeStruct((4 * HD, half), F32)
    gt, a, x_across, y_across = call(
        weight_across_kernel,
        [
            jax.ShapeDtypeStruct((SIDE, 4 * HD, 2 * TOK), BF),
            jax.ShapeDtypeStruct((2 * TOK, cols), BF),
            piece,
            piece,
        ],
        10,
        smem_in=1,
    )(info, *here, *there, att, att_there)
    x_relayed = seq_send(x_across, along("x", same))
    y_relayed = seq_send(y_across, along("y", same))
    x_opp, y_opp = call(weight_opposite_kernel, [piece] * 2, 2, smem_in=1)(info, gt, a)
    x_from_opp = seq_send(x_opp, along("x", opposite))
    y_from_opp = seq_send(y_opp, along("y", opposite))
    x_same, y_same, x_own, y_own = call(
        weight_same_kernel, [piece] * 2 + [piece32] * 2, 4, smem_in=1
    )(info, gt, a, x_relayed, y_relayed)
    x_from_same = seq_send(x_same, along("x", same))
    y_from_same = seq_send(y_same, along("y", same))
    strip = jax.ShapeDtypeStruct((HD, half), BF)
    strip32 = jax.ShapeDtypeStruct((HD, half), F32)
    sums = call(weight_sum_kernel, ([strip] * 3 + [strip32]) * 2, 6, smem_in=1)(
        info, x_own, x_from_opp, x_from_same, y_own, y_from_opp, y_from_same
    )
    last = []
    for axis, terms in (("y", sums[:4]), ("x", sums[4:])):
        last.append(terms[3])
        for term, step in zip(terms, (same, opposite, across)):
            last.append(seq_send(term, along(axis, step)))
    return call(sum_last_kernel, jax.ShapeDtypeStruct((HD, cols), BF), 8)(*last)


def per_device(queries, keys, values, out_weight, out_grad, doc_lengths):
    shape = jax.ShapeDtypeStruct
    info = jnp.stack([lax.axis_index("seq"), lax.axis_index("kv")]).astype(jnp.int32)
    cols = queries.shape[1]

    first = kv_send(out_grad, same)
    second = kv_send(out_grad, opposite)
    third = kv_send(first, same)
    here = (out_grad, first, second, third)
    there = tuple(seq_send(v, SWAP) for v in here)

    kv = jnp.concatenate([keys, values], axis=1)
    chip_before = seq_send(kv, NEXT_CHIP)
    mixed = seq_send(kv, MIXED)
    swapped = seq_send(chip_before, SWAP)

    att, lse = call(
        fwd_kernel,
        [shape((TOK, cols), BF), shape((2, 4 * TOK), F32)],
        5,
        scratch=[VM((4, TOK, 4 * TOK), F32), VM((4, TOK, TOK), F32)],
        smem_in=2,
    )(info, doc_lengths, queries, kv, chip_before, mixed, swapped)
    att_there = seq_send(att, SWAP)

    block = shape((TOK, cols), BF)
    out_across, out_opp = call(out_first_kernel, [block] * 2, 2, smem_in=1)(info, att, out_weight)
    out_relayed = kv_send(out_across, same)
    out_from_opp = kv_send(out_opp, opposite)
    out_same, out_own = call(out_second_kernel, [block, shape((TOK, cols), F32)], 3, smem_in=1)(
        info, att, out_weight, out_relayed
    )
    out_from_same = kv_send(out_same, same)
    layer_out = (out_own + out_from_opp.astype(F32) + out_from_same.astype(F32)).astype(BF)

    weight_grad = weight_gradient(info, here, there, att, att_there)

    attn_grad = call(attn_grad_kernel, block, 5, smem_in=1)(info, *here, out_weight)
    query_grad, d_own, d_chip_before, d_mixed, d_swapped = call(
        bwd_kernel,
        [
            block,
            shape((TOK, 4 * HD), F32),
            shape((TOK, 4 * HD), F32),
            shape((TOK, 4 * HD), BF),
            shape((TOK, 4 * HD), BF),
        ],
        8,
        scratch=[VM((4, TOK, TOK), F32)],
        smem_in=2,
    )(info, doc_lengths, queries, kv, chip_before, mixed, swapped, lse, att, attn_grad)
    from_mixed = seq_send(d_mixed, back(MIXED))
    from_swapped = seq_send(d_swapped, SWAP)
    from_chip = seq_send((d_chip_before + from_swapped.astype(F32)).astype(BF), back(NEXT_CHIP))
    key_grad, value_grad = call(finish_kernel, [shape((TOK, 2 * HD), BF)] * 2, 3)(
        d_own, from_chip, from_mixed
    )
    return (layer_out, query_grad, key_grad, value_grad, weight_grad)


def solution(mesh):
    placed = (P("seq", "kv"), P("seq", "kv"), P("seq", "kv"), P(None, "kv"), P("seq", "kv"), P())
    return jax.shard_map(
        per_device,
        mesh=mesh,
        in_specs=placed,
        out_specs=(P("seq", "kv"),) * 5,
        check_vma=False,
    )
```

time: 156 us -> 97.7 us (0.63)
  the two profiles are of different devices: /device:TPU:6 before, /device:TPU:1 now
where the time goes in v2:
time: 97.7 us; the launch traced here: 97.3 us
  starting transfers between devices  40.6 us (42%)
  Pallas kernels  25.5 us (26%)
  waiting for transfers between devices  21.1 us (22%)
  local copies, waits for them, and re-layouts  7.96 us (8%)
  other arithmetic  1.19 us (1%)
    ppermute x23, starting transfers between devices, seq_send(): return lax.ppermute(v, 'seq', route)  27.9 us
    ppermute x23, waiting for transfers between devices, seq_send(): return lax.ppermute(v, 'seq', route)  15.2 us
    ppermute x6, starting transfers between devices, kv_send(): return lax.ppermute(v, ('seq', 'kv'), pairs)  12.8 us
    pallas_call x1, Pallas kernels, per_device(): call(bwd_kernel, [block, shape((TOK, 4 * HD), F32), shape((TOK, 4 * HD),...  7.23 us
    unnamed x15, local copies, waits for them, and re-layouts  7.05 us
    ppermute x6, waiting for transfers between devices, kv_send(): return lax.ppermute(v, ('seq', 'kv'), pairs)  5.96 us
    pallas_call x1, Pallas kernels, per_device(): call(fwd_kernel, [shape((TOK, cols), BF), shape((2, 4 * TOK), F32)], 5, s...  4.36 us
    pallas_call x1, Pallas kernels, per_device(): call(attn_grad_kernel, block, 5, smem_in=1)(info, *here, out_weight)  2.94 us
  transfers between devices with their start and end apart: 29, of which 10 were waited for; matrix products, arithmetic and copies ran while one was open for 3% of the time, Pallas kernels for 24%

profile of v2, /device:TPU:1, one launch (start us, length us, event | category | flops | bytes accessed | tf_op | source)
XLA Modules:
  0.0 97.3 jit_solution(3722345732199811091)
XLA Ops:
  0.6 4.7 %collective-permute-start.6 = (bf16[256,1024]{1,0:T(8,128)(2,1)}, bf16[256,1024]{1,0:T(8,128)(2,1)S(1)}, u32[]{:S(2)}, u32[]{:S(2)}) collective-permute-start(bf16[256,1024]{1,0:T(8,128)(2,1)} %refs_0_.1), channel_id=1, source_target_pairs={{0,1},{1,2},{2,3},{3,0},{4,7},{5,4},{6,5},{7,6},{8,9},{9,10},{10,1... | collective-permute-start | bytes 1572872 | tf_op jit(solution)/shard_map/ppermute | solution.py:87
  7.1 3.2 %collective-permute-start = (bf16[256,512]{1,0:T(8,128)(2,1)S(1)}, bf16[256,512]{1,0:T(8,128)(2,1)S(1)}, u32[]{:S(2)}, u32[]{:S(2)}) collective-permute-start(bf16[256,512]{1,0:T(8,128)(2,1)S(1)} %constant_dynamic-update-slice_fusion.own), channel_id=1, source_target_pairs={{0,8},{4,12},{8,16},{12,20},{16,24},{20,28},{24,32},{28,36},{32,40... | collective-permute-start | bytes 786440 | tf_op jit(solution)/shard_map/ppermute | solution.py:79
  11.7 3.0 %collective-permute-start.8 = (bf16[256,1024]{1,0:T(8,128)(2,1)S(1)}, bf16[256,1024]{1,0:T(8,128)(2,1)S(1)}, u32[]{:S(2)}, u32[]{:S(2)}) collective-permute-start(bf16[256,1024]{1,0:T(8,128)(2,1)S(1)} %collective-permute-done.6.first.refs_1_), channel_id=1, source_target_pairs={{0,1},{1,2},{2,3},{3,0},{4,7},{5,4},{6,5},{7,6},{8,9},{9,10},{10,1... | collective-permute-start | bytes 1572872 | tf_op jit(solution)/shard_map/ppermute | solution.py:87
  14.7 4.9 %collective-permute-start.1 = (bf16[256,512]{1,0:T(8,128)(2,1)S(1)}, bf16[256,512]{1,0:T(8,128)(2,1)S(1)}, u32[]{:S(2)}, u32[]{:S(2)}) collective-permute-start(bf16[256,512]{1,0:T(8,128)(2,1)S(1)} %constant_dynamic-update-slice_fusion.own), channel_id=1, source_target_pairs={{0,4},{4,16},{8,12},{12,24},{16,20},{20,32},{24,28},{28,40},{32,36... | collective-permute-start | bytes 786440 | tf_op jit(solution)/shard_map/ppermute | solution.py:79
  20.3 2.6 %collective-permute-done.1.mixed = bf16[256,512]{1,0:T(8,128)(2,1)S(1)} collective-permute-done((bf16[256,512]{1,0:T(8,128)(2,1)S(1)}, bf16[256,512]{1,0:T(8,128)(2,1)S(1)}, u32[]{:S(2)}, u32[]{:S(2)}) %collective-permute-start.1) | collective-permute-done | bytes 262176 | tf_op jit(solution)/shard_map/ppermute | solution.py:79
  24.6 4.4 %shard_map.101 = (bf16[256,1024]{1,0:T(8,128)(2,1)S(1)}, f32[2,1024]{1,0:T(2,128)S(1)}) custom-call(s32[2]{0:T(128)S(1)} %pad_add_fusion.info, s32[64]{0:T(128)S(1)} %copy-done.6, bf16[256,1024]{1,0:T(8,128)(2,1)S(1)} %copy-done.2, bf16[256,512]{1,0:T(8,128)(2,1)S(1)} %constant_dynamic-update-slice_fusion.own, ...), custom_call_target="tpu_custom_call" | custom-call | flops 1000 | bytes 1000 | tf_op jit(solution)/shard_map/pallas_call | solution.py:342
  34.3 1.8 %shard_map.107 = (bf16[4,512,512]{2,1,0:T(8,128)(2,1)S(1)}, bf16[512,1024]{1,0:T(8,128)(2,1)S(1)}, bf16[512,512]{1,0:T(8,128)(2,1)S(1)}, bf16[512,512]{1,0:T(8,128)(2,1)S(1)}) custom-call(s32[2]{0:T(128)S(1)} %pad_add_fusion.info, bf16[256,1024]{1,0:T(8,128)(2,1)S(1)} %copy-done.4, bf16[256,1024]{1,0:T(8,128)(2,1)S(1)} %collective-permute-done.6.first.refs_1_, ...), custom_call_target="tpu_custom_call" | custom-call | flops 1000 | bytes 1000 | tf_op jit(solution)/shard_map/pallas_call | solution.py:292
  36.1 4.0 %collective-permute-start.17 = (bf16[512,512]{1,0:T(8,128)(2,1)S(1)}, bf16[512,512]{1,0:T(8,128)(2,1)S(1)}, u32[]{:S(2)}, u32[]{:S(2)}) collective-permute-start(bf16[512,512]{1,0:T(8,128)(2,1)S(1)} %get-tuple-element.51), channel_id=1, source_target_pairs={{0,32},{4,100},{8,40},{12,108},{16,48},{20,116},{24,56},{28,124},{... | collective-permute-start | bytes 1572872 | tf_op jit(solution)/shard_map/ppermute | solution.py:79
  40.1 3.7 %collective-permute-start.18 = (bf16[512,512]{1,0:T(8,128)(2,1)S(1)}, bf16[512,512]{1,0:T(8,128)(2,1)S(1)}, u32[]{:S(2)}, u32[]{:S(2)}) collective-permute-start(bf16[512,512]{1,0:T(8,128)(2,1)S(1)} %get-tuple-element.52), channel_id=1, source_target_pairs={{0,8},{4,28},{8,16},{12,4},{16,24},{20,12},{24,0},{28,20},{32,40},... | collective-permute-start | bytes 1572872 | tf_op jit(solution)/shard_map/ppermute | solution.py:79
  43.8 3.4 %copy-done = bf16[4096,1024]{1,0:T(8,128)(2,1)S(1)} copy-done((bf16[4096,1024]{1,0:T(8,128)(2,1)S(1)}, bf16[4096,1024]{1,0:T(8,128)(2,1)}, u32[]{:S(2)}) %copy-start) | copy-done | bytes 8388632
  47.2 1.8 %shard_map.102 = (bf16[256,1024]{1,0:T(8,128)(2,1)S(1)}, bf16[256,1024]{1,0:T(8,128)(2,1)S(1)}) custom-call(s32[2]{0:T(128)S(1)} %pad_add_fusion.info, bf16[256,1024]{1,0:T(8,128)(2,1)S(1)} %get-tuple-element.36.att.refs_8_, bf16[4096,1024]{1,0:T(8,128)(2,1)S(1)} %copy-done), custom_call_target="tpu_custom_call" | custom-call | flops 1000 | bytes 1000 | tf_op jit(solution)/shard_map/pallas_call | solution.py:352
  49.1 2.3 %collective-permute-start.3 = (bf16[256,1024]{1,0:T(8,128)(2,1)S(1)}, bf16[256,1024]{1,0:T(8,128)(2,1)S(1)}, u32[]{:S(2)}, u32[]{:S(2)}) collective-permute-start(bf16[256,1024]{1,0:T(8,128)(2,1)S(1)} %get-tuple-element.37), channel_id=1, source_target_pairs={{0,1},{1,2},{2,3},{3,0},{4,7},{5,4},{6,5},{7,6},{8,9},{9,10},{10,1... | collective-permute-start | bytes 1572872 | tf_op jit(solution)/shard_map/ppermute | solution.py:87
  52.9 2.9 %shard_map.104.attn_grad = bf16[256,1024]{1,0:T(8,128)(2,1)S(1)} custom-call(s32[2]{0:T(128)S(1)} %pad_add_fusion.info, bf16[256,1024]{1,0:T(8,128)(2,1)S(1)} %copy-done.5, bf16[256,1024]{1,0:T(8,128)(2,1)S(1)} %collective-permute-done.6.first.refs_1_, bf16[256,1024]{1,0:T(8,128)(2,1)S(1)} %collective-permute-done.7.second.refs_2_, ...), custom_call_target="tpu_custom_call" | custom-call | flops 1000 | bytes 1000 | tf_op jit(solution)/shard_map/pallas_call | solution.py:363
  55.9 7.2 %shard_map.105 = (bf16[256,1024]{1,0:T(8,128)(2,1)}, f32[256,512]{1,0:T(8,128)S(1)}, f32[256,512]{1,0:T(8,128)S(1)}, bf16[256,512]{1,0:T(8,128)(2,1)S(1)}, bf16[256,512]{1,0:T(8,128)(2,1)S(1)}) custom-call(s32[2]{0:T(128)S(1)} %pad_add_fusion.info, s32[64]{0:T(128)S(1)} %copy-done.6, bf16[256,1024]{1,0:T(8,128)(2,1)S(1)} %copy-done.3, ...), custom_call_target="tpu_custom_call" | custom-call | flops 1000 | bytes 1000 | tf_op jit(solution)/shard_map/pallas_call | solution.py:364
  64.0 1.8 %shard_map.108 = (bf16[512,512]{1,0:T(8,128)(2,1)S(1)}, bf16[512,512]{1,0:T(8,128)(2,1)S(1)}, f32[512,512]{1,0:T(8,128)S(1)}, f32[512,512]{1,0:T(8,128)S(1)}) custom-call(s32[2]{0:T(128)S(1)} %pad_add_fusion.info, bf16[4,512,512]{2,1,0:T(8,128)(2,1)S(1)} %get-tuple-element.49.gt, bf16[512,1024]{1,0:T(8,128)(2,1)S(1)} %get-tuple-element.50.a, ...), custom_call_target="tpu_custom_call" | custom-call | flops 1000 | bytes 1000 | tf_op jit(solution)/shard_map/pallas_call | solution.py:308
  65.8 1.7 %collective-permute-start.20 = (bf16[512,512]{1,0:T(8,128)(2,1)S(1)}, bf16[512,512]{1,0:T(8,128)(2,1)S(1)}, u32[]{:S(2)}, u32[]{:S(2)}) collective-permute-start(bf16[512,512]{1,0:T(8,128)(2,1)S(1)} %get-tuple-element.55), channel_id=1, source_target_pairs={{0,32},{4,100},{8,40},{12,108},{16,48},{20,116},{24,56},{28,124},{... | collective-permute-start | bytes 1572872 | tf_op jit(solution)/shard_map/ppermute | solution.py:79
  67.6 2.5 %collective-permute-start.22 = (bf16[512,512]{1,0:T(8,128)(2,1)S(1)}, bf16[512,512]{1,0:T(8,128)(2,1)S(1)}, u32[]{:S(2)}, u32[]{:S(2)}) collective-permute-start(bf16[512,512]{1,0:T(8,128)(2,1)S(1)} %get-tuple-element.58), channel_id=1, source_target_pairs={{0,8},{4,28},{8,16},{12,4},{16,24},{20,12},{24,0},{28,20},{32,40},... | collective-permute-start | bytes 1572872 | tf_op jit(solution)/shard_map/ppermute | solution.py:79
  70.6 1.8 %shard_map.103 = (bf16[256,1024]{1,0:T(8,128)(2,1)S(1)}, f32[256,1024]{1,0:T(8,128)S(1)}) custom-call(s32[2]{0:T(128)S(1)} %pad_add_fusion.info, bf16[256,1024]{1,0:T(8,128)(2,1)S(1)} %get-tuple-element.36.att.refs_8_, bf16[4096,1024]{1,0:T(8,128)(2,1)S(1)} %copy-done.1, bf16[256,1024]{1,0:T(8,128)(2,1)S(1)} %collective-permute-done.3.relayed), custom_call_target="tpu_custom_call" | custom-call | flops 1000 | bytes 1000 | tf_op jit(solution)/shard_map/pallas_call | solution.py:355
  72.4 2.3 %collective-permute-start.5 = (bf16[256,1024]{1,0:T(8,128)(2,1)S(1)}, bf16[256,1024]{1,0:T(8,128)(2,1)S(1)}, u32[]{:S(2)}, u32[]{:S(2)}) collective-permute-start(bf16[256,1024]{1,0:T(8,128)(2,1)S(1)} %get-tuple-element.40), channel_id=1, source_target_pairs={{0,1},{1,2},{2,3},{3,0},{4,7},{5,4},{6,5},{7,6},{8,9},{9,10},{10,1... | collective-permute-start | bytes 1572872 | tf_op jit(solution)/shard_map/ppermute | solution.py:87
  74.7 1.9 %collective-permute-start.11 = (bf16[256,512]{1,0:T(8,128)(2,1)S(1)}, bf16[256,512]{1,0:T(8,128)(2,1)S(1)}, u32[]{:S(2)}, u32[]{:S(2)}) collective-permute-start(bf16[256,512]{1,0:T(8,128)(2,1)S(1)} %get-tuple-element.46), channel_id=1, source_target_pairs={{4,0},{16,4},{12,8},{24,12},{20,16},{32,20},{28,24},{40,28},{36,32... | collective-permute-start | bytes 786440 | tf_op jit(solution)/shard_map/ppermute | solution.py:79
  80.6 4.6 %collective-permute-done.4 = bf16[256,1024]{1,0:T(8,128)(2,1)S(1)} collective-permute-done((bf16[256,1024]{1,0:T(8,128)(2,1)S(1)}, bf16[256,1024]{1,0:T(8,128)(2,1)S(1)}, u32[]{:S(2)}, u32[]{:S(2)}) %collective-permute-start.4) | collective-permute-done | bytes 524320 | tf_op jit(solution)/shard_map/ppermute | solution.py:87
  85.3 3.1 %collective-permute-done.10.chip_before = bf16[256,512]{1,0:T(8,128)(2,1)S(1)} collective-permute-done((bf16[256,512]{1,0:T(8,128)(2,1)S(1)}, bf16[256,512]{1,0:T(8,128)(2,1)S(1)}, u32[]{:S(2)}, u32[]{:S(2)}) %collective-permute-start.10) | collective-permute-done | bytes 262176 | tf_op jit(solution)/shard_map/ppermute | solution.py:79
  88.4 2.8 %collective-permute-done.23.refs_1_ = bf16[128,512]{1,0:T(8,128)(2,1)S(1)} collective-permute-done((bf16[128,512]{1,0:T(8,128)(2,1)S(1)}, bf16[128,512]{1,0:T(8,128)(2,1)S(1)}, u32[]{:S(2)}, u32[]{:S(2)}) %collective-permute-start.23) | collective-permute-done | bytes 131104 | tf_op jit(solution)/shard_map/ppermute | solution.py:79
  93.0 2.0 %collective-permute-done.27.refs_6_ = bf16[128,512]{1,0:T(8,128)(2,1)S(1)} collective-permute-done((bf16[128,512]{1,0:T(8,128)(2,1)S(1)}, bf16[128,512]{1,0:T(8,128)(2,1)S(1)}, u32[]{:S(2)}, u32[]{:S(2)}) %collective-permute-start.27) | collective-permute-done | bytes 131104 | tf_op jit(solution)/shard_map/ppermute | solution.py:79
  (64 shorter events, 21.9 us)
Async XLA Ops:
  0.6 11.1 %collective-permute-start.6 = (bf16[256,1024]{1,0:T(8,128)(2,1)}, bf16[256,1024]{1,0:T(8,128)(2,1)S(1)}, u32[]{:S(2)}, u32[]{:S(2)}) collective-permute-start(bf16[256,1024]{1,0:T(8,128)(2,1)} %refs_0_.1), channel_id=1, source_target_pairs={{0,1},{1,2},{2,3},{3,0},{4,7},{5,4},{6,5},{7,6},{8,9},{9,10},{10,1... | collective-permute-start | bytes 1572872 | tf_op jit(solution)/shard_map/ppermute | solution.py:87
  7.1 12.5 %collective-permute-start = (bf16[256,512]{1,0:T(8,128)(2,1)S(1)}, bf16[256,512]{1,0:T(8,128)(2,1)S(1)}, u32[]{:S(2)}, u32[]{:S(2)}) collective-permute-start(bf16[256,512]{1,0:T(8,128)(2,1)S(1)} %constant_dynamic-update-slice_fusion.own), channel_id=1, source_target_pairs={{0,8},{4,12},{8,16},{12,20},{16,24},{20,28},{24,32},{28,36},{32,40... | collective-permute-start | bytes 786440 | tf_op jit(solution)/shard_map/ppermute | solution.py:79
  10.3 19.2 %collective-permute-start.7 = (bf16[256,1024]{1,0:T(8,128)(2,1)}, bf16[256,1024]{1,0:T(8,128)(2,1)S(1)}, u32[]{:S(2)}, u32[]{:S(2)}) collective-permute-start(bf16[256,1024]{1,0:T(8,128)(2,1)} %refs_0_.1), channel_id=1, source_target_pairs={{0,3},{1,0},{2,1},{3,2},{4,5},{5,6},{6,7},{7,4},{8,11},{9,8},{10,9... | collective-permute-start | bytes 1572872 | tf_op jit(solution)/shard_map/ppermute | solution.py:87
  11.7 17.9 %collective-permute-start.8 = (bf16[256,1024]{1,0:T(8,128)(2,1)S(1)}, bf16[256,1024]{1,0:T(8,128)(2,1)S(1)}, u32[]{:S(2)}, u32[]{:S(2)}) collective-permute-start(bf16[256,1024]{1,0:T(8,128)(2,1)S(1)} %collective-permute-done.6.first.refs_1_), channel_id=1, source_target_pairs={{0,1},{1,2},{2,3},{3,0},{4,7},{5,4},{6,5},{7,6},{8,9},{9,10},{10,1... | collective-permute-start | bytes 1572872 | tf_op jit(solution)/shard_map/ppermute | solution.py:87
  14.7 8.2 %collective-permute-start.1 = (bf16[256,512]{1,0:T(8,128)(2,1)S(1)}, bf16[256,512]{1,0:T(8,128)(2,1)S(1)}, u32[]{:S(2)}, u32[]{:S(2)}) collective-permute-start(bf16[256,512]{1,0:T(8,128)(2,1)S(1)} %constant_dynamic-update-slice_fusion.own), channel_id=1, source_target_pairs={{0,4},{4,16},{8,12},{12,24},{16,20},{20,32},{24,28},{28,40},{32,36... | collective-permute-start | bytes 786440 | tf_op jit(solution)/shard_map/ppermute | solution.py:79
  19.7 10.4 %collective-permute-start.12 = (bf16[256,1024]{1,0:T(8,128)(2,1)}, bf16[256,1024]{1,0:T(8,128)(2,1)S(1)}, u32[]{:S(2)}, u32[]{:S(2)}) collective-permute-start(bf16[256,1024]{1,0:T(8,128)(2,1)} %refs_0_.1), channel_id=1, source_target_pairs={{0,4},{4,0},{8,12},{12,8},{16,20},{20,16},{24,28},{28,24},{32,36},... | collective-permute-start | bytes 1572872 | tf_op jit(solution)/shard_map/ppermute | solution.py:79
  36.1 27.0 %collective-permute-start.17 = (bf16[512,512]{1,0:T(8,128)(2,1)S(1)}, bf16[512,512]{1,0:T(8,128)(2,1)S(1)}, u32[]{:S(2)}, u32[]{:S(2)}) collective-permute-start(bf16[512,512]{1,0:T(8,128)(2,1)S(1)} %get-tuple-element.51), channel_id=1, source_target_pairs={{0,32},{4,100},{8,40},{12,108},{16,48},{20,116},{24,56},{28,124},{... | collective-permute-start | bytes 1572872 | tf_op jit(solution)/shard_map/ppermute | solution.py:79
  40.1 24.0 %collective-permute-start.18 = (bf16[512,512]{1,0:T(8,128)(2,1)S(1)}, bf16[512,512]{1,0:T(8,128)(2,1)S(1)}, u32[]{:S(2)}, u32[]{:S(2)}) collective-permute-start(bf16[512,512]{1,0:T(8,128)(2,1)S(1)} %get-tuple-element.52), channel_id=1, source_target_pairs={{0,8},{4,28},{8,16},{12,4},{16,24},{20,12},{24,0},{28,20},{32,40},... | collective-permute-start | bytes 1572872 | tf_op jit(solution)/shard_map/ppermute | solution.py:79
  49.1 18.5 %collective-permute-start.3 = (bf16[256,1024]{1,0:T(8,128)(2,1)S(1)}, bf16[256,1024]{1,0:T(8,128)(2,1)S(1)}, u32[]{:S(2)}, u32[]{:S(2)}) collective-permute-start(bf16[256,1024]{1,0:T(8,128)(2,1)S(1)} %get-tuple-element.37), channel_id=1, source_target_pairs={{0,1},{1,2},{2,3},{3,0},{4,7},{5,4},{6,5},{7,6},{8,9},{9,10},{10,1... | collective-permute-start | bytes 1572872 | tf_op jit(solution)/shard_map/ppermute | solution.py:87
  52.6 19.9 %collective-permute-start.19 = (bf16[512,512]{1,0:T(8,128)(2,1)S(1)}, bf16[512,512]{1,0:T(8,128)(2,1)S(1)}, u32[]{:S(2)}, u32[]{:S(2)}) collective-permute-start(bf16[512,512]{1,0:T(8,128)(2,1)S(1)} %get-tuple-element.54), channel_id=1, source_target_pairs={{0,96},{4,36},{8,104},{12,44},{16,112},{20,52},{24,120},{28,60},{3... | collective-permute-start | bytes 1572872 | tf_op jit(solution)/shard_map/ppermute | solution.py:79
  52.7 22.0 %collective-permute-start.21 = (bf16[512,512]{1,0:T(8,128)(2,1)S(1)}, bf16[512,512]{1,0:T(8,128)(2,1)S(1)}, u32[]{:S(2)}, u32[]{:S(2)}) collective-permute-start(bf16[512,512]{1,0:T(8,128)(2,1)S(1)} %get-tuple-element.57), channel_id=1, source_target_pairs={{0,24},{4,12},{8,0},{12,20},{16,8},{20,28},{24,16},{28,4},{32,56},... | collective-permute-start | bytes 1572872 | tf_op jit(solution)/shard_map/ppermute | solution.py:79
  63.1 7.0 %collective-permute-start.9 = (bf16[256,512]{1,0:T(8,128)(2,1)S(1)}, bf16[256,512]{1,0:T(8,128)(2,1)S(1)}, u32[]{:S(2)}, u32[]{:S(2)}) collective-permute-start(bf16[256,512]{1,0:T(8,128)(2,1)S(1)} %get-tuple-element.45), channel_id=1, source_target_pairs={{0,4},{4,0},{8,12},{12,8},{16,20},{20,16},{24,28},{28,24},{32,36},... | collective-permute-start | bytes 786440 | tf_op jit(solution)/shard_map/ppermute | solution.py:79
  65.8 10.9 %collective-permute-start.20 = (bf16[512,512]{1,0:T(8,128)(2,1)S(1)}, bf16[512,512]{1,0:T(8,128)(2,1)S(1)}, u32[]{:S(2)}, u32[]{:S(2)}) collective-permute-start(bf16[512,512]{1,0:T(8,128)(2,1)S(1)} %get-tuple-element.55), channel_id=1, source_target_pairs={{0,32},{4,100},{8,40},{12,108},{16,48},{20,116},{24,56},{28,124},{... | collective-permute-start | bytes 1572872 | tf_op jit(solution)/shard_map/ppermute | solution.py:79
  67.6 10.4 %collective-permute-start.22 = (bf16[512,512]{1,0:T(8,128)(2,1)S(1)}, bf16[512,512]{1,0:T(8,128)(2,1)S(1)}, u32[]{:S(2)}, u32[]{:S(2)}) collective-permute-start(bf16[512,512]{1,0:T(8,128)(2,1)S(1)} %get-tuple-element.58), channel_id=1, source_target_pairs={{0,8},{4,28},{8,16},{12,4},{16,24},{20,12},{24,0},{28,20},{32,40},... | collective-permute-start | bytes 1572872 | tf_op jit(solution)/shard_map/ppermute | solution.py:79
  70.1 15.1 %collective-permute-start.4 = (bf16[256,1024]{1,0:T(8,128)(2,1)S(1)}, bf16[256,1024]{1,0:T(8,128)(2,1)S(1)}, u32[]{:S(2)}, u32[]{:S(2)}) collective-permute-start(bf16[256,1024]{1,0:T(8,128)(2,1)S(1)} %get-tuple-element.39), channel_id=1, source_target_pairs={{0,3},{1,0},{2,1},{3,2},{4,5},{5,6},{6,7},{7,4},{8,11},{9,8},{10,9... | collective-permute-start | bytes 1572872 | tf_op jit(solution)/shard_map/ppermute | solution.py:87
  72.4 12.8 %collective-permute-start.5 = (bf16[256,1024]{1,0:T(8,128)(2,1)S(1)}, bf16[256,1024]{1,0:T(8,128)(2,1)S(1)}, u32[]{:S(2)}, u32[]{:S(2)}) collective-permute-start(bf16[256,1024]{1,0:T(8,128)(2,1)S(1)} %get-tuple-element.40), channel_id=1, source_target_pairs={{0,1},{1,2},{2,3},{3,0},{4,7},{5,4},{6,5},{7,6},{8,9},{9,10},{10,1... | collective-permute-start | bytes 1572872 | tf_op jit(solution)/shard_map/ppermute | solution.py:87
  74.7 10.5 %collective-permute-start.11 = (bf16[256,512]{1,0:T(8,128)(2,1)S(1)}, bf16[256,512]{1,0:T(8,128)(2,1)S(1)}, u32[]{:S(2)}, u32[]{:S(2)}) collective-permute-start(bf16[256,512]{1,0:T(8,128)(2,1)S(1)} %get-tuple-element.46), channel_id=1, source_target_pairs={{4,0},{16,4},{12,8},{24,12},{20,16},{32,20},{28,24},{40,28},{36,32... | collective-permute-start | bytes 786440 | tf_op jit(solution)/shard_map/ppermute | solution.py:79
  76.7 11.7 %collective-permute-start.10 = (bf16[256,512]{1,0:T(8,128)(2,1)S(1)}, bf16[256,512]{1,0:T(8,128)(2,1)S(1)}, u32[]{:S(2)}, u32[]{:S(2)}) collective-permute-start(bf16[256,512]{1,0:T(8,128)(2,1)S(1)} %add_convert_fusion.1), channel_id=1, source_target_pairs={{8,0},{12,4},{16,8},{20,12},{24,16},{28,20},{32,24},{36,28},{40,32... | collective-permute-start | bytes 786440 | tf_op jit(solution)/shard_map/ppermute | solution.py:79
  78.9 12.3 %collective-permute-start.23 = (bf16[128,512]{1,0:T(8,128)(2,1)S(1)}, bf16[128,512]{1,0:T(8,128)(2,1)S(1)}, u32[]{:S(2)}, u32[]{:S(2)}) collective-permute-start(bf16[128,512]{1,0:T(8,128)(2,1)S(1)} %get-tuple-element.60), channel_id=1, source_target_pairs={{0,8},{4,28},{8,16},{12,4},{16,24},{20,12},{24,0},{28,20},{32,40},... | collective-permute-start | bytes 393224 | tf_op jit(solution)/shard_map/ppermute | solution.py:79
  85.2 7.8 %collective-permute-start.24 = (bf16[128,512]{1,0:T(8,128)(2,1)S(1)}, bf16[128,512]{1,0:T(8,128)(2,1)S(1)}, u32[]{:S(2)}, u32[]{:S(2)}) collective-permute-start(bf16[128,512]{1,0:T(8,128)(2,1)S(1)} %get-tuple-element.61), channel_id=1, source_target_pairs={{0,24},{4,12},{8,0},{12,20},{16,8},{20,28},{24,16},{28,4},{32,56},... | collective-permute-start | bytes 393224 | tf_op jit(solution)/shard_map/ppermute | solution.py:79
  85.2 7.8 %collective-permute-start.25 = (bf16[128,512]{1,0:T(8,128)(2,1)S(1)}, bf16[128,512]{1,0:T(8,128)(2,1)S(1)}, u32[]{:S(2)}, u32[]{:S(2)}) collective-permute-start(bf16[128,512]{1,0:T(8,128)(2,1)S(1)} %get-tuple-element.62), channel_id=1, source_target_pairs={{0,16},{4,20},{8,24},{12,28},{16,0},{20,4},{24,8},{28,12},{32,48},... | collective-permute-start | bytes 393224 | tf_op jit(solution)/shard_map/ppermute | solution.py:79
  85.2 7.8 %collective-permute-start.26 = (bf16[128,512]{1,0:T(8,128)(2,1)S(1)}, bf16[128,512]{1,0:T(8,128)(2,1)S(1)}, u32[]{:S(2)}, u32[]{:S(2)}) collective-permute-start(bf16[128,512]{1,0:T(8,128)(2,1)S(1)} %get-tuple-element.64), channel_id=1, source_target_pairs={{0,32},{4,100},{8,40},{12,108},{16,48},{20,116},{24,56},{28,124},{... | collective-permute-start | bytes 393224 | tf_op jit(solution)/shard_map/ppermute | solution.py:79
  88.4 6.6 %collective-permute-start.27 = (bf16[128,512]{1,0:T(8,128)(2,1)S(1)}, bf16[128,512]{1,0:T(8,128)(2,1)S(1)}, u32[]{:S(2)}, u32[]{:S(2)}) collective-permute-start(bf16[128,512]{1,0:T(8,128)(2,1)S(1)} %get-tuple-element.65), channel_id=1, source_target_pairs={{0,96},{4,36},{8,104},{12,44},{16,112},{20,52},{24,120},{28,60},{3... | collective-permute-start | bytes 393224 | tf_op jit(solution)/shard_map/ppermute | solution.py:79
  91.2 5.3 %collective-permute-start.28 = (bf16[128,512]{1,0:T(8,128)(2,1)S(1)}, bf16[128,512]{1,0:T(8,128)(2,1)S(1)}, u32[]{:S(2)}, u32[]{:S(2)}) collective-permute-start(bf16[128,512]{1,0:T(8,128)(2,1)S(1)} %get-tuple-element.66), channel_id=1, source_target_pairs={{0,64},{4,68},{8,72},{12,76},{16,80},{20,84},{24,88},{28,92},{32,9... | collective-permute-start | bytes 393224 | tf_op jit(solution)/shard_map/ppermute | solution.py:79
  (12 other events, 62.1 us)

commit v3 on v2

v3 whole, which is shorter than its diff:
```python
import math

import jax
import jax.numpy as jnp
from jax import lax
from jax.experimental import pallas as pl
from jax.experimental.pallas import tpu as pltpu
from jax.sharding import PartitionSpec as P

BF = jnp.bfloat16
F32 = jnp.float32
HD = 128
TOK = 256
SIDE = 4
SCALE = HD**-0.5
EXP2_SCALE = SCALE * math.log2(math.e)
MASKED = -1e30
HBM_BYTES_PER_US = 50_000
VM = pltpu.VMEM
SM = pltpu.SMEM


def dot_nn(a, b):
    return lax.dot_general(a, b, (((1,), (0,)), ((), ())), preferred_element_type=F32)


def dot_nt(a, b):
    return lax.dot_general(a, b, (((1,), (1,)), ((), ())), preferred_element_type=F32)


def seq_route(step):
    pairs = []
    for x in range(SIDE):
        for y in range(SIDE):
            for core in range(2):
                to = step(x, y, core)
                if to is not None:
                    pairs.append(((x * SIDE + y) * 2 + core, (to[0] * SIDE + to[1]) * 2 + to[2]))
    return pairs


def chips_on(x, y, chips, core):
    chip = (x * SIDE + y + chips) % (SIDE * SIDE)
    return (chip // SIDE, chip % SIDE, core)


SWAP = seq_route(lambda x, y, c: (x, y, 1 - c))
NEXT_CHIP = seq_route(lambda x, y, c: chips_on(x, y, 1, c))
MIXED = seq_route(lambda x, y, c: (x, y, 1) if c == 0 else chips_on(x, y, 2, 0))


def back(route):
    return [(b, a) for a, b in route]


def by_core(axis_of_core, step):
    def to(x, y, c):
        if axis_of_core[c] == "x":
            return ((x + step) % SIDE, y, c)
        return (x, (y + step) % SIDE, c)

    return seq_route(to)


def same(core):
    return 1 - 2 * core


def opposite(core):
    return 2 * core - 1


def seq_send(v, route):
    return lax.ppermute(v, "seq", route)


def kv_send(v, step):
    pairs = []
    for seq in range(2 * SIDE * SIDE):
        for z in range(SIDE):
            pairs.append((seq * SIDE + z, seq * SIDE + (z + step(seq % 2)) % SIDE))
    return lax.ppermute(v, ("seq", "kv"), pairs)


def call(
    kernel, out_shape, n_in, us, scratch=(), smem_in=0, hbm_in=0, after=0, vmem_mib=24
):
    def body(*refs):
        n = smem_in + hbm_in + n_in
        kernel(*refs[:n], *refs[n + after :])

    vmem = pl.BlockSpec(memory_space=VM)
    return pl.pallas_call(
        body,
        out_shape=out_shape,
        in_specs=[pl.BlockSpec(memory_space=SM)] * smem_in
        + [pl.BlockSpec(memory_space=pltpu.HBM)] * hbm_in
        + [vmem] * n_in
        + [pl.BlockSpec(memory_space=pl.ANY)] * after,
        out_specs=jax.tree.map(lambda _: vmem, out_shape),
        scratch_shapes=list(scratch),
        compiler_params=pltpu.CompilerParams(vmem_limit_bytes=vmem_mib * 2**20),
        cost_estimate=pl.CostEstimate(
            flops=0, transcendentals=0, bytes_accessed=int(us * HBM_BYTES_PER_US)
        ),
    )


def doc_starts(lengths, pos):
    def step(n, carry):
        end, start = carry
        end = end + lengths[n]
        return end, jnp.where(pos >= end, end, start)

    return lax.fori_loop(0, 64, step, (jnp.int32(0), jnp.zeros_like(pos)))[1]


def prepare_kernel(info, lengths, q, q_heads, bias):
    core = info[0] % 2
    first = info[0] * TOK
    pos = first + lax.broadcasted_iota(jnp.int32, (1, TOK), 1)
    start = doc_starts(lengths, pos)
    for b, at in enumerate((0, -2, 2 * core - 3, -1 - 2 * core)):
        key_pos = first + at * TOK + lax.broadcasted_iota(jnp.int32, (TOK, 1), 0)
        ok = (key_pos >= start) & (key_pos <= pos)
        bias[b] = jnp.where(ok, 0.0, MASKED).astype(F32)
    for g in range(2):
        q_heads[g] = heads(q, g)


def heads(ref, g):
    return jnp.concatenate([ref[:, pl.ds((4 * g + h) * HD, HD)] for h in range(4)], axis=0)


def fwd_kernel(q, bias, own, two, mixed, swapped, att, lse, scores):
    refs = (own, two, mixed, swapped)
    for g in range(2):
        qg = q[g]
        top = jnp.full((1, 4 * TOK), MASKED, F32)
        for b, ref in enumerate(refs):
            s = dot_nt(ref[:, pl.ds(g * HD, HD)], qg) * EXP2_SCALE
            s = s + jnp.concatenate([bias[b]] * 4, axis=1)
            scores[b] = s
            top = jnp.maximum(top, jnp.max(s, axis=0, keepdims=True))
        total = jnp.zeros((1, 4 * TOK), F32)
        o = jnp.zeros((HD, 4 * TOK), F32)
        for b, ref in enumerate(refs):
            e = jnp.exp2(scores[b] - top)
            total = total + jnp.sum(e, axis=0, keepdims=True)
            o = o + dot_nn(ref[:, pl.ds((2 + g) * HD, HD)].T, e.astype(BF))
        lse[g : g + 1, :] = top + jnp.log2(total)
        o = (o / total).T
        for h in range(4):
            att[:, pl.ds((4 * g + h) * HD, HD)] = o[h * TOK : (h + 1) * TOK].astype(BF)


def bwd_kernel(
    q, bias, own, two, mixed, swapped, lse, att, attn_grad, dq, d_own, d_two, d_mixed, d_swapped
):
    refs = (own, two, mixed, swapped)
    outs = (d_own, d_two, d_mixed, d_swapped)
    for g in range(2):
        qg = q[g]
        og = heads(attn_grad, g)
        ag = heads(att, g)
        dots = jnp.sum((og.astype(F32) * ag.astype(F32)).T, axis=0, keepdims=True)
        row_lse = lse[g : g + 1, :]
        dqt = jnp.zeros((HD, 4 * TOK), F32)
        for b, (ref, out) in enumerate(zip(refs, outs)):
            kb = ref[:, pl.ds(g * HD, HD)]
            vb = ref[:, pl.ds((2 + g) * HD, HD)]
            s = dot_nt(kb, qg) * EXP2_SCALE + jnp.concatenate([bias[b]] * 4, axis=1)
            p = jnp.exp2(s - row_lse)
            out[:, pl.ds((2 + g) * HD, HD)] = dot_nn(p.astype(BF), og).astype(out.dtype)
            ds = (p * (dot_nt(vb, og) - dots) * SCALE).astype(BF)
            out[:, pl.ds(g * HD, HD)] = dot_nn(ds, qg).astype(out.dtype)
            dqt = dqt + dot_nn(kb.T, ds)
        dqs = dqt.T
        for h in range(4):
            dq[:, pl.ds((4 * g + h) * HD, HD)] = dqs[h * TOK : (h + 1) * TOK].astype(BF)


def finish_kernel(own, from_mixed, from_two, dk, dv):
    total = own[...] + from_mixed[...].astype(F32) + from_two[...].astype(F32)
    dk[...] = total[:, : 2 * HD].astype(BF)
    dv[...] = total[:, 2 * HD :].astype(BF)


def layer_sum_kernel(own, from_opp, from_same, out):
    total = own[...] + from_opp[...].astype(F32) + from_same[...].astype(F32)
    out[...] = total.astype(BF)


def stream(info, w, w_here, sems, order):
    rows = w_here.shape[1]
    copies = []
    for i, at in enumerate(order):
        source = w.at[pl.ds(pl.multiple_of((at % SIDE) * rows, rows), rows), :]
        copies.append(pltpu.make_async_copy(source, w_here.at[i], sems.at[i]))
        copies[-1].start()
    for i, copy in enumerate(copies):
        copy.wait()
        yield i, w_here[i]


def out_kernel(info, w, att, across, opp, same_term, own, w_here, sems):
    z, way = info[1], 1 - 2 * (info[0] % 2)
    outs = (across, opp, same_term, own)
    order = (z + 2, z + SIDE - way, z + SIDE + way, z)
    for i, rows in stream(info, w, w_here, sems, order):
        outs[i][...] = dot_nt(att[...], rows).astype(outs[i].dtype)


def add_kernel(a, b, out):
    out[...] = (a[...] + b[...].astype(F32)).astype(BF)


def attn_grad_kernel(info, w, g, first, second, third, out, w_here, sems):
    z, way = info[1], 1 - 2 * (info[0] % 2)
    parts = (g, first, second, third)
    order = (z, z + SIDE - way, z + SIDE + way, z + 2)
    total = None
    for i, rows in stream(info, w, w_here, sems, order):
        term = dot_nn(parts[i][...], rows)
        total = term if total is None else total + term
    out[...] = total.astype(BF)


def place(info):
    seq = info[0]
    core = seq % 2
    x, y = seq // (2 * SIDE), (seq // 2) % SIDE
    return core, jnp.where(core == 0, x, y), jnp.where(core == 0, y, x)


def weight_kernel(info, *refs):
    here, there, att, att_there, across, plus, minus, own, g, a = refs[:4], refs[4:8], *refs[8:]
    core, at, _ = place(info)
    z, way = info[1], 1 - 2 * core
    half = a.shape[1]
    columns = pl.ds(pl.multiple_of(core * half, half), half)
    a[:TOK] = att[:, columns]
    a[TOK:] = att_there[:, columns]
    for t, sources, w in ((0, here, way), (1, there, -way)):
        for source, chunk_at in zip(sources, (z, z + SIDE - w, z + SIDE + w, z + 2)):
            g[chunk_at % SIDE, t * TOK : (t + 1) * TOK, :] = source[...]
    outs = ((across, 2), (plus, 1), (minus, SIDE - 1), (own, 0))

    @pl.when(core == 0)
    def _():
        for out, step in outs:
            out[...] = dot_nn(g[(at + step) % SIDE].T, a[...]).astype(out.dtype)

    @pl.when(core == 1)
    def _():
        for out, step in outs:
            strip = pl.ds(pl.multiple_of(((at + step) % SIDE) * TOK, TOK), TOK)
            for x in range(SIDE):
                terms = dot_nn(g[x, :, strip].T, a[...])
                out[x * TOK : (x + 1) * TOK, :] = terms.astype(out.dtype)


def weight_sum_kernel(info, own, from_minus, from_plus, from_across, plus, minus, across, mine):
    core, _, at = place(info)
    for out, step in ((plus, 1), (minus, SIDE - 1), (across, 2), (mine, 0)):
        rows = pl.ds(pl.multiple_of(((at + step) % SIDE) * TOK, TOK), TOK)
        total = own[rows, :] + from_minus[rows, :].astype(F32) + from_plus[rows, :].astype(F32)
        out[...] = (total + from_across[rows, :].astype(F32)).astype(out.dtype)


def weight_halves_kernel(info, mine, a, b, c, keep, give):
    core = info[0] % 2
    for out, rows_of in ((keep, core), (give, 1 - core)):
        rows = pl.ds(pl.multiple_of(rows_of * HD, HD), HD)
        total = mine[rows, :] + a[rows, :].astype(F32) + b[rows, :].astype(F32)
        out[...] = (total + c[rows, :].astype(F32)).astype(BF)


def weight_join_kernel(info, kept, given, out):
    half = kept.shape[1]
    core = info[0] % 2
    out[:, pl.ds(pl.multiple_of(core * half, half), half)] = kept[...]
    out[:, pl.ds(pl.multiple_of((1 - core) * half, half), half)] = given[...]


def per_device(queries, keys, values, out_weight, out_grad, doc_lengths):
    shape = jax.ShapeDtypeStruct
    info = jnp.stack([lax.axis_index("seq"), lax.axis_index("kv")]).astype(jnp.int32)
    cols = queries.shape[1]
    half = cols // 2
    block = shape((TOK, cols), BF)

    first = kv_send(out_grad, same)
    second = kv_send(out_grad, opposite)

    own = jnp.pad(keys, ((0, 0), (0, 2 * HD))) + jnp.pad(values, ((0, 0), (2 * HD, 0)))
    two = seq_send(own, NEXT_CHIP)
    mixed = seq_send(own, MIXED)
    q, bias = call(
        prepare_kernel,
        [shape((2, 4 * TOK, HD), BF), shape((4, TOK, TOK), F32)],
        1,
        us=4,
        smem_in=2,
    )(info, doc_lengths, queries)
    q, bias, mixed, two, first, second = lax.optimization_barrier(
        (q, bias, mixed, two, first, second)
    )
    swapped = seq_send(two, SWAP)
    third = kv_send(first, same)
    here = (out_grad, first, second, third)
    there = tuple(seq_send(v, SWAP) for v in here)
    blocks = (own, two, mixed, swapped)

    att, lse = call(
        fwd_kernel,
        [block, shape((2, 4 * TOK), F32)],
        6,
        us=4,
        scratch=[VM((4, TOK, 4 * TOK), F32)],
    )(q, bias, *blocks)
    att_there = seq_send(att, SWAP)

    chunks = [VM((SIDE, cols, cols), BF), pltpu.SemaphoreType.DMA((SIDE,))]
    block32 = shape((TOK, cols), F32)
    out_across, out_opp, out_same, out_own = call(
        out_kernel,
        [block] * 2 + [block32] * 2,
        1,
        us=4,
        smem_in=1,
        hbm_in=1,
        after=3,
        scratch=chunks,
        vmem_mib=48,
    )(info, out_weight, att, *there[:3])
    pieces = shape((4 * TOK, half), BF)
    across, plus, minus, weight_own = call(
        weight_kernel,
        [pieces] * 3 + [shape((4 * TOK, half), F32)],
        10,
        us=4,
        smem_in=1,
        after=1,
        scratch=[VM((SIDE, 2 * TOK, 4 * TOK), BF), VM((2 * TOK, half), BF)],
    )(info, *here, *there, att, att_there, out_across)
    stage = ("x", "y")
    from_across = seq_send(across, by_core(stage, 2))
    from_minus = seq_send(plus, by_core(stage, 1))
    from_plus = seq_send(minus, by_core(stage, -1))

    attn_grad = call(
        attn_grad_kernel, block, 4, us=4, smem_in=1, hbm_in=1, after=1, scratch=chunks, vmem_mib=48
    )(info, out_weight, *here, plus)
    out_relayed = kv_send(out_across, same)
    out_from_opp = kv_send(out_opp, opposite)

    out_same = call(add_kernel, block, 2, us=1, after=1)(out_same, out_relayed, attn_grad)
    out_from_same = kv_send(out_same, same)
    part = shape((TOK, 4 * HD), F32)
    part16 = shape((TOK, 4 * HD), BF)
    query_grad, d_own, d_two, d_mixed, d_swapped = call(
        bwd_kernel, [block, part, part, part16, part16], 9, us=6.5, after=1
    )(q, bias, *blocks, lse, att, attn_grad, out_same)
    layer_out = call(layer_sum_kernel, block, 3, us=1, after=1)(
        out_own, out_from_opp, out_from_same, d_own
    )
    from_swapped = seq_send(d_swapped, SWAP)
    from_mixed = seq_send(d_mixed, back(MIXED))
    d_two = call(add_kernel, part16, 2, us=1, after=1)(d_two, from_swapped, layer_out)
    from_two = seq_send(d_two, back(NEXT_CHIP))

    strip = shape((TOK, half), BF)
    plus, minus, across, mine = call(
        weight_sum_kernel,
        [strip] * 3 + [shape((TOK, half), F32)],
        4,
        us=1,
        smem_in=1,
        after=1,
    )(info, weight_own, from_minus, from_plus, from_across, d_two)
    stage = ("y", "x")
    last = [
        seq_send(across, by_core(stage, 2)),
        seq_send(plus, by_core(stage, 1)),
        seq_send(minus, by_core(stage, -1)),
    ]
    kept, given = call(weight_halves_kernel, [shape((HD, half), BF)] * 2, 4, us=1, smem_in=1)(
        info, mine, *last
    )
    key_grad, value_grad = call(finish_kernel, [shape((TOK, 2 * HD), BF)] * 2, 3, us=1, after=1)(
        d_own, from_mixed, from_two, given
    )
    weight_grad = call(weight_join_kernel, shape((HD, cols), BF), 2, us=1, smem_in=1, after=1)(
        info, kept, seq_send(given, SWAP), key_grad
    )
    return (layer_out, query_grad, key_grad, value_grad, weight_grad)


def solution(mesh):
    placed = (P("seq", "kv"), P("seq", "kv"), P("seq", "kv"), P(None, "kv"), P("seq", "kv"), P())
    return jax.shard_map(
        per_device,
        mesh=mesh,
        in_specs=placed,
        out_specs=(P("seq", "kv"),) * 5,
        check_vma=False,
    )
```

time: 97.7 us -> 92.2 us (0.944)
  the two profiles are of different devices: /device:TPU:1 before, /device:TPU:95 now
where the time goes in v3:
time: 92.2 us; the launch traced here: 92 us
  starting transfers between devices  42.5 us (46%)
  Pallas kernels  31.1 us (34%)
  waiting for transfers between devices  12.8 us (14%)
  local copies, waits for them, and re-layouts  3.65 us (4%)
  other arithmetic  1.06 us (1%)
    ppermute x18, starting transfers between devices, seq_send(): return lax.ppermute(v, 'seq', route)  37.6 us
    ppermute x18, waiting for transfers between devices, seq_send(): return lax.ppermute(v, 'seq', route)  12 us
    pallas_call x1, Pallas kernels, per_device(): call(bwd_kernel, [block, part, part, part16, part16], 9, us=6.5, after=1)  6.23 us
    pallas_call x1, Pallas kernels, per_device(): call(attn_grad_kernel, block, 4, us=4, smem_in=1, hbm_in=1, after=1, scra...  5.25 us
    pallas_call x1, Pallas kernels, per_device(): call(out_kernel, [block] * 2 + [block32] * 2, 1, us=4, smem_in=1, hbm_in=...  5.23 us
    ppermute x6, starting transfers between devices, kv_send(): return lax.ppermute(v, ('seq', 'kv'), pairs)  4.93 us
    pallas_call x1, Pallas kernels, per_device(): call(weight_kernel, [pieces] * 3 + [shape((4 * TOK, half), F32)], 10, us=...  4.82 us
    unnamed x10, local copies, waits for them, and re-layouts  3.65 us
  transfers between devices with their start and end apart: 24, of which 7 were waited for; matrix products, arithmetic and copies ran while one was open for 1% of the time, Pallas kernels for 31%

profile of v3, /device:TPU:95, one launch (start us, length us, event | category | flops | bytes accessed | tf_op | source)
XLA Modules:
  0.0 92.0 jit_solution(13965553169056113318)
XLA Ops:
  0.7 1.5 %collective-permute-start.3 = (bf16[256,1024]{1,0:T(8,128)(2,1)}, bf16[256,1024]{1,0:T(8,128)(2,1)S(1)}, u32[]{:S(2)}, u32[]{:S(2)}) collective-permute-start(bf16[256,1024]{1,0:T(8,128)(2,1)} %refs_2_.3), channel_id=1, source_target_pairs={{0,3},{1,0},{2,1},{3,2},{4,5},{5,6},{6,7},{7,4},{8,11},{9,8},{10,9... | collective-permute-start | bytes 1572872 | tf_op jit(solution)/shard_map/ppermute | solution.py:82
  3.2 2.1 %collective-permute-start = (bf16[256,512]{1,0:T(8,128)(2,1)S(1)}, bf16[256,512]{1,0:T(8,128)(2,1)S(1)}, u32[]{:S(2)}, u32[]{:S(2)}) collective-permute-start(bf16[256,512]{1,0:T(8,128)(2,1)S(1)} %pad_add_fusion.refs_2_), channel_id=1, source_target_pairs={{0,4},{4,16},{8,12},{12,24},{16,20},{20,32},{24,28},{28,40},{32,36... | collective-permute-start | bytes 786440 | tf_op jit(solution)/shard_map/ppermute | solution.py:74
  5.2 1.9 %collective-permute-start.1 = (bf16[256,512]{1,0:T(8,128)(2,1)S(1)}, bf16[256,512]{1,0:T(8,128)(2,1)S(1)}, u32[]{:S(2)}, u32[]{:S(2)}) collective-permute-start(bf16[256,512]{1,0:T(8,128)(2,1)S(1)} %pad_add_fusion.refs_2_), channel_id=1, source_target_pairs={{0,8},{4,12},{8,16},{12,20},{16,24},{20,28},{24,32},{28,36},{32,40... | collective-permute-start | bytes 786440 | tf_op jit(solution)/shard_map/ppermute | solution.py:74
  8.9 1.2 %shard_map.101 = (bf16[2,1024,128]{2,1,0:T(8,128)(2,1)S(1)}, f32[4,256,256]{2,1,0:T(8,128)S(1)}) custom-call(s32[2]{0:T(128)S(1)} %pad_add_fusion.1.refs_0_, s32[64]{0:T(128)S(1)} %copy-done.4, bf16[256,1024]{1,0:T(8,128)(2,1)S(1)} %copy-done.2), custom_call_target="tpu_custom_call" | custom-call | bytes 200000 | tf_op jit(solution)/shard_map/pallas_call | solution.py:299
  11.0 4.4 %collective-permute-done.1.refs_3_ = bf16[256,512]{1,0:T(8,128)(2,1)S(1)} collective-permute-done((bf16[256,512]{1,0:T(8,128)(2,1)S(1)}, bf16[256,512]{1,0:T(8,128)(2,1)S(1)}, u32[]{:S(2)}, u32[]{:S(2)}) %collective-permute-start.1) | collective-permute-done | bytes 262176 | tf_op jit(solution)/shard_map/ppermute | solution.py:74
  15.5 2.6 %collective-permute-start.4 = (bf16[256,512]{1,0:T(8,128)(2,1)S(1)}, bf16[256,512]{1,0:T(8,128)(2,1)S(1)}, u32[]{:S(2)}, u32[]{:S(2)}) collective-permute-start(bf16[256,512]{1,0:T(8,128)(2,1)S(1)} %collective-permute-done.1.refs_3_), channel_id=1, source_target_pairs={{0,4},{4,0},{8,12},{12,8},{16,20},{20,16},{24,28},{28,24},{32,36},... | collective-permute-start | bytes 786440 | tf_op jit(solution)/shard_map/ppermute | solution.py:74
  19.6 3.6 %shard_map.102 = (bf16[256,1024]{1,0:T(8,128)(2,1)S(1)}, f32[2,1024]{1,0:T(2,128)S(1)}) custom-call(bf16[2,1024,128]{2,1,0:T(8,128)(2,1)S(1)} %get-tuple-element.38.refs_0_, f32[4,256,256]{2,1,0:T(8,128)S(1)} %get-tuple-element.39.refs_1_, bf16[256,512]{1,0:T(8,128)(2,1)S(1)} %pad_add_fusion.refs_2_, bf16[256,512]{1,0:T(8,128)(2,1)S(1)} %collective-permute-done.1.refs_3_, ...), custom_call_target="tpu_custom_call" | custom-call | bytes 200000 | tf_op jit(solution)/shard_map/pallas_call | solution.py:315
  23.8 1.2 %collective-permute-start.11 = (bf16[256,1024]{1,0:T(8,128)(2,1)S(1)}, bf16[256,1024]{1,0:T(8,128)(2,1)S(1)}, u32[]{:S(2)}, u32[]{:S(2)}) collective-permute-start(bf16[256,1024]{1,0:T(8,128)(2,1)S(1)} %collective-permute-done.10.refs_4_.refs_5_), channel_id=1, source_target_pairs={{0,4},{4,0},{8,12},{12,8},{16,20},{20,16},{24,28},{28,24},{32,36},... | collective-permute-start | bytes 1572872 | tf_op jit(solution)/shard_map/ppermute | solution.py:74
  25.0 5.2 %shard_map.103 = (bf16[256,1024]{1,0:T(8,128)(2,1)S(1)}, bf16[256,1024]{1,0:T(8,128)(2,1)S(1)}, f32[256,1024]{1,0:T(8,128)S(1)}, f32[256,1024]{1,0:T(8,128)S(1)}) custom-call(s32[2]{0:T(128)S(1)} %pad_add_fusion.1.refs_0_, bf16[4096,1024]{1,0:T(8,128)(2,1)} %refs_1_.7, bf16[256,1024]{1,0:T(8,128)(2,1)S(1)} %get-tuple-element.42.refs_2_.refs_9_.refs_7_, ...), custom_call_target="tpu_custom_call" | custom-call | bytes 200000 | tf_op jit(solution)/shard_map/pallas_call | solution.py:326
  30.4 4.8 %shard_map.104 = (bf16[1024,512]{1,0:T(8,128)(2,1)}, bf16[1024,512]{1,0:T(8,128)(2,1)S(1)}, bf16[1024,512]{1,0:T(8,128)(2,1)}, f32[1024,512]{1,0:T(8,128)S(1)}) custom-call(s32[2]{0:T(128)S(1)} %pad_add_fusion.1.refs_0_, bf16[256,1024]{1,0:T(8,128)(2,1)S(1)} %copy-done, bf16[256,1024]{1,0:T(8,128)(2,1)S(1)} %collective-permute-done.2.refs_2_.refs_3_, ...), custom_call_target="tpu_custom_call" | custom-call | bytes 200000 | tf_op jit(solution)/shard_map/pallas_call | solution.py:338
  35.2 1.2 %collective-permute-start.17 = (bf16[1024,512]{1,0:T(8,128)(2,1)S(1)}, bf16[1024,512]{1,0:T(8,128)(2,1)S(1)}, u32[]{:S(2)}, u32[]{:S(2)}) collective-permute-start(bf16[1024,512]{1,0:T(8,128)(2,1)S(1)} %get-tuple-element.49.refs_6_), channel_id=1, source_target_pairs={{0,32},{4,12},{8,40},{12,20},{16,48},{20,28},{24,56},{28,4},{32,64... | collective-permute-start | bytes 3145736 | tf_op jit(solution)/shard_map/ppermute | solution.py:74
  36.7 1.4 %collective-permute-start.19 = (bf16[1024,512]{1,0:T(8,128)(2,1)}, bf16[1024,512]{1,0:T(8,128)(2,1)S(1)}, u32[]{:S(2)}, u32[]{:S(2)}) collective-permute-start(bf16[1024,512]{1,0:T(8,128)(2,1)} %get-tuple-element.58), channel_id=1, source_target_pairs={{0,64},{4,20},{8,72},{12,28},{16,80},{20,4},{24,88},{28,12},{32,96... | collective-permute-start | bytes 3145736 | tf_op jit(solution)/shard_map/ppermute | solution.py:74
  38.1 2.1 %collective-permute-start.8 = (bf16[256,1024]{1,0:T(8,128)(2,1)S(1)}, bf16[256,1024]{1,0:T(8,128)(2,1)S(1)}, u32[]{:S(2)}, u32[]{:S(2)}) collective-permute-start(bf16[256,1024]{1,0:T(8,128)(2,1)S(1)} %get-tuple-element.46), channel_id=1, source_target_pairs={{0,3},{1,0},{2,1},{3,2},{4,5},{5,6},{6,7},{7,4},{8,11},{9,8},{10,9... | collective-permute-start | bytes 1572872 | tf_op jit(solution)/shard_map/ppermute | solution.py:82
  40.2 5.2 %shard_map.105.refs_2_.refs_8_ = bf16[256,1024]{1,0:T(8,128)(2,1)S(1)} custom-call(s32[2]{0:T(128)S(1)} %pad_add_fusion.1.refs_0_, bf16[4096,1024]{1,0:T(8,128)(2,1)} %refs_1_.7, bf16[256,1024]{1,0:T(8,128)(2,1)S(1)} %copy-done, bf16[256,1024]{1,0:T(8,128)(2,1)S(1)} %collective-permute-done.2.refs_2_.refs_3_, ...), custom_call_target="tpu_custom_call" | custom-call | bytes 200000 | tf_op jit(solution)/shard_map/pallas_call | solution.py:352
  45.6 1.1 %collective-permute-start.13 = (bf16[256,1024]{1,0:T(8,128)(2,1)S(1)}, bf16[256,1024]{1,0:T(8,128)(2,1)S(1)}, u32[]{:S(2)}, u32[]{:S(2)}) collective-permute-start(bf16[256,1024]{1,0:T(8,128)(2,1)S(1)} %shard_map.106.refs_9_), channel_id=1, source_target_pairs={{0,1},{1,2},{2,3},{3,0},{4,7},{5,4},{6,5},{7,6},{8,9},{9,10},{10,1... | collective-permute-start | bytes 1572872 | tf_op jit(solution)/shard_map/ppermute | solution.py:82
  46.7 6.2 %shard_map.107 = (bf16[256,1024]{1,0:T(8,128)(2,1)}, f32[256,512]{1,0:T(8,128)S(1)}, f32[256,512]{1,0:T(8,128)S(1)}, bf16[256,512]{1,0:T(8,128)(2,1)S(1)}, bf16[256,512]{1,0:T(8,128)(2,1)S(1)}) custom-call(bf16[2,1024,128]{2,1,0:T(8,128)(2,1)S(1)} %get-tuple-element.38.refs_0_, f32[4,256,256]{2,1,0:T(8,128)S(1)} %get-tuple-element.39.refs_1_, ...), custom_call_target="tpu_custom_call" | custom-call | bytes 325000 | tf_op jit(solution)/shard_map/pallas_call | solution.py:362
  52.9 1.8 %collective-permute-start.15 = (bf16[256,512]{1,0:T(8,128)(2,1)S(1)}, bf16[256,512]{1,0:T(8,128)(2,1)S(1)}, u32[]{:S(2)}, u32[]{:S(2)}) collective-permute-start(bf16[256,512]{1,0:T(8,128)(2,1)S(1)} %get-tuple-element.55), channel_id=1, source_target_pairs={{0,4},{4,0},{8,12},{12,8},{16,20},{20,16},{24,28},{28,24},{32,36},... | collective-permute-start | bytes 786440 | tf_op jit(solution)/shard_map/ppermute | solution.py:74
  57.5 5.5 %collective-permute-done.18.refs_3_ = bf16[1024,512]{1,0:T(8,128)(2,1)S(1)} collective-permute-done((bf16[1024,512]{1,0:T(8,128)(2,1)}, bf16[1024,512]{1,0:T(8,128)(2,1)S(1)}, u32[]{:S(2)}, u32[]{:S(2)}) %collective-permute-start.18) | collective-permute-done | bytes 1048608 | tf_op jit(solution)/shard_map/ppermute | solution.py:74
  64.0 1.0 %collective-permute-start.20 = (bf16[256,512]{1,0:T(8,128)(2,1)S(1)}, bf16[256,512]{1,0:T(8,128)(2,1)S(1)}, u32[]{:S(2)}, u32[]{:S(2)}) collective-permute-start(bf16[256,512]{1,0:T(8,128)(2,1)S(1)} %get-tuple-element.60), channel_id=1, source_target_pairs={{0,16},{4,68},{8,24},{12,76},{16,0},{20,84},{24,8},{28,92},{32,48}... | collective-permute-start | bytes 786440 | tf_op jit(solution)/shard_map/ppermute | solution.py:74
  65.0 1.8 %collective-permute-start.21 = (bf16[256,512]{1,0:T(8,128)(2,1)S(1)}, bf16[256,512]{1,0:T(8,128)(2,1)S(1)}, u32[]{:S(2)}, u32[]{:S(2)}) collective-permute-start(bf16[256,512]{1,0:T(8,128)(2,1)S(1)} %get-tuple-element.61), channel_id=1, source_target_pairs={{0,8},{4,36},{8,16},{12,44},{16,24},{20,52},{24,0},{28,60},{32,40}... | collective-permute-start | bytes 786440 | tf_op jit(solution)/shard_map/ppermute | solution.py:74
  66.8 7.4 %collective-permute-start.14 = (bf16[256,512]{1,0:T(8,128)(2,1)S(1)}, bf16[256,512]{1,0:T(8,128)(2,1)S(1)}, u32[]{:S(2)}, u32[]{:S(2)}) collective-permute-start(bf16[256,512]{1,0:T(8,128)(2,1)S(1)} %get-tuple-element.53), channel_id=1, source_target_pairs={{4,0},{16,4},{12,8},{24,12},{20,16},{32,20},{28,24},{40,28},{36,32... | collective-permute-start | bytes 786440 | tf_op jit(solution)/shard_map/ppermute | solution.py:74
  74.2 1.7 %collective-permute-start.16 = (bf16[256,512]{1,0:T(8,128)(2,1)S(1)}, bf16[256,512]{1,0:T(8,128)(2,1)S(1)}, u32[]{:S(2)}, u32[]{:S(2)}) collective-permute-start(bf16[256,512]{1,0:T(8,128)(2,1)S(1)} %shard_map.109.refs_5_), channel_id=1, source_target_pairs={{8,0},{12,4},{16,8},{20,12},{24,16},{28,20},{32,24},{36,28},{40,32... | collective-permute-start | bytes 786440 | tf_op jit(solution)/shard_map/ppermute | solution.py:74
  76.6 12.1 %collective-permute-start.23 = (bf16[128,512]{1,0:T(8,128)(2,1)S(1)}, bf16[128,512]{1,0:T(8,128)(2,1)S(1)}, u32[]{:S(2)}, u32[]{:S(2)}) collective-permute-start(bf16[128,512]{1,0:T(8,128)(2,1)S(1)} %get-tuple-element.63.refs_3_), channel_id=1, source_target_pairs={{0,4},{4,0},{8,12},{12,8},{16,20},{20,16},{24,28},{28,24},{32,36},... | collective-permute-start | bytes 393224 | tf_op jit(solution)/shard_map/ppermute | solution.py:74
  90.7 1.3 %shard_map.113 = bf16[128,1024]{1,0:T(8,128)(2,1)} custom-call(s32[2]{0:T(128)S(1)} %pad_add_fusion.1.refs_0_, bf16[128,512]{1,0:T(8,128)(2,1)S(1)} %get-tuple-element.66.refs_1_, bf16[128,512]{1,0:T(8,128)(2,1)S(1)} %collective-permute-done.23.refs_2_, bf16[256,256]{1,0:T(8,128)(2,1)S(1)} %copy-done.3), custom_call_target="tpu_custom_call" | custom-call | bytes 50000 | tf_op jit(solution)/shard_map/pallas_call | solution.py:394
  (49 shorter events, 12.7 us)
Async XLA Ops:
  0.6 14.8 %collective-permute-start.2 = (bf16[256,1024]{1,0:T(8,128)(2,1)}, bf16[256,1024]{1,0:T(8,128)(2,1)S(1)}, u32[]{:S(2)}, u32[]{:S(2)}) collective-permute-start(bf16[256,1024]{1,0:T(8,128)(2,1)} %refs_2_.3), channel_id=1, source_target_pairs={{0,1},{1,2},{2,3},{3,0},{4,7},{5,4},{6,5},{7,6},{8,9},{9,10},{10,1... | collective-permute-start | bytes 1572872 | tf_op jit(solution)/shard_map/ppermute | solution.py:82
  0.7 14.7 %collective-permute-start.3 = (bf16[256,1024]{1,0:T(8,128)(2,1)}, bf16[256,1024]{1,0:T(8,128)(2,1)S(1)}, u32[]{:S(2)}, u32[]{:S(2)}) collective-permute-start(bf16[256,1024]{1,0:T(8,128)(2,1)} %refs_2_.3), channel_id=1, source_target_pairs={{0,3},{1,0},{2,1},{3,2},{4,5},{5,6},{6,7},{7,4},{8,11},{9,8},{10,9... | collective-permute-start | bytes 1572872 | tf_op jit(solution)/shard_map/ppermute | solution.py:82
  3.2 7.8 %collective-permute-start = (bf16[256,512]{1,0:T(8,128)(2,1)S(1)}, bf16[256,512]{1,0:T(8,128)(2,1)S(1)}, u32[]{:S(2)}, u32[]{:S(2)}) collective-permute-start(bf16[256,512]{1,0:T(8,128)(2,1)S(1)} %pad_add_fusion.refs_2_), channel_id=1, source_target_pairs={{0,4},{4,16},{8,12},{12,24},{16,20},{20,32},{24,28},{28,40},{32,36... | collective-permute-start | bytes 786440 | tf_op jit(solution)/shard_map/ppermute | solution.py:74
  5.2 10.2 %collective-permute-start.1 = (bf16[256,512]{1,0:T(8,128)(2,1)S(1)}, bf16[256,512]{1,0:T(8,128)(2,1)S(1)}, u32[]{:S(2)}, u32[]{:S(2)}) collective-permute-start(bf16[256,512]{1,0:T(8,128)(2,1)S(1)} %pad_add_fusion.refs_2_), channel_id=1, source_target_pairs={{0,8},{4,12},{8,16},{12,20},{16,24},{20,28},{24,32},{28,36},{32,40... | collective-permute-start | bytes 786440 | tf_op jit(solution)/shard_map/ppermute | solution.py:74
  15.4 8.3 %collective-permute-start.10 = (bf16[256,1024]{1,0:T(8,128)(2,1)S(1)}, bf16[256,1024]{1,0:T(8,128)(2,1)S(1)}, u32[]{:S(2)}, u32[]{:S(2)}) collective-permute-start(bf16[256,1024]{1,0:T(8,128)(2,1)S(1)} %collective-permute-done.2.refs_2_.refs_3_), channel_id=1, source_target_pairs={{0,1},{1,2},{2,3},{3,0},{4,7},{5,4},{6,5},{7,6},{8,9},{9,10},{10,1... | collective-permute-start | bytes 1572872 | tf_op jit(solution)/shard_map/ppermute | solution.py:82
  15.5 4.1 %collective-permute-start.4 = (bf16[256,512]{1,0:T(8,128)(2,1)S(1)}, bf16[256,512]{1,0:T(8,128)(2,1)S(1)}, u32[]{:S(2)}, u32[]{:S(2)}) collective-permute-start(bf16[256,512]{1,0:T(8,128)(2,1)S(1)} %collective-permute-done.1.refs_3_), channel_id=1, source_target_pairs={{0,4},{4,0},{8,12},{12,8},{16,20},{20,16},{24,28},{28,24},{32,36},... | collective-permute-start | bytes 786440 | tf_op jit(solution)/shard_map/ppermute | solution.py:74
  18.1 6.9 %collective-permute-start.5 = (bf16[256,1024]{1,0:T(8,128)(2,1)}, bf16[256,1024]{1,0:T(8,128)(2,1)S(1)}, u32[]{:S(2)}, u32[]{:S(2)}) collective-permute-start(bf16[256,1024]{1,0:T(8,128)(2,1)} %refs_2_.3), channel_id=1, source_target_pairs={{0,4},{4,0},{8,12},{12,8},{16,20},{20,16},{24,28},{28,24},{32,36},... | collective-permute-start | bytes 1572872 | tf_op jit(solution)/shard_map/ppermute | solution.py:74
  18.1 6.9 %collective-permute-start.6 = (bf16[256,1024]{1,0:T(8,128)(2,1)S(1)}, bf16[256,1024]{1,0:T(8,128)(2,1)S(1)}, u32[]{:S(2)}, u32[]{:S(2)}) collective-permute-start(bf16[256,1024]{1,0:T(8,128)(2,1)S(1)} %collective-permute-done.2.refs_2_.refs_3_), channel_id=1, source_target_pairs={{0,4},{4,0},{8,12},{12,8},{16,20},{20,16},{24,28},{28,24},{32,36},... | collective-permute-start | bytes 1572872 | tf_op jit(solution)/shard_map/ppermute | solution.py:74
  18.6 6.4 %collective-permute-start.7 = (bf16[256,1024]{1,0:T(8,128)(2,1)S(1)}, bf16[256,1024]{1,0:T(8,128)(2,1)S(1)}, u32[]{:S(2)}, u32[]{:S(2)}) collective-permute-start(bf16[256,1024]{1,0:T(8,128)(2,1)S(1)} %collective-permute-done.3.refs_3_.refs_4_), channel_id=1, source_target_pairs={{0,4},{4,0},{8,12},{12,8},{16,20},{20,16},{24,28},{28,24},{32,36},... | collective-permute-start | bytes 1572872 | tf_op jit(solution)/shard_map/ppermute | solution.py:74
  23.2 7.2 %collective-permute-start.12 = (bf16[256,1024]{1,0:T(8,128)(2,1)S(1)}, bf16[256,1024]{1,0:T(8,128)(2,1)S(1)}, u32[]{:S(2)}, u32[]{:S(2)}) collective-permute-start(bf16[256,1024]{1,0:T(8,128)(2,1)S(1)} %get-tuple-element.42.refs_2_.refs_9_.refs_7_), channel_id=1, source_target_pairs={{0,4},{4,0},{8,12},{12,8},{16,20},{20,16},{24,28},{28,24},{32,36},... | collective-permute-start | bytes 1572872 | tf_op jit(solution)/shard_map/ppermute | solution.py:74
  23.8 6.6 %collective-permute-start.11 = (bf16[256,1024]{1,0:T(8,128)(2,1)S(1)}, bf16[256,1024]{1,0:T(8,128)(2,1)S(1)}, u32[]{:S(2)}, u32[]{:S(2)}) collective-permute-start(bf16[256,1024]{1,0:T(8,128)(2,1)S(1)} %collective-permute-done.10.refs_4_.refs_5_), channel_id=1, source_target_pairs={{0,4},{4,0},{8,12},{12,8},{16,20},{20,16},{24,28},{28,24},{32,36},... | collective-permute-start | bytes 1572872 | tf_op jit(solution)/shard_map/ppermute | solution.py:74
  30.3 15.2 %collective-permute-start.9 = (bf16[256,1024]{1,0:T(8,128)(2,1)S(1)}, bf16[256,1024]{1,0:T(8,128)(2,1)S(1)}, u32[]{:S(2)}, u32[]{:S(2)}) collective-permute-start(bf16[256,1024]{1,0:T(8,128)(2,1)S(1)} %get-tuple-element.48.refs_11_), channel_id=1, source_target_pairs={{0,1},{1,2},{2,3},{3,0},{4,7},{5,4},{6,5},{7,6},{8,9},{9,10},{10,1... | collective-permute-start | bytes 1572872 | tf_op jit(solution)/shard_map/ppermute | solution.py:82
  35.2 22.3 %collective-permute-start.17 = (bf16[1024,512]{1,0:T(8,128)(2,1)S(1)}, bf16[1024,512]{1,0:T(8,128)(2,1)S(1)}, u32[]{:S(2)}, u32[]{:S(2)}) collective-permute-start(bf16[1024,512]{1,0:T(8,128)(2,1)S(1)} %get-tuple-element.49.refs_6_), channel_id=1, source_target_pairs={{0,32},{4,12},{8,40},{12,20},{16,48},{20,28},{24,56},{28,4},{32,64... | collective-permute-start | bytes 3145736 | tf_op jit(solution)/shard_map/ppermute | solution.py:74
  36.4 26.6 %collective-permute-start.18 = (bf16[1024,512]{1,0:T(8,128)(2,1)}, bf16[1024,512]{1,0:T(8,128)(2,1)S(1)}, u32[]{:S(2)}, u32[]{:S(2)}) collective-permute-start(bf16[1024,512]{1,0:T(8,128)(2,1)} %get-tuple-element.57), channel_id=1, source_target_pairs={{0,96},{4,28},{8,104},{12,4},{16,112},{20,12},{24,120},{28,20},{32... | collective-permute-start | bytes 3145736 | tf_op jit(solution)/shard_map/ppermute | solution.py:74
  36.7 26.3 %collective-permute-start.19 = (bf16[1024,512]{1,0:T(8,128)(2,1)}, bf16[1024,512]{1,0:T(8,128)(2,1)S(1)}, u32[]{:S(2)}, u32[]{:S(2)}) collective-permute-start(bf16[1024,512]{1,0:T(8,128)(2,1)} %get-tuple-element.58), channel_id=1, source_target_pairs={{0,64},{4,20},{8,72},{12,28},{16,80},{20,4},{24,88},{28,12},{32,96... | collective-permute-start | bytes 3145736 | tf_op jit(solution)/shard_map/ppermute | solution.py:74
  38.1 14.8 %collective-permute-start.8 = (bf16[256,1024]{1,0:T(8,128)(2,1)S(1)}, bf16[256,1024]{1,0:T(8,128)(2,1)S(1)}, u32[]{:S(2)}, u32[]{:S(2)}) collective-permute-start(bf16[256,1024]{1,0:T(8,128)(2,1)S(1)} %get-tuple-element.46), channel_id=1, source_target_pairs={{0,3},{1,0},{2,1},{3,2},{4,5},{5,6},{6,7},{7,4},{8,11},{9,8},{10,9... | collective-permute-start | bytes 1572872 | tf_op jit(solution)/shard_map/ppermute | solution.py:82
  45.6 9.8 %collective-permute-start.13 = (bf16[256,1024]{1,0:T(8,128)(2,1)S(1)}, bf16[256,1024]{1,0:T(8,128)(2,1)S(1)}, u32[]{:S(2)}, u32[]{:S(2)}) collective-permute-start(bf16[256,1024]{1,0:T(8,128)(2,1)S(1)} %shard_map.106.refs_9_), channel_id=1, source_target_pairs={{0,1},{1,2},{2,3},{3,0},{4,7},{5,4},{6,5},{7,6},{8,9},{9,10},{10,1... | collective-permute-start | bytes 1572872 | tf_op jit(solution)/shard_map/ppermute | solution.py:82
  52.9 3.5 %collective-permute-start.15 = (bf16[256,512]{1,0:T(8,128)(2,1)S(1)}, bf16[256,512]{1,0:T(8,128)(2,1)S(1)}, u32[]{:S(2)}, u32[]{:S(2)}) collective-permute-start(bf16[256,512]{1,0:T(8,128)(2,1)S(1)} %get-tuple-element.55), channel_id=1, source_target_pairs={{0,4},{4,0},{8,12},{12,8},{16,20},{20,16},{24,28},{28,24},{32,36},... | collective-permute-start | bytes 786440 | tf_op jit(solution)/shard_map/ppermute | solution.py:74
  64.0 12.0 %collective-permute-start.20 = (bf16[256,512]{1,0:T(8,128)(2,1)S(1)}, bf16[256,512]{1,0:T(8,128)(2,1)S(1)}, u32[]{:S(2)}, u32[]{:S(2)}) collective-permute-start(bf16[256,512]{1,0:T(8,128)(2,1)S(1)} %get-tuple-element.60), channel_id=1, source_target_pairs={{0,16},{4,68},{8,24},{12,76},{16,0},{20,84},{24,8},{28,92},{32,48}... | collective-permute-start | bytes 786440 | tf_op jit(solution)/shard_map/ppermute | solution.py:74
  65.0 10.9 %collective-permute-start.21 = (bf16[256,512]{1,0:T(8,128)(2,1)S(1)}, bf16[256,512]{1,0:T(8,128)(2,1)S(1)}, u32[]{:S(2)}, u32[]{:S(2)}) collective-permute-start(bf16[256,512]{1,0:T(8,128)(2,1)S(1)} %get-tuple-element.61), channel_id=1, source_target_pairs={{0,8},{4,36},{8,16},{12,44},{16,24},{20,52},{24,0},{28,60},{32,40}... | collective-permute-start | bytes 786440 | tf_op jit(solution)/shard_map/ppermute | solution.py:74
  66.8 9.1 %collective-permute-start.22 = (bf16[256,512]{1,0:T(8,128)(2,1)S(1)}, bf16[256,512]{1,0:T(8,128)(2,1)S(1)}, u32[]{:S(2)}, u32[]{:S(2)}) collective-permute-start(bf16[256,512]{1,0:T(8,128)(2,1)S(1)} %get-tuple-element.62), channel_id=1, source_target_pairs={{0,24},{4,100},{8,0},{12,108},{16,8},{20,116},{24,16},{28,124},{32... | collective-permute-start | bytes 786440 | tf_op jit(solution)/shard_map/ppermute | solution.py:74
  66.8 22.0 %collective-permute-start.14 = (bf16[256,512]{1,0:T(8,128)(2,1)S(1)}, bf16[256,512]{1,0:T(8,128)(2,1)S(1)}, u32[]{:S(2)}, u32[]{:S(2)}) collective-permute-start(bf16[256,512]{1,0:T(8,128)(2,1)S(1)} %get-tuple-element.53), channel_id=1, source_target_pairs={{4,0},{16,4},{12,8},{24,12},{20,16},{32,20},{28,24},{40,28},{36,32... | collective-permute-start | bytes 786440 | tf_op jit(solution)/shard_map/ppermute | solution.py:74
  74.2 14.6 %collective-permute-start.16 = (bf16[256,512]{1,0:T(8,128)(2,1)S(1)}, bf16[256,512]{1,0:T(8,128)(2,1)S(1)}, u32[]{:S(2)}, u32[]{:S(2)}) collective-permute-start(bf16[256,512]{1,0:T(8,128)(2,1)S(1)} %shard_map.109.refs_5_), channel_id=1, source_target_pairs={{8,0},{12,4},{16,8},{20,12},{24,16},{28,20},{32,24},{36,28},{40,32... | collective-permute-start | bytes 786440 | tf_op jit(solution)/shard_map/ppermute | solution.py:74
  76.6 13.1 %collective-permute-start.23 = (bf16[128,512]{1,0:T(8,128)(2,1)S(1)}, bf16[128,512]{1,0:T(8,128)(2,1)S(1)}, u32[]{:S(2)}, u32[]{:S(2)}) collective-permute-start(bf16[128,512]{1,0:T(8,128)(2,1)S(1)} %get-tuple-element.63.refs_3_), channel_id=1, source_target_pairs={{0,4},{4,0},{8,12},{12,8},{16,20},{20,16},{24,28},{28,24},{32,36},... | collective-permute-start | bytes 393224 | tf_op jit(solution)/shard_map/ppermute | solution.py:74
  (5 other events, 33.4 us)

commit v4 on v3

--- a/solution.py
+++ b/solution.py
@@ -180,49 +180,49 @@
             dq[:, pl.ds((4 * g + h) * HD, HD)] = dqs[h * TOK : (h + 1) * TOK].astype(BF)
 
 
-def finish_kernel(own, from_mixed, from_two, dk, dv):
+def finish_kernel(own, from_mixed, from_two, dk, dv, token):
     total = own[...] + from_mixed[...].astype(F32) + from_two[...].astype(F32)
     dk[...] = total[:, : 2 * HD].astype(BF)
     dv[...] = total[:, 2 * HD :].astype(BF)
-
-
-def layer_sum_kernel(own, from_opp, from_same, out):
+    token[...] = jnp.zeros_like(token)
+
+
+def layer_sum_kernel(own, from_opp, from_same, out, token):
     total = own[...] + from_opp[...].astype(F32) + from_same[...].astype(F32)
     out[...] = total.astype(BF)
-
-
-def stream(info, w, w_here, sems, order):
-    rows = w_here.shape[1]
-    copies = []
-    for i, at in enumerate(order):
-        source = w.at[pl.ds(pl.multiple_of((at % SIDE) * rows, rows), rows), :]
-        copies.append(pltpu.make_async_copy(source, w_here.at[i], sems.at[i]))
-        copies[-1].start()
-    for i, copy in enumerate(copies):
-        copy.wait()
-        yield i, w_here[i]
-
-
-def out_kernel(info, w, att, across, opp, same_term, own, w_here, sems):
+    token[...] = jnp.zeros_like(token)
+
+
+def chunk(ref, at, size):
+    return ref[pl.ds(pl.multiple_of((at % SIDE) * size, size), size), :]
+
+
+def out_first_kernel(info, att, w, across, opp):
     z, way = info[1], 1 - 2 * (info[0] % 2)
-    outs = (across, opp, same_term, own)
-    order = (z + 2, z + SIDE - way, z + SIDE + way, z)
-    for i, rows in stream(info, w, w_here, sems, order):
-        outs[i][...] = dot_nt(att[...], rows).astype(outs[i].dtype)
+    rows = w.shape[0] // SIDE
+    across[...] = dot_nt(att[...], chunk(w, z + 2, rows)).astype(BF)
+    opp[...] = dot_nt(att[...], chunk(w, z + SIDE - way, rows)).astype(BF)
+
+
+def out_second_kernel(info, att, w, relayed, same_out, own):
+    z, way = info[1], 1 - 2 * (info[0] % 2)
+    rows = w.shape[0] // SIDE
+    term = dot_nt(att[...], chunk(w, z + SIDE + way, rows))
+    same_out[...] = (term + relayed[...].astype(F32)).astype(BF)
+    own[...] = dot_nt(att[...], chunk(w, z, rows))
 
 
 def add_kernel(a, b, out):
     out[...] = (a[...] + b[...].astype(F32)).astype(BF)
 
 
-def attn_grad_kernel(info, w, g, first, second, third, out, w_here, sems):
+def attn_grad_kernel(info, g, first, second, third, w, out):
     z, way = info[1], 1 - 2 * (info[0] % 2)
-    parts = (g, first, second, third)
-    order = (z, z + SIDE - way, z + SIDE + way, z + 2)
-    total = None
-    for i, rows in stream(info, w, w_here, sems, order):
-        term = dot_nn(parts[i][...], rows)
-        total = term if total is None else total + term
+    rows = w.shape[0] // SIDE
+    total = dot_nn(g[...], chunk(w, z, rows))
+    total = total + dot_nn(first[...], chunk(w, z + SIDE - way, rows))
+    total = total + dot_nn(second[...], chunk(w, z + SIDE + way, rows))
+    total = total + dot_nn(third[...], chunk(w, z + 2, rows))
     out[...] = total.astype(BF)
 
 
@@ -233,10 +233,27 @@
     return core, jnp.where(core == 0, x, y), jnp.where(core == 0, y, x)
 
 
-def weight_kernel(info, *refs):
-    here, there, att, att_there, across, plus, minus, own, g, a = refs[:4], refs[4:8], *refs[8:]
+def weight_terms(info, g, a, outs):
     core, at, _ = place(info)
-    z, way = info[1], 1 - 2 * core
+
+    @pl.when(core == 0)
+    def _():
+        for out, step in outs:
+            out[...] = dot_nn(g[(at + step) % SIDE].T, a[...]).astype(out.dtype)
+
+    @pl.when(core == 1)
+    def _():
+        for out, step in outs:
+            strip = pl.ds(pl.multiple_of(((at + step) % SIDE) * TOK, TOK), TOK)
+            for x in range(SIDE):
+                terms = dot_nn(g[x, :, strip].T, a[...])
+                out[x * TOK : (x + 1) * TOK, :] = terms.astype(out.dtype)
+
+
+def weight_across_kernel(info, *refs):
+    here, there, att, att_there, across, g, a = refs[:4], refs[4:8], *refs[8:]
+    core, z = info[0] % 2, info[1]
+    way = 1 - 2 * core
     half = a.shape[1]
     columns = pl.ds(pl.multiple_of(core * half, half), half)
     a[:TOK] = att[:, columns]
@@ -244,20 +261,11 @@
     for t, sources, w in ((0, here, way), (1, there, -way)):
         for source, chunk_at in zip(sources, (z, z + SIDE - w, z + SIDE + w, z + 2)):
             g[chunk_at % SIDE, t * TOK : (t + 1) * TOK, :] = source[...]
-    outs = ((across, 2), (plus, 1), (minus, SIDE - 1), (own, 0))
-
-    @pl.when(core == 0)
-    def _():
-        for out, step in outs:
-            out[...] = dot_nn(g[(at + step) % SIDE].T, a[...]).astype(out.dtype)
-
-    @pl.when(core == 1)
-    def _():
-        for out, step in outs:
-            strip = pl.ds(pl.multiple_of(((at + step) % SIDE) * TOK, TOK), TOK)
-            for x in range(SIDE):
-                terms = dot_nn(g[x, :, strip].T, a[...])
-                out[x * TOK : (x + 1) * TOK, :] = terms.astype(out.dtype)
+    weight_terms(info, g, a, ((across, 2),))
+
+
+def weight_next_kernel(info, g, a, plus, minus, own):
+    weight_terms(info, g, a, ((plus, 1), (minus, SIDE - 1), (own, 0)))
 
 
 def weight_sum_kernel(info, own, from_minus, from_plus, from_across, plus, minus, across, mine):
@@ -290,12 +298,13 @@
     half = cols // 2
     block = shape((TOK, cols), BF)
 
-    first = kv_send(out_grad, same)
-    second = kv_send(out_grad, opposite)
-
     own = jnp.pad(keys, ((0, 0), (0, 2 * HD))) + jnp.pad(values, ((0, 0), (2 * HD, 0)))
     two = seq_send(own, NEXT_CHIP)
     mixed = seq_send(own, MIXED)
+
+    first = kv_send(out_grad, same)
+    second = kv_send(lax.optimization_barrier((out_grad, own))[0], opposite)
+
     q, bias = call(
         prepare_kernel,
         [shape((2, 4 * TOK, HD), BF), shape((4, TOK, TOK), F32)],
@@ -303,13 +312,8 @@
         us=4,
         smem_in=2,
     )(info, doc_lengths, queries)
-    q, bias, mixed, two, first, second = lax.optimization_barrier(
-        (q, bias, mixed, two, first, second)
-    )
+    q, bias, mixed, two, first = lax.optimization_barrier((q, bias, mixed, two, first))
     swapped = seq_send(two, SWAP)
-    third = kv_send(first, same)
-    here = (out_grad, first, second, third)
-    there = tuple(seq_send(v, SWAP) for v in here)
     blocks = (own, two, mixed, swapped)
 
     att, lse = call(
@@ -319,56 +323,51 @@
         us=4,
         scratch=[VM((4, TOK, 4 * TOK), F32)],
     )(q, bias, *blocks)
+    third = kv_send(first, same)
+    first, second, _ = lax.optimization_barrier((first, second, att))
     att_there = seq_send(att, SWAP)
 
-    chunks = [VM((SIDE, cols, cols), BF), pltpu.SemaphoreType.DMA((SIDE,))]
-    block32 = shape((TOK, cols), F32)
-    out_across, out_opp, out_same, out_own = call(
-        out_kernel,
-        [block] * 2 + [block32] * 2,
-        1,
-        us=4,
-        smem_in=1,
-        hbm_in=1,
-        after=3,
-        scratch=chunks,
-        vmem_mib=48,
-    )(info, out_weight, att, *there[:3])
+    out_across, out_opp = call(out_first_kernel, [block] * 2, 2, us=2, smem_in=1)(info, att, out_weight)
+    out_relayed = kv_send(out_across, same)
+    out_from_opp = kv_send(out_opp, opposite)
+
+    here = (out_grad, first, second, third)
+    later = lax.optimization_barrier((third, out_across))[0]
+    there = tuple(seq_send(v, SWAP) for v in (out_grad, first, second, later))
     pieces = shape((4 * TOK, half), BF)
-    across, plus, minus, weight_own = call(
-        weight_kernel,
-        [pieces] * 3 + [shape((4 * TOK, half), F32)],
+    across, g, a = call(
+        weight_across_kernel,
+        [pieces, shape((SIDE, 2 * TOK, 4 * TOK), BF), shape((2 * TOK, half), BF)],
         10,
         us=4,
         smem_in=1,
         after=1,
-        scratch=[VM((SIDE, 2 * TOK, 4 * TOK), BF), VM((2 * TOK, half), BF)],
     )(info, *here, *there, att, att_there, out_across)
     stage = ("x", "y")
     from_across = seq_send(across, by_core(stage, 2))
+    plus, minus, weight_own = call(
+        weight_next_kernel, [pieces] * 2 + [shape((4 * TOK, half), F32)], 2, us=4, smem_in=1
+    )(info, g, a)
     from_minus = seq_send(plus, by_core(stage, 1))
     from_plus = seq_send(minus, by_core(stage, -1))
 
-    attn_grad = call(
-        attn_grad_kernel, block, 4, us=4, smem_in=1, hbm_in=1, after=1, scratch=chunks, vmem_mib=48
-    )(info, out_weight, *here, plus)
-    out_relayed = kv_send(out_across, same)
-    out_from_opp = kv_send(out_opp, opposite)
-
-    out_same = call(add_kernel, block, 2, us=1, after=1)(out_same, out_relayed, attn_grad)
-    out_from_same = kv_send(out_same, same)
+    attn_grad = call(attn_grad_kernel, block, 5, us=3, smem_in=1, after=1)(
+        info, *here, out_weight, plus
+    )
+
     part = shape((TOK, 4 * HD), F32)
     part16 = shape((TOK, 4 * HD), BF)
     query_grad, d_own, d_two, d_mixed, d_swapped = call(
-        bwd_kernel, [block, part, part, part16, part16], 9, us=6.5, after=1
-    )(q, bias, *blocks, lse, att, attn_grad, out_same)
-    layer_out = call(layer_sum_kernel, block, 3, us=1, after=1)(
-        out_own, out_from_opp, out_from_same, d_own
-    )
+        bwd_kernel, [block, part, part, part16, part16], 9, us=6.5, after=2
+    )(q, bias, *blocks, lse, att, attn_grad, out_relayed, out_from_opp)
     from_swapped = seq_send(d_swapped, SWAP)
     from_mixed = seq_send(d_mixed, back(MIXED))
-    d_two = call(add_kernel, part16, 2, us=1, after=1)(d_two, from_swapped, layer_out)
+    out_same, out_own = call(
+        out_second_kernel, [block, shape((TOK, cols), F32)], 3, us=2, smem_in=1, after=1
+    )(info, att, out_weight, out_relayed, d_own)
+    d_two = call(add_kernel, part16, 2, us=1, after=1)(d_two, from_swapped, out_same)
     from_two = seq_send(d_two, back(NEXT_CHIP))
+    out_from_same = kv_send(lax.optimization_barrier((out_same, d_two))[0], same)
 
     strip = shape((TOK, half), BF)
     plus, minus, across, mine = call(
@@ -385,14 +384,17 @@
         seq_send(plus, by_core(stage, 1)),
         seq_send(minus, by_core(stage, -1)),
     ]
-    kept, given = call(weight_halves_kernel, [shape((HD, half), BF)] * 2, 4, us=1, smem_in=1)(
-        info, mine, *last
-    )
-    key_grad, value_grad = call(finish_kernel, [shape((TOK, 2 * HD), BF)] * 2, 3, us=1, after=1)(
-        d_own, from_mixed, from_two, given
-    )
-    weight_grad = call(weight_join_kernel, shape((HD, cols), BF), 2, us=1, smem_in=1, after=1)(
-        info, kept, seq_send(given, SWAP), key_grad
+    layer_out, token = call(layer_sum_kernel, [block, shape((8, HD), F32)], 3, us=1, after=1)(
+        out_own, out_from_opp, out_from_same, across
+    )
+    key_grad, value_grad, token = call(
+        finish_kernel, [shape((TOK, 2 * HD), BF)] * 2 + [shape((8, HD), F32)], 3, us=1, after=1
+    )(d_own, from_mixed, from_two, token)
+    kept, given = call(weight_halves_kernel, [shape((HD, half), BF)] * 2, 4, us=1, smem_in=1, after=1)(
+        info, mine, *last, token
+    )
+    weight_grad = call(weight_join_kernel, shape((HD, cols), BF), 2, us=1, smem_in=1)(
+        info, kept, seq_send(given, SWAP)
     )
     return (layer_out, query_grad, key_grad, value_grad, weight_grad)
 

time: 92.2 us -> 85.2 us (0.924)
  the two profiles are of different devices: /device:TPU:95 before, /device:TPU:1 now
where the time goes in v4:
time: 85.2 us; the launch traced here: 83.5 us
  starting transfers between devices  28.4 us (33%)
  Pallas kernels  26.6 us (31%)
  waiting for transfers between devices  21.6 us (25%)
  local copies, waits for them, and re-layouts  5.09 us (6%)
  other arithmetic  1.06 us (1%)
    ppermute x18, waiting for transfers between devices, seq_send(): return lax.ppermute(v, 'seq', route)  21.2 us
    ppermute x18, starting transfers between devices, seq_send(): return lax.ppermute(v, 'seq', route)  16 us
    ppermute x6, starting transfers between devices, kv_send(): return lax.ppermute(v, ('seq', 'kv'), pairs)  12.4 us
    pallas_call x1, Pallas kernels, per_device(): call(bwd_kernel, [block, part, part, part16, part16], 9, us=6.5, after=2)  6.22 us
    unnamed x12, local copies, waits for them, and re-layouts  5.09 us
    pallas_call x1, Pallas kernels, per_device(): call(fwd_kernel, [block, shape((2, 4 * TOK), F32)], 6, us=4, scratch=[VM(...  3.58 us
    pallas_call x1, Pallas kernels, per_device(): call(attn_grad_kernel, block, 5, us=3, smem_in=1, after=1)  2.92 us
    pallas_call x1, Pallas kernels, per_device(): call(weight_next_kernel, [pieces] * 2 + [shape((4 * TOK, half), F32)], 2,...  2.62 us
  transfers between devices with their start and end apart: 24, of which 8 were waited for; matrix products, arithmetic and copies ran while one was open for 1% of the time, Pallas kernels for 29%

profile of v4, /device:TPU:1, one launch (start us, length us, event | category | flops | bytes accessed | tf_op | source)
XLA Modules:
  0.0 83.5 jit_solution(4589490017533119216)
XLA Ops:
  0.6 4.7 %collective-permute-start.2 = (bf16[256,1024]{1,0:T(8,128)(2,1)}, bf16[256,1024]{1,0:T(8,128)(2,1)S(1)}, u32[]{:S(2)}, u32[]{:S(2)}) collective-permute-start(bf16[256,1024]{1,0:T(8,128)(2,1)} %refs_1_.5), channel_id=1, source_target_pairs={{0,1},{1,2},{2,3},{3,0},{4,7},{5,4},{6,5},{7,6},{8,9},{9,10},{10,1... | collective-permute-start | bytes 1572872 | tf_op jit(solution)/shard_map/ppermute | solution.py:82
  6.3 1.4 %collective-permute-start.1 = (bf16[256,512]{1,0:T(8,128)(2,1)S(1)}, bf16[256,512]{1,0:T(8,128)(2,1)S(1)}, u32[]{:S(2)}, u32[]{:S(2)}) collective-permute-start(bf16[256,512]{1,0:T(8,128)(2,1)S(1)} %pad_add_fusion.refs_2_), channel_id=1, source_target_pairs={{0,8},{4,12},{8,16},{12,20},{16,24},{20,28},{24,32},{28,36},{32,40... | collective-permute-start | bytes 786440 | tf_op jit(solution)/shard_map/ppermute | solution.py:74
  7.6 1.6 %collective-permute-start = (bf16[256,512]{1,0:T(8,128)(2,1)S(1)}, bf16[256,512]{1,0:T(8,128)(2,1)S(1)}, u32[]{:S(2)}, u32[]{:S(2)}) collective-permute-start(bf16[256,512]{1,0:T(8,128)(2,1)S(1)} %pad_add_fusion.refs_2_), channel_id=1, source_target_pairs={{0,4},{4,16},{8,12},{12,24},{16,20},{20,32},{24,28},{28,40},{32,36... | collective-permute-start | bytes 786440 | tf_op jit(solution)/shard_map/ppermute | solution.py:74
  9.3 1.6 %collective-permute-start.5 = (bf16[256,1024]{1,0:T(8,128)(2,1)}, bf16[256,1024]{1,0:T(8,128)(2,1)S(1)}, u32[]{:S(2)}, u32[]{:S(2)}) collective-permute-start(bf16[256,1024]{1,0:T(8,128)(2,1)} %refs_1_.5), channel_id=1, source_target_pairs={{0,3},{1,0},{2,1},{3,2},{4,5},{5,6},{6,7},{7,4},{8,11},{9,8},{10,9... | collective-permute-start | bytes 1572872 | tf_op jit(solution)/shard_map/ppermute | solution.py:82
  13.9 5.9 %collective-permute-done.1.refs_3_ = bf16[256,512]{1,0:T(8,128)(2,1)S(1)} collective-permute-done((bf16[256,512]{1,0:T(8,128)(2,1)S(1)}, bf16[256,512]{1,0:T(8,128)(2,1)S(1)}, u32[]{:S(2)}, u32[]{:S(2)}) %collective-permute-start.1) | collective-permute-done | bytes 262176 | tf_op jit(solution)/shard_map/ppermute | solution.py:74
  20.0 1.5 %collective-permute-start.6 = (bf16[256,1024]{1,0:T(8,128)(2,1)S(1)}, bf16[256,1024]{1,0:T(8,128)(2,1)S(1)}, u32[]{:S(2)}, u32[]{:S(2)}) collective-permute-start(bf16[256,1024]{1,0:T(8,128)(2,1)S(1)} %collective-permute-done.2.refs_2_), channel_id=1, source_target_pairs={{0,1},{1,2},{2,3},{3,0},{4,7},{5,4},{6,5},{7,6},{8,9},{9,10},{10,1... | collective-permute-start | bytes 1572872 | tf_op jit(solution)/shard_map/ppermute | solution.py:82
  21.5 3.6 %shard_map.102 = (bf16[256,1024]{1,0:T(8,128)(2,1)S(1)}, f32[2,1024]{1,0:T(2,128)S(1)}) custom-call(bf16[2,1024,128]{2,1,0:T(8,128)(2,1)S(1)} %get-tuple-element.47.refs_0_, f32[4,256,256]{2,1,0:T(8,128)S(1)} %get-tuple-element.48.refs_1_, bf16[256,512]{1,0:T(8,128)(2,1)S(1)} %pad_add_fusion.refs_2_, bf16[256,512]{1,0:T(8,128)(2,1)S(1)} %collective-permute-done.1.refs_3_, ...), custom_call_target="tpu_custom_call" | custom-call | bytes 200000 | tf_op jit(solution)/shard_map/pallas_call | solution.py:319
  26.2 3.4 %copy-done = bf16[4096,1024]{1,0:T(8,128)(2,1)S(1)} copy-done((bf16[4096,1024]{1,0:T(8,128)(2,1)S(1)}, bf16[4096,1024]{1,0:T(8,128)(2,1)}, u32[]{:S(2)}) %copy-start) | copy-done | bytes 8388632
  29.6 1.8 %shard_map.103 = (bf16[256,1024]{1,0:T(8,128)(2,1)S(1)}, bf16[256,1024]{1,0:T(8,128)(2,1)S(1)}) custom-call(s32[2]{0:T(128)S(1)} %pad_add_fusion.1.refs_0_, bf16[256,1024]{1,0:T(8,128)(2,1)S(1)} %get-tuple-element.51.refs_1_.refs_9_.refs_7_, bf16[4096,1024]{1,0:T(8,128)(2,1)S(1)} %copy-done), custom_call_target="tpu_custom_call" | custom-call | bytes 100000 | tf_op jit(solution)/shard_map/pallas_call | solution.py:330
  31.6 2.7 %collective-permute-start.4 = (bf16[256,1024]{1,0:T(8,128)(2,1)S(1)}, bf16[256,1024]{1,0:T(8,128)(2,1)S(1)}, u32[]{:S(2)}, u32[]{:S(2)}) collective-permute-start(bf16[256,1024]{1,0:T(8,128)(2,1)S(1)} %get-tuple-element.52.refs_11_), channel_id=1, source_target_pairs={{0,1},{1,2},{2,3},{3,0},{4,7},{5,4},{6,5},{7,6},{8,9},{9,10},{10,1... | collective-permute-start | bytes 1572872 | tf_op jit(solution)/shard_map/ppermute | solution.py:82
  34.3 1.6 %shard_map.104 = (bf16[1024,512]{1,0:T(8,128)(2,1)S(1)}, bf16[4,512,1024]{2,1,0:T(8,128)(2,1)S(1)}, bf16[512,512]{1,0:T(8,128)(2,1)S(1)}) custom-call(s32[2]{0:T(128)S(1)} %pad_add_fusion.1.refs_0_, bf16[256,1024]{1,0:T(8,128)(2,1)S(1)} %copy-done.1, bf16[256,1024]{1,0:T(8,128)(2,1)S(1)} %collective-permute-done.2.refs_2_, ...), custom_call_target="tpu_custom_call" | custom-call | bytes 200000 | tf_op jit(solution)/shard_map/pallas_call | solution.py:338
  35.9 2.6 %shard_map.105 = (bf16[1024,512]{1,0:T(8,128)(2,1)S(1)}, bf16[1024,512]{1,0:T(8,128)(2,1)S(1)}, f32[1024,512]{1,0:T(8,128)S(1)}) custom-call(s32[2]{0:T(128)S(1)} %pad_add_fusion.1.refs_0_, bf16[4,512,1024]{2,1,0:T(8,128)(2,1)S(1)} %get-tuple-element.59.refs_1_, bf16[512,512]{1,0:T(8,128)(2,1)S(1)} %get-tuple-element.60.refs_2_), custom_call_target="tpu_custom_call" | custom-call | bytes 200000 | tf_op jit(solution)/shard_map/pallas_call | solution.py:348
  40.5 1.7 %collective-permute-start.17 = (bf16[1024,512]{1,0:T(8,128)(2,1)S(1)}, bf16[1024,512]{1,0:T(8,128)(2,1)S(1)}, u32[]{:S(2)}, u32[]{:S(2)}) collective-permute-start(bf16[1024,512]{1,0:T(8,128)(2,1)S(1)} %get-tuple-element.71), channel_id=1, source_target_pairs={{0,64},{4,20},{8,72},{12,28},{16,80},{20,4},{24,88},{28,12},{32,96... | collective-permute-start | bytes 3145736 | tf_op jit(solution)/shard_map/ppermute | solution.py:74
  42.3 2.9 %shard_map.106.refs_8_ = bf16[256,1024]{1,0:T(8,128)(2,1)S(1)} custom-call(s32[2]{0:T(128)S(1)} %pad_add_fusion.1.refs_0_, bf16[256,1024]{1,0:T(8,128)(2,1)S(1)} %copy-done.1, bf16[256,1024]{1,0:T(8,128)(2,1)S(1)} %collective-permute-done.2.refs_2_, bf16[256,1024]{1,0:T(8,128)(2,1)S(1)} %collective-permute-done.5.refs_3_, ...), custom_call_target="tpu_custom_call" | custom-call | bytes 150000 | tf_op jit(solution)/shard_map/pallas_call | solution.py:354
  45.6 6.2 %shard_map.107 = (bf16[256,1024]{1,0:T(8,128)(2,1)}, f32[256,512]{1,0:T(8,128)S(1)}, f32[256,512]{1,0:T(8,128)S(1)}, bf16[256,512]{1,0:T(8,128)(2,1)S(1)}, bf16[256,512]{1,0:T(8,128)(2,1)S(1)}) custom-call(bf16[2,1024,128]{2,1,0:T(8,128)(2,1)S(1)} %get-tuple-element.47.refs_0_, f32[4,256,256]{2,1,0:T(8,128)S(1)} %get-tuple-element.48.refs_1_, ...), custom_call_target="tpu_custom_call" | custom-call | bytes 325000 | tf_op jit(solution)/shard_map/pallas_call | solution.py:360
  51.8 1.6 %collective-permute-start.13 = (bf16[256,512]{1,0:T(8,128)(2,1)S(1)}, bf16[256,512]{1,0:T(8,128)(2,1)S(1)}, u32[]{:S(2)}, u32[]{:S(2)}) collective-permute-start(bf16[256,512]{1,0:T(8,128)(2,1)S(1)} %get-tuple-element.67), channel_id=1, source_target_pairs={{0,4},{4,0},{8,12},{12,8},{16,20},{20,16},{24,28},{28,24},{32,36},... | collective-permute-start | bytes 786440 | tf_op jit(solution)/shard_map/ppermute | solution.py:74
  53.4 1.8 %shard_map.108 = (bf16[256,1024]{1,0:T(8,128)(2,1)S(1)}, f32[256,1024]{1,0:T(8,128)S(1)}) custom-call(s32[2]{0:T(128)S(1)} %pad_add_fusion.1.refs_0_, bf16[256,1024]{1,0:T(8,128)(2,1)S(1)} %get-tuple-element.51.refs_1_.refs_9_.refs_7_, bf16[4096,1024]{1,0:T(8,128)(2,1)S(1)} %bitcast.3, bf16[256,1024]{1,0:T(8,128)(2,1)S(1)} %collective-permute-done.4.refs_9_.refs_3_, ...), custom_call_target="tpu_custom_call" | custom-call | bytes 100000 | tf_op jit(solution)/shard_map/pallas_call | solution.py:365
  55.3 2.0 %collective-permute-start.14 = (bf16[256,1024]{1,0:T(8,128)(2,1)S(1)}, bf16[256,1024]{1,0:T(8,128)(2,1)S(1)}, u32[]{:S(2)}, u32[]{:S(2)}) collective-permute-start(bf16[256,1024]{1,0:T(8,128)(2,1)S(1)} %get-tuple-element.68.refs_2_), channel_id=1, source_target_pairs={{0,1},{1,2},{2,3},{3,0},{4,7},{5,4},{6,5},{7,6},{8,9},{9,10},{10,1... | collective-permute-start | bytes 1572872 | tf_op jit(solution)/shard_map/ppermute | solution.py:82
  57.3 1.6 %collective-permute-start.19 = (bf16[256,512]{1,0:T(8,128)(2,1)S(1)}, bf16[256,512]{1,0:T(8,128)(2,1)S(1)}, u32[]{:S(2)}, u32[]{:S(2)}) collective-permute-start(bf16[256,512]{1,0:T(8,128)(2,1)S(1)} %shard_map.109.refs_5_), channel_id=1, source_target_pairs={{8,0},{12,4},{16,8},{20,12},{24,16},{28,20},{32,24},{36,28},{40,32... | collective-permute-start | bytes 786440 | tf_op jit(solution)/shard_map/ppermute | solution.py:74
  58.9 9.6 %collective-permute-done.17.refs_4_ = bf16[1024,512]{1,0:T(8,128)(2,1)S(1)} collective-permute-done((bf16[1024,512]{1,0:T(8,128)(2,1)S(1)}, bf16[1024,512]{1,0:T(8,128)(2,1)S(1)}, u32[]{:S(2)}, u32[]{:S(2)}) %collective-permute-start.17) | collective-permute-done | bytes 1048608 | tf_op jit(solution)/shard_map/ppermute | solution.py:74
  69.5 1.6 %collective-permute-start.21 = (bf16[256,512]{1,0:T(8,128)(2,1)S(1)}, bf16[256,512]{1,0:T(8,128)(2,1)S(1)}, u32[]{:S(2)}, u32[]{:S(2)}) collective-permute-start(bf16[256,512]{1,0:T(8,128)(2,1)S(1)} %get-tuple-element.80), channel_id=1, source_target_pairs={{0,8},{4,36},{8,16},{12,44},{16,24},{20,52},{24,0},{28,60},{32,40}... | collective-permute-start | bytes 786440 | tf_op jit(solution)/shard_map/ppermute | solution.py:74
  71.1 1.4 %collective-permute-start.22 = (bf16[256,512]{1,0:T(8,128)(2,1)S(1)}, bf16[256,512]{1,0:T(8,128)(2,1)S(1)}, u32[]{:S(2)}, u32[]{:S(2)}) collective-permute-start(bf16[256,512]{1,0:T(8,128)(2,1)S(1)} %get-tuple-element.81), channel_id=1, source_target_pairs={{0,24},{4,100},{8,0},{12,108},{16,8},{20,116},{24,16},{28,124},{32... | collective-permute-start | bytes 786440 | tf_op jit(solution)/shard_map/ppermute | solution.py:74
  72.5 1.6 %collective-permute-start.20 = (bf16[256,512]{1,0:T(8,128)(2,1)S(1)}, bf16[256,512]{1,0:T(8,128)(2,1)S(1)}, u32[]{:S(2)}, u32[]{:S(2)}) collective-permute-start(bf16[256,512]{1,0:T(8,128)(2,1)S(1)} %get-tuple-element.72.refs_3_), channel_id=1, source_target_pairs={{0,16},{4,68},{8,24},{12,76},{16,0},{20,84},{24,8},{28,92},{32,48}... | collective-permute-start | bytes 786440 | tf_op jit(solution)/shard_map/ppermute | solution.py:74
  76.6 3.5 %collective-permute-done.20.refs_2_ = bf16[256,512]{1,0:T(8,128)(2,1)S(1)} collective-permute-done((bf16[256,512]{1,0:T(8,128)(2,1)S(1)}, bf16[256,512]{1,0:T(8,128)(2,1)S(1)}, u32[]{:S(2)}, u32[]{:S(2)}) %collective-permute-start.20) | collective-permute-done | bytes 262176 | tf_op jit(solution)/shard_map/ppermute | solution.py:74
  (53 shorter events, 14.9 us)
Async XLA Ops:
  0.6 19.2 %collective-permute-start.2 = (bf16[256,1024]{1,0:T(8,128)(2,1)}, bf16[256,1024]{1,0:T(8,128)(2,1)S(1)}, u32[]{:S(2)}, u32[]{:S(2)}) collective-permute-start(bf16[256,1024]{1,0:T(8,128)(2,1)} %refs_1_.5), channel_id=1, source_target_pairs={{0,1},{1,2},{2,3},{3,0},{4,7},{5,4},{6,5},{7,6},{8,9},{9,10},{10,1... | collective-permute-start | bytes 1572872 | tf_op jit(solution)/shard_map/ppermute | solution.py:82
  6.3 13.5 %collective-permute-start.1 = (bf16[256,512]{1,0:T(8,128)(2,1)S(1)}, bf16[256,512]{1,0:T(8,128)(2,1)S(1)}, u32[]{:S(2)}, u32[]{:S(2)}) collective-permute-start(bf16[256,512]{1,0:T(8,128)(2,1)S(1)} %pad_add_fusion.refs_2_), channel_id=1, source_target_pairs={{0,8},{4,12},{8,16},{12,20},{16,24},{20,28},{24,32},{28,36},{32,40... | collective-permute-start | bytes 786440 | tf_op jit(solution)/shard_map/ppermute | solution.py:74
  7.6 12.2 %collective-permute-start = (bf16[256,512]{1,0:T(8,128)(2,1)S(1)}, bf16[256,512]{1,0:T(8,128)(2,1)S(1)}, u32[]{:S(2)}, u32[]{:S(2)}) collective-permute-start(bf16[256,512]{1,0:T(8,128)(2,1)S(1)} %pad_add_fusion.refs_2_), channel_id=1, source_target_pairs={{0,4},{4,16},{8,12},{12,24},{16,20},{20,32},{24,28},{28,40},{32,36... | collective-permute-start | bytes 786440 | tf_op jit(solution)/shard_map/ppermute | solution.py:74
  9.3 15.8 %collective-permute-start.5 = (bf16[256,1024]{1,0:T(8,128)(2,1)}, bf16[256,1024]{1,0:T(8,128)(2,1)S(1)}, u32[]{:S(2)}, u32[]{:S(2)}) collective-permute-start(bf16[256,1024]{1,0:T(8,128)(2,1)} %refs_1_.5), channel_id=1, source_target_pairs={{0,3},{1,0},{2,1},{3,2},{4,5},{5,6},{6,7},{7,4},{8,11},{9,8},{10,9... | collective-permute-start | bytes 1572872 | tf_op jit(solution)/shard_map/ppermute | solution.py:82
  19.8 1.7 %collective-permute-start.3 = (bf16[256,512]{1,0:T(8,128)(2,1)S(1)}, bf16[256,512]{1,0:T(8,128)(2,1)S(1)}, u32[]{:S(2)}, u32[]{:S(2)}) collective-permute-start(bf16[256,512]{1,0:T(8,128)(2,1)S(1)} %collective-permute-done.1.refs_3_), channel_id=1, source_target_pairs={{0,4},{4,0},{8,12},{12,8},{16,20},{20,16},{24,28},{28,24},{32,36},... | collective-permute-start | bytes 786440 | tf_op jit(solution)/shard_map/ppermute | solution.py:74
  20.0 11.4 %collective-permute-start.6 = (bf16[256,1024]{1,0:T(8,128)(2,1)S(1)}, bf16[256,1024]{1,0:T(8,128)(2,1)S(1)}, u32[]{:S(2)}, u32[]{:S(2)}) collective-permute-start(bf16[256,1024]{1,0:T(8,128)(2,1)S(1)} %collective-permute-done.2.refs_2_), channel_id=1, source_target_pairs={{0,1},{1,2},{2,3},{3,0},{4,7},{5,4},{6,5},{7,6},{8,9},{9,10},{10,1... | collective-permute-start | bytes 1572872 | tf_op jit(solution)/shard_map/ppermute | solution.py:82
  21.5 10.1 %collective-permute-start.7 = (bf16[256,1024]{1,0:T(8,128)(2,1)}, bf16[256,1024]{1,0:T(8,128)(2,1)S(1)}, u32[]{:S(2)}, u32[]{:S(2)}) collective-permute-start(bf16[256,1024]{1,0:T(8,128)(2,1)} %refs_1_.5), channel_id=1, source_target_pairs={{0,4},{4,0},{8,12},{12,8},{16,20},{20,16},{24,28},{28,24},{32,36},... | collective-permute-start | bytes 1572872 | tf_op jit(solution)/shard_map/ppermute | solution.py:74
  25.1 6.5 %collective-permute-start.8 = (bf16[256,1024]{1,0:T(8,128)(2,1)S(1)}, bf16[256,1024]{1,0:T(8,128)(2,1)S(1)}, u32[]{:S(2)}, u32[]{:S(2)}) collective-permute-start(bf16[256,1024]{1,0:T(8,128)(2,1)S(1)} %collective-permute-done.2.refs_2_), channel_id=1, source_target_pairs={{0,4},{4,0},{8,12},{12,8},{16,20},{20,16},{24,28},{28,24},{32,36},... | collective-permute-start | bytes 1572872 | tf_op jit(solution)/shard_map/ppermute | solution.py:74
  25.7 8.6 %collective-permute-start.11 = (bf16[256,1024]{1,0:T(8,128)(2,1)S(1)}, bf16[256,1024]{1,0:T(8,128)(2,1)S(1)}, u32[]{:S(2)}, u32[]{:S(2)}) collective-permute-start(bf16[256,1024]{1,0:T(8,128)(2,1)S(1)} %get-tuple-element.51.refs_1_.refs_9_.refs_7_), channel_id=1, source_target_pairs={{0,4},{4,0},{8,12},{12,8},{16,20},{20,16},{24,28},{28,24},{32,36},... | collective-permute-start | bytes 1572872 | tf_op jit(solution)/shard_map/ppermute | solution.py:74
  25.8 8.5 %collective-permute-start.9 = (bf16[256,1024]{1,0:T(8,128)(2,1)S(1)}, bf16[256,1024]{1,0:T(8,128)(2,1)S(1)}, u32[]{:S(2)}, u32[]{:S(2)}) collective-permute-start(bf16[256,1024]{1,0:T(8,128)(2,1)S(1)} %collective-permute-done.5.refs_3_), channel_id=1, source_target_pairs={{0,4},{4,0},{8,12},{12,8},{16,20},{20,16},{24,28},{28,24},{32,36},... | collective-permute-start | bytes 1572872 | tf_op jit(solution)/shard_map/ppermute | solution.py:74
  31.4 2.9 %collective-permute-start.10 = (bf16[256,1024]{1,0:T(8,128)(2,1)S(1)}, bf16[256,1024]{1,0:T(8,128)(2,1)S(1)}, u32[]{:S(2)}, u32[]{:S(2)}) collective-permute-start(bf16[256,1024]{1,0:T(8,128)(2,1)S(1)} %collective-permute-done.6.refs_4_), channel_id=1, source_target_pairs={{0,4},{4,0},{8,12},{12,8},{16,20},{20,16},{24,28},{28,24},{32,36},... | collective-permute-start | bytes 1572872 | tf_op jit(solution)/shard_map/ppermute | solution.py:74
  31.6 13.6 %collective-permute-start.12 = (bf16[256,1024]{1,0:T(8,128)(2,1)S(1)}, bf16[256,1024]{1,0:T(8,128)(2,1)S(1)}, u32[]{:S(2)}, u32[]{:S(2)}) collective-permute-start(bf16[256,1024]{1,0:T(8,128)(2,1)S(1)} %get-tuple-element.62), channel_id=1, source_target_pairs={{0,3},{1,0},{2,1},{3,2},{4,5},{5,6},{6,7},{7,4},{8,11},{9,8},{10,9... | collective-permute-start | bytes 1572872 | tf_op jit(solution)/shard_map/ppermute | solution.py:82
  31.6 14.0 %collective-permute-start.4 = (bf16[256,1024]{1,0:T(8,128)(2,1)S(1)}, bf16[256,1024]{1,0:T(8,128)(2,1)S(1)}, u32[]{:S(2)}, u32[]{:S(2)}) collective-permute-start(bf16[256,1024]{1,0:T(8,128)(2,1)S(1)} %get-tuple-element.52.refs_11_), channel_id=1, source_target_pairs={{0,1},{1,2},{2,3},{3,0},{4,7},{5,4},{6,5},{7,6},{8,9},{9,10},{10,1... | collective-permute-start | bytes 1572872 | tf_op jit(solution)/shard_map/ppermute | solution.py:82
  38.5 18.7 %collective-permute-start.16 = (bf16[1024,512]{1,0:T(8,128)(2,1)S(1)}, bf16[1024,512]{1,0:T(8,128)(2,1)S(1)}, u32[]{:S(2)}, u32[]{:S(2)}) collective-permute-start(bf16[1024,512]{1,0:T(8,128)(2,1)S(1)} %get-tuple-element.70), channel_id=1, source_target_pairs={{0,96},{4,28},{8,104},{12,4},{16,112},{20,12},{24,120},{28,20},{32... | collective-permute-start | bytes 3145736 | tf_op jit(solution)/shard_map/ppermute | solution.py:74
  39.5 19.4 %collective-permute-start.15 = (bf16[1024,512]{1,0:T(8,128)(2,1)S(1)}, bf16[1024,512]{1,0:T(8,128)(2,1)S(1)}, u32[]{:S(2)}, u32[]{:S(2)}) collective-permute-start(bf16[1024,512]{1,0:T(8,128)(2,1)S(1)} %get-tuple-element.61.refs_6_), channel_id=1, source_target_pairs={{0,32},{4,12},{8,40},{12,20},{16,48},{20,28},{24,56},{28,4},{32,64... | collective-permute-start | bytes 3145736 | tf_op jit(solution)/shard_map/ppermute | solution.py:74
  40.5 27.9 %collective-permute-start.17 = (bf16[1024,512]{1,0:T(8,128)(2,1)S(1)}, bf16[1024,512]{1,0:T(8,128)(2,1)S(1)}, u32[]{:S(2)}, u32[]{:S(2)}) collective-permute-start(bf16[1024,512]{1,0:T(8,128)(2,1)S(1)} %get-tuple-element.71), channel_id=1, source_target_pairs={{0,64},{4,20},{8,72},{12,28},{16,80},{20,4},{24,88},{28,12},{32,96... | collective-permute-start | bytes 3145736 | tf_op jit(solution)/shard_map/ppermute | solution.py:74
  51.8 3.4 %collective-permute-start.13 = (bf16[256,512]{1,0:T(8,128)(2,1)S(1)}, bf16[256,512]{1,0:T(8,128)(2,1)S(1)}, u32[]{:S(2)}, u32[]{:S(2)}) collective-permute-start(bf16[256,512]{1,0:T(8,128)(2,1)S(1)} %get-tuple-element.67), channel_id=1, source_target_pairs={{0,4},{4,0},{8,12},{12,8},{16,20},{20,16},{24,28},{28,24},{32,36},... | collective-permute-start | bytes 786440 | tf_op jit(solution)/shard_map/ppermute | solution.py:74
  55.3 17.2 %collective-permute-start.14 = (bf16[256,1024]{1,0:T(8,128)(2,1)S(1)}, bf16[256,1024]{1,0:T(8,128)(2,1)S(1)}, u32[]{:S(2)}, u32[]{:S(2)}) collective-permute-start(bf16[256,1024]{1,0:T(8,128)(2,1)S(1)} %get-tuple-element.68.refs_2_), channel_id=1, source_target_pairs={{0,1},{1,2},{2,3},{3,0},{4,7},{5,4},{6,5},{7,6},{8,9},{9,10},{10,1... | collective-permute-start | bytes 1572872 | tf_op jit(solution)/shard_map/ppermute | solution.py:82
  57.3 17.8 %collective-permute-start.18 = (bf16[256,512]{1,0:T(8,128)(2,1)S(1)}, bf16[256,512]{1,0:T(8,128)(2,1)S(1)}, u32[]{:S(2)}, u32[]{:S(2)}) collective-permute-start(bf16[256,512]{1,0:T(8,128)(2,1)S(1)} %get-tuple-element.75), channel_id=1, source_target_pairs={{4,0},{16,4},{12,8},{24,12},{20,16},{32,20},{28,24},{40,28},{36,32... | collective-permute-start | bytes 786440 | tf_op jit(solution)/shard_map/ppermute | solution.py:74
  57.3 17.9 %collective-permute-start.19 = (bf16[256,512]{1,0:T(8,128)(2,1)S(1)}, bf16[256,512]{1,0:T(8,128)(2,1)S(1)}, u32[]{:S(2)}, u32[]{:S(2)}) collective-permute-start(bf16[256,512]{1,0:T(8,128)(2,1)S(1)} %shard_map.109.refs_5_), channel_id=1, source_target_pairs={{8,0},{12,4},{16,8},{20,12},{24,16},{28,20},{32,24},{36,28},{40,32... | collective-permute-start | bytes 786440 | tf_op jit(solution)/shard_map/ppermute | solution.py:74
  69.5 6.7 %collective-permute-start.21 = (bf16[256,512]{1,0:T(8,128)(2,1)S(1)}, bf16[256,512]{1,0:T(8,128)(2,1)S(1)}, u32[]{:S(2)}, u32[]{:S(2)}) collective-permute-start(bf16[256,512]{1,0:T(8,128)(2,1)S(1)} %get-tuple-element.80), channel_id=1, source_target_pairs={{0,8},{4,36},{8,16},{12,44},{16,24},{20,52},{24,0},{28,60},{32,40}... | collective-permute-start | bytes 786440 | tf_op jit(solution)/shard_map/ppermute | solution.py:74
  71.1 5.5 %collective-permute-start.22 = (bf16[256,512]{1,0:T(8,128)(2,1)S(1)}, bf16[256,512]{1,0:T(8,128)(2,1)S(1)}, u32[]{:S(2)}, u32[]{:S(2)}) collective-permute-start(bf16[256,512]{1,0:T(8,128)(2,1)S(1)} %get-tuple-element.81), channel_id=1, source_target_pairs={{0,24},{4,100},{8,0},{12,108},{16,8},{20,116},{24,16},{28,124},{32... | collective-permute-start | bytes 786440 | tf_op jit(solution)/shard_map/ppermute | solution.py:74
  72.5 7.7 %collective-permute-start.20 = (bf16[256,512]{1,0:T(8,128)(2,1)S(1)}, bf16[256,512]{1,0:T(8,128)(2,1)S(1)}, u32[]{:S(2)}, u32[]{:S(2)}) collective-permute-start(bf16[256,512]{1,0:T(8,128)(2,1)S(1)} %get-tuple-element.72.refs_3_), channel_id=1, source_target_pairs={{0,16},{4,68},{8,24},{12,76},{16,0},{20,84},{24,8},{28,92},{32,48}... | collective-permute-start | bytes 786440 | tf_op jit(solution)/shard_map/ppermute | solution.py:74
  80.8 1.4 %collective-permute-start.23 = (bf16[128,512]{1,0:T(8,128)(2,1)S(1)}, bf16[128,512]{1,0:T(8,128)(2,1)S(1)}, u32[]{:S(2)}, u32[]{:S(2)}) collective-permute-start(bf16[128,512]{1,0:T(8,128)(2,1)S(1)} %get-tuple-element.84), channel_id=1, source_target_pairs={{0,4},{4,0},{8,12},{12,8},{16,20},{20,16},{24,28},{28,24},{32,36},... | collective-permute-start | bytes 393224 | tf_op jit(solution)/shard_map/ppermute | solution.py:74
  (6 other events, 33.2 us)

commit v5 on v4

--- a/solution.py
+++ b/solution.py
@@ -115,7 +115,7 @@
     return lax.fori_loop(0, 64, step, (jnp.int32(0), jnp.zeros_like(pos)))[1]
 
 
-def prepare_kernel(info, lengths, q, q_heads, bias):
+def prepare_kernel(info, lengths, q, w, q_heads, bias):
     core = info[0] % 2
     first = info[0] * TOK
     pos = first + lax.broadcasted_iota(jnp.int32, (1, TOK), 1)
@@ -308,10 +308,10 @@
     q, bias = call(
         prepare_kernel,
         [shape((2, 4 * TOK, HD), BF), shape((4, TOK, TOK), F32)],
-        1,
+        2,
         us=4,
         smem_in=2,
-    )(info, doc_lengths, queries)
+    )(info, doc_lengths, queries, out_weight)
     q, bias, mixed, two, first = lax.optimization_barrier((q, bias, mixed, two, first))
     swapped = seq_send(two, SWAP)
     blocks = (own, two, mixed, swapped)
@@ -328,8 +328,6 @@
     att_there = seq_send(att, SWAP)
 
     out_across, out_opp = call(out_first_kernel, [block] * 2, 2, us=2, smem_in=1)(info, att, out_weight)
-    out_relayed = kv_send(out_across, same)
-    out_from_opp = kv_send(out_opp, opposite)
 
     here = (out_grad, first, second, third)
     later = lax.optimization_barrier((third, out_across))[0]
@@ -351,6 +349,10 @@
     from_minus = seq_send(plus, by_core(stage, 1))
     from_plus = seq_send(minus, by_core(stage, -1))
 
+    send_across, send_opp, _ = lax.optimization_barrier((out_across, out_opp, plus))
+    out_relayed = kv_send(send_across, same)
+    out_from_opp = kv_send(send_opp, opposite)
+
     attn_grad = call(attn_grad_kernel, block, 5, us=3, smem_in=1, after=1)(
         info, *here, out_weight, plus
     )
@@ -358,14 +360,16 @@
     part = shape((TOK, 4 * HD), F32)
     part16 = shape((TOK, 4 * HD), BF)
     query_grad, d_own, d_two, d_mixed, d_swapped = call(
-        bwd_kernel, [block, part, part, part16, part16], 9, us=6.5, after=2
-    )(q, bias, *blocks, lse, att, attn_grad, out_relayed, out_from_opp)
+        bwd_kernel, [block, part, part, part16, part16], 9, us=6.5
+    )(q, bias, *blocks, lse, att, attn_grad)
     from_swapped = seq_send(d_swapped, SWAP)
     from_mixed = seq_send(d_mixed, back(MIXED))
     out_same, out_own = call(
-        out_second_kernel, [block, shape((TOK, cols), F32)], 3, us=2, smem_in=1, after=1
-    )(info, att, out_weight, out_relayed, d_own)
-    d_two = call(add_kernel, part16, 2, us=1, after=1)(d_two, from_swapped, out_same)
+        out_second_kernel, [block, shape((TOK, cols), F32)], 3, us=2, smem_in=1, after=2
+    )(info, att, out_weight, out_relayed, d_own, out_from_opp)
+    d_two = call(add_kernel, part16, 2, us=1, after=2)(
+        d_two, from_swapped, out_same, from_across
+    )
     from_two = seq_send(d_two, back(NEXT_CHIP))
     out_from_same = kv_send(lax.optimization_barrier((out_same, d_two))[0], same)
 
@@ -388,8 +392,8 @@
         out_own, out_from_opp, out_from_same, across
     )
     key_grad, value_grad, token = call(
-        finish_kernel, [shape((TOK, 2 * HD), BF)] * 2 + [shape((8, HD), F32)], 3, us=1, after=1
-    )(d_own, from_mixed, from_two, token)
+        finish_kernel, [shape((TOK, 2 * HD), BF)] * 2 + [shape((8, HD), F32)], 3, us=1, after=2
+    )(d_own, from_mixed, from_two, token, last[0])
     kept, given = call(weight_halves_kernel, [shape((HD, half), BF)] * 2, 4, us=1, smem_in=1, after=1)(
         info, mine, *last, token
     )

time: 85.2 us -> 80.3 us (0.942); the launches traced: 83.5 us -> 80.1 us
  waiting for transfers between devices: 21.6 us -> 15 us
  starting transfers between devices: 28.4 us -> 31.7 us
    ppermute x18, starting transfers between devices: 16 us -> 22.8 us  [seq_send(): return lax.ppermute(v, 'seq', route)]
    ppermute x18, waiting for transfers between devices: 21.2 us -> 14.5 us  [seq_send(): return lax.ppermute(v, 'seq', route)]
    ppermute x6, starting transfers between devices: 12.4 us -> 8.87 us  [kv_send(): return lax.ppermute(v, ('seq', 'kv'), pairs)]
    unnamed x12 -> x10, local copies, waits for them, and re-layouts: 5.09 us -> 5.08 us
where the time goes in v5:
time: 80.3 us; the launch traced here: 80.1 us
  starting transfers between devices  31.7 us (39%)
  Pallas kernels  26.5 us (33%)
  waiting for transfers between devices  15 us (19%)
  local copies, waits for them, and re-layouts  5.08 us (6%)
  other arithmetic  1.06 us (1%)
    ppermute x18, starting transfers between devices, seq_send(): return lax.ppermute(v, 'seq', route)  22.8 us
    ppermute x18, waiting for transfers between devices, seq_send(): return lax.ppermute(v, 'seq', route)  14.5 us
    ppermute x6, starting transfers between devices, kv_send(): return lax.ppermute(v, ('seq', 'kv'), pairs)  8.87 us
    pallas_call x1, Pallas kernels, per_device(): call(bwd_kernel, [block, part, part, part16, part16], 9, us=6.5)  6.21 us
    unnamed x10, local copies, waits for them, and re-layouts  5.08 us
    pallas_call x1, Pallas kernels, per_device(): call(fwd_kernel, [block, shape((2, 4 * TOK), F32)], 6, us=4, scratch=[VM(...  3.57 us
    pallas_call x1, Pallas kernels, per_device(): call(attn_grad_kernel, block, 5, us=3, smem_in=1, after=1)  2.92 us
    pallas_call x1, Pallas kernels, per_device(): call(weight_next_kernel, [pieces] * 2 + [shape((4 * TOK, half), F32)], 2,...  2.61 us
  transfers between devices with their start and end apart: 24, of which 8 were waited for; matrix products, arithmetic and copies ran while one was open for 1% of the time, Pallas kernels for 29%

profile of v5, /device:TPU:1, one launch (start us, length us, event | category | flops | bytes accessed | tf_op | source)
XLA Modules:
  0.0 80.1 jit_solution(942948445057362340)
XLA Ops:
  0.6 4.7 %collective-permute-start.2 = (bf16[256,1024]{1,0:T(8,128)(2,1)}, bf16[256,1024]{1,0:T(8,128)(2,1)S(1)}, u32[]{:S(2)}, u32[]{:S(2)}) collective-permute-start(bf16[256,1024]{1,0:T(8,128)(2,1)} %refs_1_.5), channel_id=1, source_target_pairs={{0,1},{1,2},{2,3},{3,0},{4,7},{5,4},{6,5},{7,6},{8,9},{9,10},{10,1... | collective-permute-start | bytes 1572872 | tf_op jit(solution)/shard_map/ppermute | solution.py:82
  6.3 1.4 %collective-permute-start.1 = (bf16[256,512]{1,0:T(8,128)(2,1)S(1)}, bf16[256,512]{1,0:T(8,128)(2,1)S(1)}, u32[]{:S(2)}, u32[]{:S(2)}) collective-permute-start(bf16[256,512]{1,0:T(8,128)(2,1)S(1)} %pad_add_fusion.refs_2_), channel_id=1, source_target_pairs={{0,8},{4,12},{8,16},{12,20},{16,24},{20,28},{24,32},{28,36},{32,40... | collective-permute-start | bytes 786440 | tf_op jit(solution)/shard_map/ppermute | solution.py:74
  7.6 1.6 %collective-permute-start = (bf16[256,512]{1,0:T(8,128)(2,1)S(1)}, bf16[256,512]{1,0:T(8,128)(2,1)S(1)}, u32[]{:S(2)}, u32[]{:S(2)}) collective-permute-start(bf16[256,512]{1,0:T(8,128)(2,1)S(1)} %pad_add_fusion.refs_2_), channel_id=1, source_target_pairs={{0,4},{4,16},{8,12},{12,24},{16,20},{20,32},{24,28},{28,40},{32,36... | collective-permute-start | bytes 786440 | tf_op jit(solution)/shard_map/ppermute | solution.py:74
  9.3 1.6 %collective-permute-start.4 = (bf16[256,1024]{1,0:T(8,128)(2,1)}, bf16[256,1024]{1,0:T(8,128)(2,1)S(1)}, u32[]{:S(2)}, u32[]{:S(2)}) collective-permute-start(bf16[256,1024]{1,0:T(8,128)(2,1)} %refs_1_.5), channel_id=1, source_target_pairs={{0,3},{1,0},{2,1},{3,2},{4,5},{5,6},{6,7},{7,4},{8,11},{9,8},{10,9... | collective-permute-start | bytes 1572872 | tf_op jit(solution)/shard_map/ppermute | solution.py:82
  11.0 3.4 %copy-done = bf16[4096,1024]{1,0:T(8,128)(2,1)S(1)} copy-done((bf16[4096,1024]{1,0:T(8,128)(2,1)S(1)}, bf16[4096,1024]{1,0:T(8,128)(2,1)}, u32[]{:S(2)}) %copy-start) | copy-done | bytes 8388632
  17.3 2.5 %collective-permute-done.1.refs_3_ = bf16[256,512]{1,0:T(8,128)(2,1)S(1)} collective-permute-done((bf16[256,512]{1,0:T(8,128)(2,1)S(1)}, bf16[256,512]{1,0:T(8,128)(2,1)S(1)}, u32[]{:S(2)}, u32[]{:S(2)}) %collective-permute-start.1) | collective-permute-done | bytes 262176 | tf_op jit(solution)/shard_map/ppermute | solution.py:74
  21.4 3.6 %shard_map.102 = (bf16[256,1024]{1,0:T(8,128)(2,1)S(1)}, f32[2,1024]{1,0:T(2,128)S(1)}) custom-call(bf16[2,1024,128]{2,1,0:T(8,128)(2,1)S(1)} %get-tuple-element.49.refs_0_, f32[4,256,256]{2,1,0:T(8,128)S(1)} %get-tuple-element.50.refs_1_, bf16[256,512]{1,0:T(8,128)(2,1)S(1)} %pad_add_fusion.refs_2_, bf16[256,512]{1,0:T(8,128)(2,1)S(1)} %collective-permute-done.1.refs_3_, ...), custom_call_target="tpu_custom_call" | custom-call | bytes 200000 | tf_op jit(solution)/shard_map/pallas_call | solution.py:319
  25.2 1.8 %shard_map.103 = (bf16[256,1024]{1,0:T(8,128)(2,1)S(1)}, bf16[256,1024]{1,0:T(8,128)(2,1)S(1)}) custom-call(s32[2]{0:T(128)S(1)} %pad_add_fusion.1.refs_0_, bf16[256,1024]{1,0:T(8,128)(2,1)S(1)} %get-tuple-element.53.refs_1_.refs_9_.refs_7_, bf16[4096,1024]{1,0:T(8,128)(2,1)S(1)} %copy-done.1), custom_call_target="tpu_custom_call" | custom-call | bytes 100000 | tf_op jit(solution)/shard_map/pallas_call | solution.py:330
  28.1 2.3 %collective-permute-start.9 = (bf16[256,1024]{1,0:T(8,128)(2,1)S(1)}, bf16[256,1024]{1,0:T(8,128)(2,1)S(1)}, u32[]{:S(2)}, u32[]{:S(2)}) collective-permute-start(bf16[256,1024]{1,0:T(8,128)(2,1)S(1)} %collective-permute-done.5.refs_4_), channel_id=1, source_target_pairs={{0,4},{4,0},{8,12},{12,8},{16,20},{20,16},{24,28},{28,24},{32,36},... | collective-permute-start | bytes 1572872 | tf_op jit(solution)/shard_map/ppermute | solution.py:74
  30.4 1.5 %collective-permute-done.9.refs_8_ = bf16[256,1024]{1,0:T(8,128)(2,1)S(1)} collective-permute-done((bf16[256,1024]{1,0:T(8,128)(2,1)S(1)}, bf16[256,1024]{1,0:T(8,128)(2,1)S(1)}, u32[]{:S(2)}, u32[]{:S(2)}) %collective-permute-start.9) | collective-permute-done | bytes 524320 | tf_op jit(solution)/shard_map/ppermute | solution.py:74
  32.0 1.6 %shard_map.104 = (bf16[1024,512]{1,0:T(8,128)(2,1)S(1)}, bf16[4,512,1024]{2,1,0:T(8,128)(2,1)S(1)}, bf16[512,512]{1,0:T(8,128)(2,1)S(1)}) custom-call(s32[2]{0:T(128)S(1)} %pad_add_fusion.1.refs_0_, bf16[256,1024]{1,0:T(8,128)(2,1)S(1)} %copy-done.2, bf16[256,1024]{1,0:T(8,128)(2,1)S(1)} %collective-permute-done.2.refs_2_, ...), custom_call_target="tpu_custom_call" | custom-call | bytes 200000 | tf_op jit(solution)/shard_map/pallas_call | solution.py:336
  33.7 2.6 %shard_map.105 = (bf16[1024,512]{1,0:T(8,128)(2,1)S(1)}, bf16[1024,512]{1,0:T(8,128)(2,1)S(1)}, f32[1024,512]{1,0:T(8,128)S(1)}) custom-call(s32[2]{0:T(128)S(1)} %pad_add_fusion.1.refs_0_, bf16[4,512,1024]{2,1,0:T(8,128)(2,1)S(1)} %get-tuple-element.61.refs_1_, bf16[512,512]{1,0:T(8,128)(2,1)S(1)} %get-tuple-element.62.refs_2_), custom_call_target="tpu_custom_call" | custom-call | bytes 200000 | tf_op jit(solution)/shard_map/pallas_call | solution.py:346
  36.3 1.6 %collective-permute-start.11 = (bf16[256,1024]{1,0:T(8,128)(2,1)S(1)}, bf16[256,1024]{1,0:T(8,128)(2,1)S(1)}, u32[]{:S(2)}, u32[]{:S(2)}) collective-permute-start(bf16[256,1024]{1,0:T(8,128)(2,1)S(1)} %get-tuple-element.64.refs_11_), channel_id=1, source_target_pairs={{0,1},{1,2},{2,3},{3,0},{4,7},{5,4},{6,5},{7,6},{8,9},{9,10},{10,1... | collective-permute-start | bytes 1572872 | tf_op jit(solution)/shard_map/ppermute | solution.py:82
  38.0 4.6 %collective-permute-start.17 = (bf16[1024,512]{1,0:T(8,128)(2,1)S(1)}, bf16[1024,512]{1,0:T(8,128)(2,1)S(1)}, u32[]{:S(2)}, u32[]{:S(2)}) collective-permute-start(bf16[1024,512]{1,0:T(8,128)(2,1)S(1)} %get-tuple-element.75), channel_id=1, source_target_pairs={{0,96},{4,28},{8,104},{12,4},{16,112},{20,12},{24,120},{28,20},{32... | collective-permute-start | bytes 3145736 | tf_op jit(solution)/shard_map/ppermute | solution.py:74
  42.5 2.9 %shard_map.106.refs_8_ = bf16[256,1024]{1,0:T(8,128)(2,1)S(1)} custom-call(s32[2]{0:T(128)S(1)} %pad_add_fusion.1.refs_0_, bf16[256,1024]{1,0:T(8,128)(2,1)S(1)} %copy-done.2, bf16[256,1024]{1,0:T(8,128)(2,1)S(1)} %collective-permute-done.2.refs_2_, bf16[256,1024]{1,0:T(8,128)(2,1)S(1)} %collective-permute-done.4.refs_3_, ...), custom_call_target="tpu_custom_call" | custom-call | bytes 150000 | tf_op jit(solution)/shard_map/pallas_call | solution.py:356
  45.5 6.2 %shard_map.107 = (bf16[256,1024]{1,0:T(8,128)(2,1)}, f32[256,512]{1,0:T(8,128)S(1)}, f32[256,512]{1,0:T(8,128)S(1)}, bf16[256,512]{1,0:T(8,128)(2,1)S(1)}, bf16[256,512]{1,0:T(8,128)(2,1)S(1)}) custom-call(bf16[2,1024,128]{2,1,0:T(8,128)(2,1)S(1)} %get-tuple-element.49.refs_0_, f32[4,256,256]{2,1,0:T(8,128)S(1)} %get-tuple-element.50.refs_1_, ...), custom_call_target="tpu_custom_call" | custom-call | bytes 325000 | tf_op jit(solution)/shard_map/pallas_call | solution.py:362
  51.7 1.8 %collective-permute-start.13 = (bf16[256,512]{1,0:T(8,128)(2,1)S(1)}, bf16[256,512]{1,0:T(8,128)(2,1)S(1)}, u32[]{:S(2)}, u32[]{:S(2)}) collective-permute-start(bf16[256,512]{1,0:T(8,128)(2,1)S(1)} %get-tuple-element.71), channel_id=1, source_target_pairs={{0,4},{4,0},{8,12},{12,8},{16,20},{20,16},{24,28},{28,24},{32,36},... | collective-permute-start | bytes 786440 | tf_op jit(solution)/shard_map/ppermute | solution.py:74
  53.5 1.8 %shard_map.108 = (bf16[256,1024]{1,0:T(8,128)(2,1)S(1)}, f32[256,1024]{1,0:T(8,128)S(1)}) custom-call(s32[2]{0:T(128)S(1)} %pad_add_fusion.1.refs_0_, bf16[256,1024]{1,0:T(8,128)(2,1)S(1)} %get-tuple-element.53.refs_1_.refs_9_.refs_7_, bf16[4096,1024]{1,0:T(8,128)(2,1)S(1)} %copy-done.1, bf16[256,1024]{1,0:T(8,128)(2,1)S(1)} %collective-permute-done.11.refs_3_, ...), custom_call_target="tpu_custom_call" | custom-call | bytes 100000 | tf_op jit(solution)/shard_map/pallas_call | solution.py:367
  56.4 5.2 %collective-permute-start.19 = (bf16[256,512]{1,0:T(8,128)(2,1)S(1)}, bf16[256,512]{1,0:T(8,128)(2,1)S(1)}, u32[]{:S(2)}, u32[]{:S(2)}) collective-permute-start(bf16[256,512]{1,0:T(8,128)(2,1)S(1)} %shard_map.109.refs_5_), channel_id=1, source_target_pairs={{8,0},{12,4},{16,8},{20,12},{24,16},{28,20},{32,24},{36,28},{40,32... | collective-permute-start | bytes 786440 | tf_op jit(solution)/shard_map/ppermute | solution.py:74
  64.2 2.4 %collective-permute-start.22 = (bf16[256,512]{1,0:T(8,128)(2,1)S(1)}, bf16[256,512]{1,0:T(8,128)(2,1)S(1)}, u32[]{:S(2)}, u32[]{:S(2)}) collective-permute-start(bf16[256,512]{1,0:T(8,128)(2,1)S(1)} %get-tuple-element.85), channel_id=1, source_target_pairs={{0,24},{4,100},{8,0},{12,108},{16,8},{20,116},{24,16},{28,124},{32... | collective-permute-start | bytes 786440 | tf_op jit(solution)/shard_map/ppermute | solution.py:74
  67.5 2.3 %collective-permute-done.20.refs_4_.refs_2_ = bf16[256,512]{1,0:T(8,128)(2,1)S(1)} collective-permute-done((bf16[256,512]{1,0:T(8,128)(2,1)S(1)}, bf16[256,512]{1,0:T(8,128)(2,1)S(1)}, u32[]{:S(2)}, u32[]{:S(2)}) %collective-permute-start.20) | collective-permute-done | bytes 262176 | tf_op jit(solution)/shard_map/ppermute | solution.py:74
  70.5 2.0 %collective-permute-done.21.refs_3_ = bf16[256,512]{1,0:T(8,128)(2,1)S(1)} collective-permute-done((bf16[256,512]{1,0:T(8,128)(2,1)S(1)}, bf16[256,512]{1,0:T(8,128)(2,1)S(1)}, u32[]{:S(2)}, u32[]{:S(2)}) %collective-permute-start.21) | collective-permute-done | bytes 262176 | tf_op jit(solution)/shard_map/ppermute | solution.py:74
  72.5 4.1 %collective-permute-done.22.refs_4_ = bf16[256,512]{1,0:T(8,128)(2,1)S(1)} collective-permute-done((bf16[256,512]{1,0:T(8,128)(2,1)S(1)}, bf16[256,512]{1,0:T(8,128)(2,1)S(1)}, u32[]{:S(2)}, u32[]{:S(2)}) %collective-permute-start.22) | collective-permute-done | bytes 262176 | tf_op jit(solution)/shard_map/ppermute | solution.py:74
  78.8 1.3 %shard_map.114 = bf16[128,1024]{1,0:T(8,128)(2,1)} custom-call(s32[2]{0:T(128)S(1)} %pad_add_fusion.1.refs_0_, bf16[128,512]{1,0:T(8,128)(2,1)S(1)} %get-tuple-element.87.refs_1_, bf16[128,512]{1,0:T(8,128)(2,1)S(1)} %collective-permute-done.23.refs_2_), custom_call_target="tpu_custom_call" | custom-call | bytes 50000 | tf_op jit(solution)/shard_map/pallas_call | solution.py:400
  (50 shorter events, 14.4 us)
Async XLA Ops:
  0.6 19.2 %collective-permute-start.2 = (bf16[256,1024]{1,0:T(8,128)(2,1)}, bf16[256,1024]{1,0:T(8,128)(2,1)S(1)}, u32[]{:S(2)}, u32[]{:S(2)}) collective-permute-start(bf16[256,1024]{1,0:T(8,128)(2,1)} %refs_1_.5), channel_id=1, source_target_pairs={{0,1},{1,2},{2,3},{3,0},{4,7},{5,4},{6,5},{7,6},{8,9},{9,10},{10,1... | collective-permute-start | bytes 1572872 | tf_op jit(solution)/shard_map/ppermute | solution.py:82
  6.3 13.5 %collective-permute-start.1 = (bf16[256,512]{1,0:T(8,128)(2,1)S(1)}, bf16[256,512]{1,0:T(8,128)(2,1)S(1)}, u32[]{:S(2)}, u32[]{:S(2)}) collective-permute-start(bf16[256,512]{1,0:T(8,128)(2,1)S(1)} %pad_add_fusion.refs_2_), channel_id=1, source_target_pairs={{0,8},{4,12},{8,16},{12,20},{16,24},{20,28},{24,32},{28,36},{32,40... | collective-permute-start | bytes 786440 | tf_op jit(solution)/shard_map/ppermute | solution.py:74
  7.6 12.2 %collective-permute-start = (bf16[256,512]{1,0:T(8,128)(2,1)S(1)}, bf16[256,512]{1,0:T(8,128)(2,1)S(1)}, u32[]{:S(2)}, u32[]{:S(2)}) collective-permute-start(bf16[256,512]{1,0:T(8,128)(2,1)S(1)} %pad_add_fusion.refs_2_), channel_id=1, source_target_pairs={{0,4},{4,16},{8,12},{12,24},{16,20},{20,32},{24,28},{28,40},{32,36... | collective-permute-start | bytes 786440 | tf_op jit(solution)/shard_map/ppermute | solution.py:74
  9.3 17.8 %collective-permute-start.4 = (bf16[256,1024]{1,0:T(8,128)(2,1)}, bf16[256,1024]{1,0:T(8,128)(2,1)S(1)}, u32[]{:S(2)}, u32[]{:S(2)}) collective-permute-start(bf16[256,1024]{1,0:T(8,128)(2,1)} %refs_1_.5), channel_id=1, source_target_pairs={{0,3},{1,0},{2,1},{3,2},{4,5},{5,6},{6,7},{7,4},{8,11},{9,8},{10,9... | collective-permute-start | bytes 1572872 | tf_op jit(solution)/shard_map/ppermute | solution.py:82
  19.8 8.3 %collective-permute-start.5 = (bf16[256,1024]{1,0:T(8,128)(2,1)S(1)}, bf16[256,1024]{1,0:T(8,128)(2,1)S(1)}, u32[]{:S(2)}, u32[]{:S(2)}) collective-permute-start(bf16[256,1024]{1,0:T(8,128)(2,1)S(1)} %collective-permute-done.2.refs_2_), channel_id=1, source_target_pairs={{0,1},{1,2},{2,3},{3,0},{4,7},{5,4},{6,5},{7,6},{8,9},{9,10},{10,1... | collective-permute-start | bytes 1572872 | tf_op jit(solution)/shard_map/ppermute | solution.py:82
  19.8 1.6 %collective-permute-start.3 = (bf16[256,512]{1,0:T(8,128)(2,1)S(1)}, bf16[256,512]{1,0:T(8,128)(2,1)S(1)}, u32[]{:S(2)}, u32[]{:S(2)}) collective-permute-start(bf16[256,512]{1,0:T(8,128)(2,1)S(1)} %collective-permute-done.1.refs_3_), channel_id=1, source_target_pairs={{0,4},{4,0},{8,12},{12,8},{16,20},{20,16},{24,28},{28,24},{32,36},... | collective-permute-start | bytes 786440 | tf_op jit(solution)/shard_map/ppermute | solution.py:74
  20.0 10.4 %collective-permute-start.6 = (bf16[256,1024]{1,0:T(8,128)(2,1)S(1)}, bf16[256,1024]{1,0:T(8,128)(2,1)S(1)}, u32[]{:S(2)}, u32[]{:S(2)}) collective-permute-start(bf16[256,1024]{1,0:T(8,128)(2,1)S(1)} %copy-done.2), channel_id=1, source_target_pairs={{0,4},{4,0},{8,12},{12,8},{16,20},{20,16},{24,28},{28,24},{32,36},... | collective-permute-start | bytes 1572872 | tf_op jit(solution)/shard_map/ppermute | solution.py:74
  25.0 5.4 %collective-permute-start.10 = (bf16[256,1024]{1,0:T(8,128)(2,1)S(1)}, bf16[256,1024]{1,0:T(8,128)(2,1)S(1)}, u32[]{:S(2)}, u32[]{:S(2)}) collective-permute-start(bf16[256,1024]{1,0:T(8,128)(2,1)S(1)} %get-tuple-element.53.refs_1_.refs_9_.refs_7_), channel_id=1, source_target_pairs={{0,4},{4,0},{8,12},{12,8},{16,20},{20,16},{24,28},{28,24},{32,36},... | collective-permute-start | bytes 1572872 | tf_op jit(solution)/shard_map/ppermute | solution.py:74
  27.1 3.3 %collective-permute-start.7 = (bf16[256,1024]{1,0:T(8,128)(2,1)S(1)}, bf16[256,1024]{1,0:T(8,128)(2,1)S(1)}, u32[]{:S(2)}, u32[]{:S(2)}) collective-permute-start(bf16[256,1024]{1,0:T(8,128)(2,1)S(1)} %collective-permute-done.2.refs_2_), channel_id=1, source_target_pairs={{0,4},{4,0},{8,12},{12,8},{16,20},{20,16},{24,28},{28,24},{32,36},... | collective-permute-start | bytes 1572872 | tf_op jit(solution)/shard_map/ppermute | solution.py:74
  27.5 2.9 %collective-permute-start.8 = (bf16[256,1024]{1,0:T(8,128)(2,1)S(1)}, bf16[256,1024]{1,0:T(8,128)(2,1)S(1)}, u32[]{:S(2)}, u32[]{:S(2)}) collective-permute-start(bf16[256,1024]{1,0:T(8,128)(2,1)S(1)} %collective-permute-done.4.refs_3_), channel_id=1, source_target_pairs={{0,4},{4,0},{8,12},{12,8},{16,20},{20,16},{24,28},{28,24},{32,36},... | collective-permute-start | bytes 1572872 | tf_op jit(solution)/shard_map/ppermute | solution.py:74
  28.1 3.8 %collective-permute-start.9 = (bf16[256,1024]{1,0:T(8,128)(2,1)S(1)}, bf16[256,1024]{1,0:T(8,128)(2,1)S(1)}, u32[]{:S(2)}, u32[]{:S(2)}) collective-permute-start(bf16[256,1024]{1,0:T(8,128)(2,1)S(1)} %collective-permute-done.5.refs_4_), channel_id=1, source_target_pairs={{0,4},{4,0},{8,12},{12,8},{16,20},{20,16},{24,28},{28,24},{32,36},... | collective-permute-start | bytes 1572872 | tf_op jit(solution)/shard_map/ppermute | solution.py:74
  33.6 21.8 %collective-permute-start.14 = (bf16[1024,512]{1,0:T(8,128)(2,1)S(1)}, bf16[1024,512]{1,0:T(8,128)(2,1)S(1)}, u32[]{:S(2)}, u32[]{:S(2)}) collective-permute-start(bf16[1024,512]{1,0:T(8,128)(2,1)S(1)} %get-tuple-element.72), channel_id=1, source_target_pairs={{0,64},{4,20},{8,72},{12,28},{16,80},{20,4},{24,88},{28,12},{32,96... | collective-permute-start | bytes 3145736 | tf_op jit(solution)/shard_map/ppermute | solution.py:74
  36.3 15.4 %collective-permute-start.11 = (bf16[256,1024]{1,0:T(8,128)(2,1)S(1)}, bf16[256,1024]{1,0:T(8,128)(2,1)S(1)}, u32[]{:S(2)}, u32[]{:S(2)}) collective-permute-start(bf16[256,1024]{1,0:T(8,128)(2,1)S(1)} %get-tuple-element.64.refs_11_), channel_id=1, source_target_pairs={{0,1},{1,2},{2,3},{3,0},{4,7},{5,4},{6,5},{7,6},{8,9},{9,10},{10,1... | collective-permute-start | bytes 1572872 | tf_op jit(solution)/shard_map/ppermute | solution.py:82
  38.0 15.6 %collective-permute-start.12 = (bf16[256,1024]{1,0:T(8,128)(2,1)S(1)}, bf16[256,1024]{1,0:T(8,128)(2,1)S(1)}, u32[]{:S(2)}, u32[]{:S(2)}) collective-permute-start(bf16[256,1024]{1,0:T(8,128)(2,1)S(1)} %get-tuple-element.67), channel_id=1, source_target_pairs={{0,3},{1,0},{2,1},{3,2},{4,5},{5,6},{6,7},{7,4},{8,11},{9,8},{10,9... | collective-permute-start | bytes 1572872 | tf_op jit(solution)/shard_map/ppermute | solution.py:82
  38.0 23.6 %collective-permute-start.17 = (bf16[1024,512]{1,0:T(8,128)(2,1)S(1)}, bf16[1024,512]{1,0:T(8,128)(2,1)S(1)}, u32[]{:S(2)}, u32[]{:S(2)}) collective-permute-start(bf16[1024,512]{1,0:T(8,128)(2,1)S(1)} %get-tuple-element.75), channel_id=1, source_target_pairs={{0,96},{4,28},{8,104},{12,4},{16,112},{20,12},{24,120},{28,20},{32... | collective-permute-start | bytes 3145736 | tf_op jit(solution)/shard_map/ppermute | solution.py:74
  42.5 19.0 %collective-permute-start.16 = (bf16[1024,512]{1,0:T(8,128)(2,1)S(1)}, bf16[1024,512]{1,0:T(8,128)(2,1)S(1)}, u32[]{:S(2)}, u32[]{:S(2)}) collective-permute-start(bf16[1024,512]{1,0:T(8,128)(2,1)S(1)} %get-tuple-element.63.refs_6_), channel_id=1, source_target_pairs={{0,32},{4,12},{8,40},{12,20},{16,48},{20,28},{24,56},{28,4},{32,64... | collective-permute-start | bytes 3145736 | tf_op jit(solution)/shard_map/ppermute | solution.py:74
  51.7 3.7 %collective-permute-start.13 = (bf16[256,512]{1,0:T(8,128)(2,1)S(1)}, bf16[256,512]{1,0:T(8,128)(2,1)S(1)}, u32[]{:S(2)}, u32[]{:S(2)}) collective-permute-start(bf16[256,512]{1,0:T(8,128)(2,1)S(1)} %get-tuple-element.71), channel_id=1, source_target_pairs={{0,4},{4,0},{8,12},{12,8},{16,20},{20,16},{24,28},{28,24},{32,36},... | collective-permute-start | bytes 786440 | tf_op jit(solution)/shard_map/ppermute | solution.py:74
  55.5 8.7 %collective-permute-start.15 = (bf16[256,1024]{1,0:T(8,128)(2,1)S(1)}, bf16[256,1024]{1,0:T(8,128)(2,1)S(1)}, u32[]{:S(2)}, u32[]{:S(2)}) collective-permute-start(bf16[256,1024]{1,0:T(8,128)(2,1)S(1)} %get-tuple-element.73.refs_2_), channel_id=1, source_target_pairs={{0,1},{1,2},{2,3},{3,0},{4,7},{5,4},{6,5},{7,6},{8,9},{9,10},{10,1... | collective-permute-start | bytes 1572872 | tf_op jit(solution)/shard_map/ppermute | solution.py:82
  56.4 11.1 %collective-permute-start.18 = (bf16[256,512]{1,0:T(8,128)(2,1)S(1)}, bf16[256,512]{1,0:T(8,128)(2,1)S(1)}, u32[]{:S(2)}, u32[]{:S(2)}) collective-permute-start(bf16[256,512]{1,0:T(8,128)(2,1)S(1)} %get-tuple-element.79), channel_id=1, source_target_pairs={{4,0},{16,4},{12,8},{24,12},{20,16},{32,20},{28,24},{40,28},{36,32... | collective-permute-start | bytes 786440 | tf_op jit(solution)/shard_map/ppermute | solution.py:74
  56.4 13.4 %collective-permute-start.19 = (bf16[256,512]{1,0:T(8,128)(2,1)S(1)}, bf16[256,512]{1,0:T(8,128)(2,1)S(1)}, u32[]{:S(2)}, u32[]{:S(2)}) collective-permute-start(bf16[256,512]{1,0:T(8,128)(2,1)S(1)} %shard_map.109.refs_5_), channel_id=1, source_target_pairs={{8,0},{12,4},{16,8},{20,12},{24,16},{28,20},{32,24},{36,28},{40,32... | collective-permute-start | bytes 786440 | tf_op jit(solution)/shard_map/ppermute | solution.py:74
  62.6 7.1 %collective-permute-start.20 = (bf16[256,512]{1,0:T(8,128)(2,1)S(1)}, bf16[256,512]{1,0:T(8,128)(2,1)S(1)}, u32[]{:S(2)}, u32[]{:S(2)}) collective-permute-start(bf16[256,512]{1,0:T(8,128)(2,1)S(1)} %get-tuple-element.76.refs_3_), channel_id=1, source_target_pairs={{0,16},{4,68},{8,24},{12,76},{16,0},{20,84},{24,8},{28,92},{32,48}... | collective-permute-start | bytes 786440 | tf_op jit(solution)/shard_map/ppermute | solution.py:74
  63.8 8.7 %collective-permute-start.21 = (bf16[256,512]{1,0:T(8,128)(2,1)S(1)}, bf16[256,512]{1,0:T(8,128)(2,1)S(1)}, u32[]{:S(2)}, u32[]{:S(2)}) collective-permute-start(bf16[256,512]{1,0:T(8,128)(2,1)S(1)} %get-tuple-element.84), channel_id=1, source_target_pairs={{0,8},{4,36},{8,16},{12,44},{16,24},{20,52},{24,0},{28,60},{32,40}... | collective-permute-start | bytes 786440 | tf_op jit(solution)/shard_map/ppermute | solution.py:74
  64.2 12.5 %collective-permute-start.22 = (bf16[256,512]{1,0:T(8,128)(2,1)S(1)}, bf16[256,512]{1,0:T(8,128)(2,1)S(1)}, u32[]{:S(2)}, u32[]{:S(2)}) collective-permute-start(bf16[256,512]{1,0:T(8,128)(2,1)S(1)} %get-tuple-element.85), channel_id=1, source_target_pairs={{0,24},{4,100},{8,0},{12,108},{16,8},{20,116},{24,16},{28,124},{32... | collective-permute-start | bytes 786440 | tf_op jit(solution)/shard_map/ppermute | solution.py:74
  77.3 1.5 %collective-permute-start.23 = (bf16[128,512]{1,0:T(8,128)(2,1)S(1)}, bf16[128,512]{1,0:T(8,128)(2,1)S(1)}, u32[]{:S(2)}, u32[]{:S(2)}) collective-permute-start(bf16[128,512]{1,0:T(8,128)(2,1)S(1)} %get-tuple-element.88), channel_id=1, source_target_pairs={{0,4},{4,0},{8,12},{12,8},{16,20},{20,16},{24,28},{28,24},{32,36},... | collective-permute-start | bytes 393224 | tf_op jit(solution)/shard_map/ppermute | solution.py:74
  (5 other events, 18.2 us)

commit v6 on v5

--- a/solution.py
+++ b/solution.py
@@ -330,8 +330,7 @@
     out_across, out_opp = call(out_first_kernel, [block] * 2, 2, us=2, smem_in=1)(info, att, out_weight)
 
     here = (out_grad, first, second, third)
-    later = lax.optimization_barrier((third, out_across))[0]
-    there = tuple(seq_send(v, SWAP) for v in (out_grad, first, second, later))
+    there = tuple(seq_send(v, SWAP) for v in (out_grad, first, second, third))
     pieces = shape((4 * TOK, half), BF)
     across, g, a = call(
         weight_across_kernel,

time: 80.3 us -> 79.3 us (0.988)
  waiting for transfers between devices: 15 us -> 13.6 us
    ppermute x18, waiting for transfers between devices: 14.5 us -> 11.2 us  [seq_send(): return lax.ppermute(v, 'seq', route)]
    ppermute x6, waiting for transfers between devices: 0.48 us -> 2.41 us  [kv_send(): return lax.ppermute(v, ('seq', 'kv'), pairs)]
    ppermute x18, starting transfers between devices: 22.8 us -> 23.6 us  [seq_send(): return lax.ppermute(v, 'seq', route)]
where the time goes in v6:
time: 79.3 us; the launch traced here: 79.1 us
  starting transfers between devices  32.1 us (40%)
  Pallas kernels  26.5 us (33%)
  waiting for transfers between devices  13.6 us (17%)
  local copies, waits for them, and re-layouts  5.08 us (6%)
  other arithmetic  1.06 us (1%)
  between operations  0.8 us (1%)
    ppermute x18, starting transfers between devices, seq_send(): return lax.ppermute(v, 'seq', route)  23.6 us
    ppermute x18, waiting for transfers between devices, seq_send(): return lax.ppermute(v, 'seq', route)  11.2 us
    ppermute x6, starting transfers between devices, kv_send(): return lax.ppermute(v, ('seq', 'kv'), pairs)  8.46 us
    pallas_call x1, Pallas kernels, per_device(): call(bwd_kernel, [block, part, part, part16, part16], 9, us=6.5)  6.21 us
    unnamed x10, local copies, waits for them, and re-layouts  5.08 us
    pallas_call x1, Pallas kernels, per_device(): call(fwd_kernel, [block, shape((2, 4 * TOK), F32)], 6, us=4, scratch=[VM(...  3.57 us
    pallas_call x1, Pallas kernels, per_device(): call(attn_grad_kernel, block, 5, us=3, smem_in=1, after=1)  2.92 us
    pallas_call x1, Pallas kernels, per_device(): call(weight_next_kernel, [pieces] * 2 + [shape((4 * TOK, half), F32)], 2,...  2.61 us
  transfers between devices with their start and end apart: 24, of which 8 were waited for; matrix products, arithmetic and copies ran while one was open for 1% of the time, Pallas kernels for 29%

profile of v6, /device:TPU:1, one launch (start us, length us, event | category | flops | bytes accessed | tf_op | source)
XLA Modules:
  0.0 79.1 jit_solution(1254730151129727706)
XLA Ops:
  0.6 4.7 %collective-permute-start.2 = (bf16[256,1024]{1,0:T(8,128)(2,1)}, bf16[256,1024]{1,0:T(8,128)(2,1)S(1)}, u32[]{:S(2)}, u32[]{:S(2)}) collective-permute-start(bf16[256,1024]{1,0:T(8,128)(2,1)} %refs_1_.5), channel_id=1, source_target_pairs={{0,1},{1,2},{2,3},{3,0},{4,7},{5,4},{6,5},{7,6},{8,9},{9,10},{10,1... | collective-permute-start | bytes 1572872 | tf_op jit(solution)/shard_map/ppermute | solution.py:82
  6.3 1.4 %collective-permute-start.1 = (bf16[256,512]{1,0:T(8,128)(2,1)S(1)}, bf16[256,512]{1,0:T(8,128)(2,1)S(1)}, u32[]{:S(2)}, u32[]{:S(2)}) collective-permute-start(bf16[256,512]{1,0:T(8,128)(2,1)S(1)} %pad_add_fusion.refs_2_), channel_id=1, source_target_pairs={{0,8},{4,12},{8,16},{12,20},{16,24},{20,28},{24,32},{28,36},{32,40... | collective-permute-start | bytes 786440 | tf_op jit(solution)/shard_map/ppermute | solution.py:74
  7.6 1.6 %collective-permute-start = (bf16[256,512]{1,0:T(8,128)(2,1)S(1)}, bf16[256,512]{1,0:T(8,128)(2,1)S(1)}, u32[]{:S(2)}, u32[]{:S(2)}) collective-permute-start(bf16[256,512]{1,0:T(8,128)(2,1)S(1)} %pad_add_fusion.refs_2_), channel_id=1, source_target_pairs={{0,4},{4,16},{8,12},{12,24},{16,20},{20,32},{24,28},{28,40},{32,36... | collective-permute-start | bytes 786440 | tf_op jit(solution)/shard_map/ppermute | solution.py:74
  9.3 1.6 %collective-permute-start.4 = (bf16[256,1024]{1,0:T(8,128)(2,1)}, bf16[256,1024]{1,0:T(8,128)(2,1)S(1)}, u32[]{:S(2)}, u32[]{:S(2)}) collective-permute-start(bf16[256,1024]{1,0:T(8,128)(2,1)} %refs_1_.5), channel_id=1, source_target_pairs={{0,3},{1,0},{2,1},{3,2},{4,5},{5,6},{6,7},{7,4},{8,11},{9,8},{10,9... | collective-permute-start | bytes 1572872 | tf_op jit(solution)/shard_map/ppermute | solution.py:82
  11.0 3.4 %copy-done = bf16[4096,1024]{1,0:T(8,128)(2,1)S(1)} copy-done((bf16[4096,1024]{1,0:T(8,128)(2,1)S(1)}, bf16[4096,1024]{1,0:T(8,128)(2,1)}, u32[]{:S(2)}) %copy-start) | copy-done | bytes 8388632
  17.3 2.5 %collective-permute-done.1.refs_3_ = bf16[256,512]{1,0:T(8,128)(2,1)S(1)} collective-permute-done((bf16[256,512]{1,0:T(8,128)(2,1)S(1)}, bf16[256,512]{1,0:T(8,128)(2,1)S(1)}, u32[]{:S(2)}, u32[]{:S(2)}) %collective-permute-start.1) | collective-permute-done | bytes 262176 | tf_op jit(solution)/shard_map/ppermute | solution.py:74
  21.4 3.6 %shard_map.102 = (bf16[256,1024]{1,0:T(8,128)(2,1)S(1)}, f32[2,1024]{1,0:T(2,128)S(1)}) custom-call(bf16[2,1024,128]{2,1,0:T(8,128)(2,1)S(1)} %get-tuple-element.48.refs_0_, f32[4,256,256]{2,1,0:T(8,128)S(1)} %get-tuple-element.49.refs_1_, bf16[256,512]{1,0:T(8,128)(2,1)S(1)} %pad_add_fusion.refs_2_, bf16[256,512]{1,0:T(8,128)(2,1)S(1)} %collective-permute-done.1.refs_3_, ...), custom_call_target="tpu_custom_call" | custom-call | bytes 200000 | tf_op jit(solution)/shard_map/pallas_call | solution.py:319
  25.7 2.4 %collective-permute-done.5.refs_4_ = bf16[256,1024]{1,0:T(8,128)(2,1)S(1)} collective-permute-done((bf16[256,1024]{1,0:T(8,128)(2,1)S(1)}, bf16[256,1024]{1,0:T(8,128)(2,1)S(1)}, u32[]{:S(2)}, u32[]{:S(2)}) %collective-permute-start.5) | collective-permute-done | bytes 524320 | tf_op jit(solution)/shard_map/ppermute | solution.py:82
  28.1 2.3 %collective-permute-start.9 = (bf16[256,1024]{1,0:T(8,128)(2,1)S(1)}, bf16[256,1024]{1,0:T(8,128)(2,1)S(1)}, u32[]{:S(2)}, u32[]{:S(2)}) collective-permute-start(bf16[256,1024]{1,0:T(8,128)(2,1)S(1)} %collective-permute-done.5.refs_4_), channel_id=1, source_target_pairs={{0,4},{4,0},{8,12},{12,8},{16,20},{20,16},{24,28},{28,24},{32,36},... | collective-permute-start | bytes 1572872 | tf_op jit(solution)/shard_map/ppermute | solution.py:74
  30.4 1.8 %shard_map.103 = (bf16[256,1024]{1,0:T(8,128)(2,1)S(1)}, bf16[256,1024]{1,0:T(8,128)(2,1)S(1)}) custom-call(s32[2]{0:T(128)S(1)} %pad_add_fusion.1.refs_0_, bf16[256,1024]{1,0:T(8,128)(2,1)S(1)} %get-tuple-element.52.refs_1_.refs_9_.refs_7_, bf16[4096,1024]{1,0:T(8,128)(2,1)S(1)} %copy-done.1), custom_call_target="tpu_custom_call" | custom-call | bytes 100000 | tf_op jit(solution)/shard_map/pallas_call | solution.py:330
  32.3 1.6 %shard_map.104 = (bf16[1024,512]{1,0:T(8,128)(2,1)S(1)}, bf16[4,512,1024]{2,1,0:T(8,128)(2,1)S(1)}, bf16[512,512]{1,0:T(8,128)(2,1)S(1)}) custom-call(s32[2]{0:T(128)S(1)} %pad_add_fusion.1.refs_0_, bf16[256,1024]{1,0:T(8,128)(2,1)S(1)} %copy-done.2, bf16[256,1024]{1,0:T(8,128)(2,1)S(1)} %collective-permute-done.2.refs_2_, ...), custom_call_target="tpu_custom_call" | custom-call | bytes 200000 | tf_op jit(solution)/shard_map/pallas_call | solution.py:335
  34.1 2.6 %shard_map.105 = (bf16[1024,512]{1,0:T(8,128)(2,1)S(1)}, bf16[1024,512]{1,0:T(8,128)(2,1)S(1)}, f32[1024,512]{1,0:T(8,128)S(1)}) custom-call(s32[2]{0:T(128)S(1)} %pad_add_fusion.1.refs_0_, bf16[4,512,1024]{2,1,0:T(8,128)(2,1)S(1)} %get-tuple-element.59.refs_1_, bf16[512,512]{1,0:T(8,128)(2,1)S(1)} %get-tuple-element.60.refs_2_), custom_call_target="tpu_custom_call" | custom-call | bytes 200000 | tf_op jit(solution)/shard_map/pallas_call | solution.py:345
  37.0 1.3 %collective-permute-start.12 = (bf16[256,1024]{1,0:T(8,128)(2,1)S(1)}, bf16[256,1024]{1,0:T(8,128)(2,1)S(1)}, u32[]{:S(2)}, u32[]{:S(2)}) collective-permute-start(bf16[256,1024]{1,0:T(8,128)(2,1)S(1)} %get-tuple-element.65), channel_id=1, source_target_pairs={{0,3},{1,0},{2,1},{3,2},{4,5},{5,6},{6,7},{7,4},{8,11},{9,8},{10,9... | collective-permute-start | bytes 1572872 | tf_op jit(solution)/shard_map/ppermute | solution.py:82
  38.2 4.6 %collective-permute-start.17 = (bf16[1024,512]{1,0:T(8,128)(2,1)S(1)}, bf16[1024,512]{1,0:T(8,128)(2,1)S(1)}, u32[]{:S(2)}, u32[]{:S(2)}) collective-permute-start(bf16[1024,512]{1,0:T(8,128)(2,1)S(1)} %get-tuple-element.73), channel_id=1, source_target_pairs={{0,96},{4,28},{8,104},{12,4},{16,112},{20,12},{24,120},{28,20},{32... | collective-permute-start | bytes 3145736 | tf_op jit(solution)/shard_map/ppermute | solution.py:74
  42.8 2.9 %shard_map.106.refs_8_ = bf16[256,1024]{1,0:T(8,128)(2,1)S(1)} custom-call(s32[2]{0:T(128)S(1)} %pad_add_fusion.1.refs_0_, bf16[256,1024]{1,0:T(8,128)(2,1)S(1)} %copy-done.2, bf16[256,1024]{1,0:T(8,128)(2,1)S(1)} %collective-permute-done.2.refs_2_, bf16[256,1024]{1,0:T(8,128)(2,1)S(1)} %collective-permute-done.4.refs_3_, ...), custom_call_target="tpu_custom_call" | custom-call | bytes 150000 | tf_op jit(solution)/shard_map/pallas_call | solution.py:355
  45.7 6.2 %shard_map.107 = (bf16[256,1024]{1,0:T(8,128)(2,1)}, f32[256,512]{1,0:T(8,128)S(1)}, f32[256,512]{1,0:T(8,128)S(1)}, bf16[256,512]{1,0:T(8,128)(2,1)S(1)}, bf16[256,512]{1,0:T(8,128)(2,1)S(1)}) custom-call(bf16[2,1024,128]{2,1,0:T(8,128)(2,1)S(1)} %get-tuple-element.48.refs_0_, f32[4,256,256]{2,1,0:T(8,128)S(1)} %get-tuple-element.49.refs_1_, ...), custom_call_target="tpu_custom_call" | custom-call | bytes 325000 | tf_op jit(solution)/shard_map/pallas_call | solution.py:361
  52.7 1.8 %shard_map.108 = (bf16[256,1024]{1,0:T(8,128)(2,1)S(1)}, f32[256,1024]{1,0:T(8,128)S(1)}) custom-call(s32[2]{0:T(128)S(1)} %pad_add_fusion.1.refs_0_, bf16[256,1024]{1,0:T(8,128)(2,1)S(1)} %get-tuple-element.52.refs_1_.refs_9_.refs_7_, bf16[4096,1024]{1,0:T(8,128)(2,1)S(1)} %copy-done.1, bf16[256,1024]{1,0:T(8,128)(2,1)S(1)} %collective-permute-done.11.refs_3_, ...), custom_call_target="tpu_custom_call" | custom-call | bytes 100000 | tf_op jit(solution)/shard_map/pallas_call | solution.py:366
  55.3 5.2 %collective-permute-start.19 = (bf16[256,512]{1,0:T(8,128)(2,1)S(1)}, bf16[256,512]{1,0:T(8,128)(2,1)S(1)}, u32[]{:S(2)}, u32[]{:S(2)}) collective-permute-start(bf16[256,512]{1,0:T(8,128)(2,1)S(1)} %shard_map.109.refs_5_), channel_id=1, source_target_pairs={{8,0},{12,4},{16,8},{20,12},{24,16},{28,20},{32,24},{36,28},{40,32... | collective-permute-start | bytes 786440 | tf_op jit(solution)/shard_map/ppermute | solution.py:74
  62.3 1.9 %collective-permute-start.20 = (bf16[256,512]{1,0:T(8,128)(2,1)S(1)}, bf16[256,512]{1,0:T(8,128)(2,1)S(1)}, u32[]{:S(2)}, u32[]{:S(2)}) collective-permute-start(bf16[256,512]{1,0:T(8,128)(2,1)S(1)} %get-tuple-element.74.refs_3_), channel_id=1, source_target_pairs={{0,16},{4,68},{8,24},{12,76},{16,0},{20,84},{24,8},{28,92},{32,48}... | collective-permute-start | bytes 786440 | tf_op jit(solution)/shard_map/ppermute | solution.py:74
  64.5 2.4 %collective-permute-start.22 = (bf16[256,512]{1,0:T(8,128)(2,1)S(1)}, bf16[256,512]{1,0:T(8,128)(2,1)S(1)}, u32[]{:S(2)}, u32[]{:S(2)}) collective-permute-start(bf16[256,512]{1,0:T(8,128)(2,1)S(1)} %get-tuple-element.83), channel_id=1, source_target_pairs={{0,24},{4,100},{8,0},{12,108},{16,8},{20,116},{24,16},{28,124},{32... | collective-permute-start | bytes 786440 | tf_op jit(solution)/shard_map/ppermute | solution.py:74
  67.8 1.3 %collective-permute-done.20.refs_4_.refs_2_ = bf16[256,512]{1,0:T(8,128)(2,1)S(1)} collective-permute-done((bf16[256,512]{1,0:T(8,128)(2,1)S(1)}, bf16[256,512]{1,0:T(8,128)(2,1)S(1)}, u32[]{:S(2)}, u32[]{:S(2)}) %collective-permute-start.20) | collective-permute-done | bytes 262176 | tf_op jit(solution)/shard_map/ppermute | solution.py:74
  69.9 2.2 %collective-permute-done.21.refs_3_ = bf16[256,512]{1,0:T(8,128)(2,1)S(1)} collective-permute-done((bf16[256,512]{1,0:T(8,128)(2,1)S(1)}, bf16[256,512]{1,0:T(8,128)(2,1)S(1)}, u32[]{:S(2)}, u32[]{:S(2)}) %collective-permute-start.21) | collective-permute-done | bytes 262176 | tf_op jit(solution)/shard_map/ppermute | solution.py:74
  72.2 2.2 %collective-permute-done.22.refs_4_ = bf16[256,512]{1,0:T(8,128)(2,1)S(1)} collective-permute-done((bf16[256,512]{1,0:T(8,128)(2,1)S(1)}, bf16[256,512]{1,0:T(8,128)(2,1)S(1)}, u32[]{:S(2)}, u32[]{:S(2)}) %collective-permute-start.22) | collective-permute-done | bytes 262176 | tf_op jit(solution)/shard_map/ppermute | solution.py:74
  75.1 1.8 %collective-permute-start.23 = (bf16[128,512]{1,0:T(8,128)(2,1)S(1)}, bf16[128,512]{1,0:T(8,128)(2,1)S(1)}, u32[]{:S(2)}, u32[]{:S(2)}) collective-permute-start(bf16[128,512]{1,0:T(8,128)(2,1)S(1)} %get-tuple-element.86), channel_id=1, source_target_pairs={{0,4},{4,0},{8,12},{12,8},{16,20},{20,16},{24,28},{28,24},{32,36},... | collective-permute-start | bytes 393224 | tf_op jit(solution)/shard_map/ppermute | solution.py:74
  (50 shorter events, 14.9 us)
Async XLA Ops:
  0.6 19.2 %collective-permute-start.2 = (bf16[256,1024]{1,0:T(8,128)(2,1)}, bf16[256,1024]{1,0:T(8,128)(2,1)S(1)}, u32[]{:S(2)}, u32[]{:S(2)}) collective-permute-start(bf16[256,1024]{1,0:T(8,128)(2,1)} %refs_1_.5), channel_id=1, source_target_pairs={{0,1},{1,2},{2,3},{3,0},{4,7},{5,4},{6,5},{7,6},{8,9},{9,10},{10,1... | collective-permute-start | bytes 1572872 | tf_op jit(solution)/shard_map/ppermute | solution.py:82
  6.3 13.5 %collective-permute-start.1 = (bf16[256,512]{1,0:T(8,128)(2,1)S(1)}, bf16[256,512]{1,0:T(8,128)(2,1)S(1)}, u32[]{:S(2)}, u32[]{:S(2)}) collective-permute-start(bf16[256,512]{1,0:T(8,128)(2,1)S(1)} %pad_add_fusion.refs_2_), channel_id=1, source_target_pairs={{0,8},{4,12},{8,16},{12,20},{16,24},{20,28},{24,32},{28,36},{32,40... | collective-permute-start | bytes 786440 | tf_op jit(solution)/shard_map/ppermute | solution.py:74
  7.6 12.2 %collective-permute-start = (bf16[256,512]{1,0:T(8,128)(2,1)S(1)}, bf16[256,512]{1,0:T(8,128)(2,1)S(1)}, u32[]{:S(2)}, u32[]{:S(2)}) collective-permute-start(bf16[256,512]{1,0:T(8,128)(2,1)S(1)} %pad_add_fusion.refs_2_), channel_id=1, source_target_pairs={{0,4},{4,16},{8,12},{12,24},{16,20},{20,32},{24,28},{28,40},{32,36... | collective-permute-start | bytes 786440 | tf_op jit(solution)/shard_map/ppermute | solution.py:74
  9.3 16.0 %collective-permute-start.4 = (bf16[256,1024]{1,0:T(8,128)(2,1)}, bf16[256,1024]{1,0:T(8,128)(2,1)S(1)}, u32[]{:S(2)}, u32[]{:S(2)}) collective-permute-start(bf16[256,1024]{1,0:T(8,128)(2,1)} %refs_1_.5), channel_id=1, source_target_pairs={{0,3},{1,0},{2,1},{3,2},{4,5},{5,6},{6,7},{7,4},{8,11},{9,8},{10,9... | collective-permute-start | bytes 1572872 | tf_op jit(solution)/shard_map/ppermute | solution.py:82
  19.8 8.3 %collective-permute-start.5 = (bf16[256,1024]{1,0:T(8,128)(2,1)S(1)}, bf16[256,1024]{1,0:T(8,128)(2,1)S(1)}, u32[]{:S(2)}, u32[]{:S(2)}) collective-permute-start(bf16[256,1024]{1,0:T(8,128)(2,1)S(1)} %collective-permute-done.2.refs_2_), channel_id=1, source_target_pairs={{0,1},{1,2},{2,3},{3,0},{4,7},{5,4},{6,5},{7,6},{8,9},{9,10},{10,1... | collective-permute-start | bytes 1572872 | tf_op jit(solution)/shard_map/ppermute | solution.py:82
  19.8 1.6 %collective-permute-start.3 = (bf16[256,512]{1,0:T(8,128)(2,1)S(1)}, bf16[256,512]{1,0:T(8,128)(2,1)S(1)}, u32[]{:S(2)}, u32[]{:S(2)}) collective-permute-start(bf16[256,512]{1,0:T(8,128)(2,1)S(1)} %collective-permute-done.1.refs_3_), channel_id=1, source_target_pairs={{0,4},{4,0},{8,12},{12,8},{16,20},{20,16},{24,28},{28,24},{32,36},... | collective-permute-start | bytes 786440 | tf_op jit(solution)/shard_map/ppermute | solution.py:74
  20.0 12.2 %collective-permute-start.6 = (bf16[256,1024]{1,0:T(8,128)(2,1)S(1)}, bf16[256,1024]{1,0:T(8,128)(2,1)S(1)}, u32[]{:S(2)}, u32[]{:S(2)}) collective-permute-start(bf16[256,1024]{1,0:T(8,128)(2,1)S(1)} %copy-done.2), channel_id=1, source_target_pairs={{0,4},{4,0},{8,12},{12,8},{16,20},{20,16},{24,28},{28,24},{32,36},... | collective-permute-start | bytes 1572872 | tf_op jit(solution)/shard_map/ppermute | solution.py:74
  25.0 7.3 %collective-permute-start.10 = (bf16[256,1024]{1,0:T(8,128)(2,1)S(1)}, bf16[256,1024]{1,0:T(8,128)(2,1)S(1)}, u32[]{:S(2)}, u32[]{:S(2)}) collective-permute-start(bf16[256,1024]{1,0:T(8,128)(2,1)S(1)} %get-tuple-element.52.refs_1_.refs_9_.refs_7_), channel_id=1, source_target_pairs={{0,4},{4,0},{8,12},{12,8},{16,20},{20,16},{24,28},{28,24},{32,36},... | collective-permute-start | bytes 1572872 | tf_op jit(solution)/shard_map/ppermute | solution.py:74
  25.2 7.0 %collective-permute-start.7 = (bf16[256,1024]{1,0:T(8,128)(2,1)S(1)}, bf16[256,1024]{1,0:T(8,128)(2,1)S(1)}, u32[]{:S(2)}, u32[]{:S(2)}) collective-permute-start(bf16[256,1024]{1,0:T(8,128)(2,1)S(1)} %collective-permute-done.2.refs_2_), channel_id=1, source_target_pairs={{0,4},{4,0},{8,12},{12,8},{16,20},{20,16},{24,28},{28,24},{32,36},... | collective-permute-start | bytes 1572872 | tf_op jit(solution)/shard_map/ppermute | solution.py:74
  25.6 6.7 %collective-permute-start.8 = (bf16[256,1024]{1,0:T(8,128)(2,1)S(1)}, bf16[256,1024]{1,0:T(8,128)(2,1)S(1)}, u32[]{:S(2)}, u32[]{:S(2)}) collective-permute-start(bf16[256,1024]{1,0:T(8,128)(2,1)S(1)} %collective-permute-done.4.refs_3_), channel_id=1, source_target_pairs={{0,4},{4,0},{8,12},{12,8},{16,20},{20,16},{24,28},{28,24},{32,36},... | collective-permute-start | bytes 1572872 | tf_op jit(solution)/shard_map/ppermute | solution.py:74
  28.1 4.2 %collective-permute-start.9 = (bf16[256,1024]{1,0:T(8,128)(2,1)S(1)}, bf16[256,1024]{1,0:T(8,128)(2,1)S(1)}, u32[]{:S(2)}, u32[]{:S(2)}) collective-permute-start(bf16[256,1024]{1,0:T(8,128)(2,1)S(1)} %collective-permute-done.5.refs_4_), channel_id=1, source_target_pairs={{0,4},{4,0},{8,12},{12,8},{16,20},{20,16},{24,28},{28,24},{32,36},... | collective-permute-start | bytes 1572872 | tf_op jit(solution)/shard_map/ppermute | solution.py:74
  33.9 20.6 %collective-permute-start.14 = (bf16[1024,512]{1,0:T(8,128)(2,1)S(1)}, bf16[1024,512]{1,0:T(8,128)(2,1)S(1)}, u32[]{:S(2)}, u32[]{:S(2)}) collective-permute-start(bf16[1024,512]{1,0:T(8,128)(2,1)S(1)} %get-tuple-element.70), channel_id=1, source_target_pairs={{0,64},{4,20},{8,72},{12,28},{16,80},{20,4},{24,88},{28,12},{32,96... | collective-permute-start | bytes 3145736 | tf_op jit(solution)/shard_map/ppermute | solution.py:74
  36.7 15.3 %collective-permute-start.11 = (bf16[256,1024]{1,0:T(8,128)(2,1)S(1)}, bf16[256,1024]{1,0:T(8,128)(2,1)S(1)}, u32[]{:S(2)}, u32[]{:S(2)}) collective-permute-start(bf16[256,1024]{1,0:T(8,128)(2,1)S(1)} %get-tuple-element.62.refs_11_), channel_id=1, source_target_pairs={{0,1},{1,2},{2,3},{3,0},{4,7},{5,4},{6,5},{7,6},{8,9},{9,10},{10,1... | collective-permute-start | bytes 1572872 | tf_op jit(solution)/shard_map/ppermute | solution.py:82
  37.0 15.8 %collective-permute-start.12 = (bf16[256,1024]{1,0:T(8,128)(2,1)S(1)}, bf16[256,1024]{1,0:T(8,128)(2,1)S(1)}, u32[]{:S(2)}, u32[]{:S(2)}) collective-permute-start(bf16[256,1024]{1,0:T(8,128)(2,1)S(1)} %get-tuple-element.65), channel_id=1, source_target_pairs={{0,3},{1,0},{2,1},{3,2},{4,5},{5,6},{6,7},{7,4},{8,11},{9,8},{10,9... | collective-permute-start | bytes 1572872 | tf_op jit(solution)/shard_map/ppermute | solution.py:82
  38.2 22.2 %collective-permute-start.17 = (bf16[1024,512]{1,0:T(8,128)(2,1)S(1)}, bf16[1024,512]{1,0:T(8,128)(2,1)S(1)}, u32[]{:S(2)}, u32[]{:S(2)}) collective-permute-start(bf16[1024,512]{1,0:T(8,128)(2,1)S(1)} %get-tuple-element.73), channel_id=1, source_target_pairs={{0,96},{4,28},{8,104},{12,4},{16,112},{20,12},{24,120},{28,20},{32... | collective-permute-start | bytes 3145736 | tf_op jit(solution)/shard_map/ppermute | solution.py:74
  42.8 18.5 %collective-permute-start.16 = (bf16[1024,512]{1,0:T(8,128)(2,1)S(1)}, bf16[1024,512]{1,0:T(8,128)(2,1)S(1)}, u32[]{:S(2)}, u32[]{:S(2)}) collective-permute-start(bf16[1024,512]{1,0:T(8,128)(2,1)S(1)} %get-tuple-element.61.refs_6_), channel_id=1, source_target_pairs={{0,32},{4,12},{8,40},{12,20},{16,48},{20,28},{24,56},{28,4},{32,64... | collective-permute-start | bytes 3145736 | tf_op jit(solution)/shard_map/ppermute | solution.py:74
  52.0 2.6 %collective-permute-start.13 = (bf16[256,512]{1,0:T(8,128)(2,1)S(1)}, bf16[256,512]{1,0:T(8,128)(2,1)S(1)}, u32[]{:S(2)}, u32[]{:S(2)}) collective-permute-start(bf16[256,512]{1,0:T(8,128)(2,1)S(1)} %get-tuple-element.69), channel_id=1, source_target_pairs={{0,4},{4,0},{8,12},{12,8},{16,20},{20,16},{24,28},{28,24},{32,36},... | collective-permute-start | bytes 786440 | tf_op jit(solution)/shard_map/ppermute | solution.py:74
  54.6 9.9 %collective-permute-start.15 = (bf16[256,1024]{1,0:T(8,128)(2,1)S(1)}, bf16[256,1024]{1,0:T(8,128)(2,1)S(1)}, u32[]{:S(2)}, u32[]{:S(2)}) collective-permute-start(bf16[256,1024]{1,0:T(8,128)(2,1)S(1)} %get-tuple-element.71.refs_2_), channel_id=1, source_target_pairs={{0,1},{1,2},{2,3},{3,0},{4,7},{5,4},{6,5},{7,6},{8,9},{9,10},{10,1... | collective-permute-start | bytes 1572872 | tf_op jit(solution)/shard_map/ppermute | solution.py:82
  55.3 12.6 %collective-permute-start.18 = (bf16[256,512]{1,0:T(8,128)(2,1)S(1)}, bf16[256,512]{1,0:T(8,128)(2,1)S(1)}, u32[]{:S(2)}, u32[]{:S(2)}) collective-permute-start(bf16[256,512]{1,0:T(8,128)(2,1)S(1)} %get-tuple-element.77), channel_id=1, source_target_pairs={{4,0},{16,4},{12,8},{24,12},{20,16},{32,20},{28,24},{40,28},{36,32... | collective-permute-start | bytes 786440 | tf_op jit(solution)/shard_map/ppermute | solution.py:74
  55.3 13.9 %collective-permute-start.19 = (bf16[256,512]{1,0:T(8,128)(2,1)S(1)}, bf16[256,512]{1,0:T(8,128)(2,1)S(1)}, u32[]{:S(2)}, u32[]{:S(2)}) collective-permute-start(bf16[256,512]{1,0:T(8,128)(2,1)S(1)} %shard_map.109.refs_5_), channel_id=1, source_target_pairs={{8,0},{12,4},{16,8},{20,12},{24,16},{28,20},{32,24},{36,28},{40,32... | collective-permute-start | bytes 786440 | tf_op jit(solution)/shard_map/ppermute | solution.py:74
  62.3 6.9 %collective-permute-start.20 = (bf16[256,512]{1,0:T(8,128)(2,1)S(1)}, bf16[256,512]{1,0:T(8,128)(2,1)S(1)}, u32[]{:S(2)}, u32[]{:S(2)}) collective-permute-start(bf16[256,512]{1,0:T(8,128)(2,1)S(1)} %get-tuple-element.74.refs_3_), channel_id=1, source_target_pairs={{0,16},{4,68},{8,24},{12,76},{16,0},{20,84},{24,8},{28,92},{32,48}... | collective-permute-start | bytes 786440 | tf_op jit(solution)/shard_map/ppermute | solution.py:74
  64.2 8.0 %collective-permute-start.21 = (bf16[256,512]{1,0:T(8,128)(2,1)S(1)}, bf16[256,512]{1,0:T(8,128)(2,1)S(1)}, u32[]{:S(2)}, u32[]{:S(2)}) collective-permute-start(bf16[256,512]{1,0:T(8,128)(2,1)S(1)} %get-tuple-element.82), channel_id=1, source_target_pairs={{0,8},{4,36},{8,16},{12,44},{16,24},{20,52},{24,0},{28,60},{32,40}... | collective-permute-start | bytes 786440 | tf_op jit(solution)/shard_map/ppermute | solution.py:74
  64.5 9.9 %collective-permute-start.22 = (bf16[256,512]{1,0:T(8,128)(2,1)S(1)}, bf16[256,512]{1,0:T(8,128)(2,1)S(1)}, u32[]{:S(2)}, u32[]{:S(2)}) collective-permute-start(bf16[256,512]{1,0:T(8,128)(2,1)S(1)} %get-tuple-element.83), channel_id=1, source_target_pairs={{0,24},{4,100},{8,0},{12,108},{16,8},{20,116},{24,16},{28,124},{32... | collective-permute-start | bytes 786440 | tf_op jit(solution)/shard_map/ppermute | solution.py:74
  75.1 2.7 %collective-permute-start.23 = (bf16[128,512]{1,0:T(8,128)(2,1)S(1)}, bf16[128,512]{1,0:T(8,128)(2,1)S(1)}, u32[]{:S(2)}, u32[]{:S(2)}) collective-permute-start(bf16[128,512]{1,0:T(8,128)(2,1)S(1)} %get-tuple-element.86), channel_id=1, source_target_pairs={{0,4},{4,0},{8,12},{12,8},{16,20},{20,16},{24,28},{28,24},{32,36},... | collective-permute-start | bytes 393224 | tf_op jit(solution)/shard_map/ppermute | solution.py:74
  (5 other events, 23.4 us)

commit v7 on v6

--- a/solution.py
+++ b/solution.py
@@ -264,8 +264,12 @@
     weight_terms(info, g, a, ((across, 2),))
 
 
-def weight_next_kernel(info, g, a, plus, minus, own):
-    weight_terms(info, g, a, ((plus, 1), (minus, SIDE - 1), (own, 0)))
+def weight_next_kernel(info, g, a, plus, minus):
+    weight_terms(info, g, a, ((plus, 1), (minus, SIDE - 1)))
+
+
+def weight_own_kernel(info, g, a, own):
+    weight_terms(info, g, a, ((own, 0),))
 
 
 def weight_sum_kernel(info, own, from_minus, from_plus, from_across, plus, minus, across, mine):
@@ -342,9 +346,7 @@
     )(info, *here, *there, att, att_there, out_across)
     stage = ("x", "y")
     from_across = seq_send(across, by_core(stage, 2))
-    plus, minus, weight_own = call(
-        weight_next_kernel, [pieces] * 2 + [shape((4 * TOK, half), F32)], 2, us=4, smem_in=1
-    )(info, g, a)
+    plus, minus = call(weight_next_kernel, [pieces] * 2, 2, us=4, smem_in=1)(info, g, a)
     from_minus = seq_send(plus, by_core(stage, 1))
     from_plus = seq_send(minus, by_core(stage, -1))
 
@@ -372,6 +374,9 @@
     from_two = seq_send(d_two, back(NEXT_CHIP))
     out_from_same = kv_send(lax.optimization_barrier((out_same, d_two))[0], same)
 
+    weight_own = call(weight_own_kernel, shape((4 * TOK, half), F32), 2, us=1, smem_in=1, after=1)(
+        info, g, a, d_two
+    )
     strip = shape((TOK, half), BF)
     plus, minus, across, mine = call(
         weight_sum_kernel,

time: 79.3 us -> 80.1 us (1.010)
  Pallas kernels: 26.5 us -> 27.5 us
    pallas_call x1 -> x2, Pallas kernels: 2.61 us -> 3.6 us  [the longest x1 2.07 us: per_device(): call(weight_next_kernel, [pieces] * 2, 2, us=4, smem_in=1)(info, g, a)]
  transfers between devices with their start and end apart: 24 -> 24, of which waited for: 8 -> 8; matrix products, arithmetic and copies ran while one was open for 1% -> 1% of each run, Pallas kernels for 29% -> 30%
where the time goes in v7:
time: 80.1 us; the launch traced here: 79.9 us
  starting transfers between devices  31.3 us (39%)
  Pallas kernels  27.5 us (34%)
  waiting for transfers between devices  14.1 us (18%)
  local copies, waits for them, and re-layouts  5.08 us (6%)
  other arithmetic  1.06 us (1%)
    ppermute x18, starting transfers between devices, seq_send(): return lax.ppermute(v, 'seq', route)  22.9 us
    ppermute x18, waiting for transfers between devices, seq_send(): return lax.ppermute(v, 'seq', route)  11.7 us
    ppermute x6, starting transfers between devices, kv_send(): return lax.ppermute(v, ('seq', 'kv'), pairs)  8.44 us
    pallas_call x1, Pallas kernels, per_device(): call(bwd_kernel, [block, part, part, part16, part16], 9, us=6.5)  6.21 us
    unnamed x10, local copies, waits for them, and re-layouts  5.08 us
    pallas_call x1, Pallas kernels, per_device(): call(fwd_kernel, [block, shape((2, 4 * TOK), F32)], 6, us=4, scratch=[VM(...  3.57 us
    pallas_call x1, Pallas kernels, per_device(): call(attn_grad_kernel, block, 5, us=3, smem_in=1, after=1)  2.92 us
    ppermute x6, waiting for transfers between devices, kv_send(): return lax.ppermute(v, ('seq', 'kv'), pairs)  2.41 us
  transfers between devices with their start and end apart: 24, of which 8 were waited for; matrix products, arithmetic and copies ran while one was open for 1% of the time, Pallas kernels for 30%

profile of v7, /device:TPU:1, one launch (start us, length us, event | category | flops | bytes accessed | tf_op | source)
XLA Modules:
  0.0 79.9 jit_solution(9187830593089399613)
XLA Ops:
  0.6 4.7 %collective-permute-start.2 = (bf16[256,1024]{1,0:T(8,128)(2,1)}, bf16[256,1024]{1,0:T(8,128)(2,1)S(1)}, u32[]{:S(2)}, u32[]{:S(2)}) collective-permute-start(bf16[256,1024]{1,0:T(8,128)(2,1)} %refs_1_.5), channel_id=1, source_target_pairs={{0,1},{1,2},{2,3},{3,0},{4,7},{5,4},{6,5},{7,6},{8,9},{9,10},{10,1... | collective-permute-start | bytes 1572872 | tf_op jit(solution)/shard_map/ppermute | solution.py:82
  6.3 1.4 %collective-permute-start.1 = (bf16[256,512]{1,0:T(8,128)(2,1)S(1)}, bf16[256,512]{1,0:T(8,128)(2,1)S(1)}, u32[]{:S(2)}, u32[]{:S(2)}) collective-permute-start(bf16[256,512]{1,0:T(8,128)(2,1)S(1)} %pad_add_fusion.refs_2_), channel_id=1, source_target_pairs={{0,8},{4,12},{8,16},{12,20},{16,24},{20,28},{24,32},{28,36},{32,40... | collective-permute-start | bytes 786440 | tf_op jit(solution)/shard_map/ppermute | solution.py:74
  7.6 1.6 %collective-permute-start = (bf16[256,512]{1,0:T(8,128)(2,1)S(1)}, bf16[256,512]{1,0:T(8,128)(2,1)S(1)}, u32[]{:S(2)}, u32[]{:S(2)}) collective-permute-start(bf16[256,512]{1,0:T(8,128)(2,1)S(1)} %pad_add_fusion.refs_2_), channel_id=1, source_target_pairs={{0,4},{4,16},{8,12},{12,24},{16,20},{20,32},{24,28},{28,40},{32,36... | collective-permute-start | bytes 786440 | tf_op jit(solution)/shard_map/ppermute | solution.py:74
  9.3 1.6 %collective-permute-start.4 = (bf16[256,1024]{1,0:T(8,128)(2,1)}, bf16[256,1024]{1,0:T(8,128)(2,1)S(1)}, u32[]{:S(2)}, u32[]{:S(2)}) collective-permute-start(bf16[256,1024]{1,0:T(8,128)(2,1)} %refs_1_.5), channel_id=1, source_target_pairs={{0,3},{1,0},{2,1},{3,2},{4,5},{5,6},{6,7},{7,4},{8,11},{9,8},{10,9... | collective-permute-start | bytes 1572872 | tf_op jit(solution)/shard_map/ppermute | solution.py:82
  11.0 3.4 %copy-done = bf16[4096,1024]{1,0:T(8,128)(2,1)S(1)} copy-done((bf16[4096,1024]{1,0:T(8,128)(2,1)S(1)}, bf16[4096,1024]{1,0:T(8,128)(2,1)}, u32[]{:S(2)}) %copy-start) | copy-done | bytes 8388632
  17.3 2.5 %collective-permute-done.1.refs_3_ = bf16[256,512]{1,0:T(8,128)(2,1)S(1)} collective-permute-done((bf16[256,512]{1,0:T(8,128)(2,1)S(1)}, bf16[256,512]{1,0:T(8,128)(2,1)S(1)}, u32[]{:S(2)}, u32[]{:S(2)}) %collective-permute-start.1) | collective-permute-done | bytes 262176 | tf_op jit(solution)/shard_map/ppermute | solution.py:74
  21.4 3.6 %shard_map.102 = (bf16[256,1024]{1,0:T(8,128)(2,1)S(1)}, f32[2,1024]{1,0:T(2,128)S(1)}) custom-call(bf16[2,1024,128]{2,1,0:T(8,128)(2,1)S(1)} %get-tuple-element.47.refs_0_, f32[4,256,256]{2,1,0:T(8,128)S(1)} %get-tuple-element.48.refs_1_, bf16[256,512]{1,0:T(8,128)(2,1)S(1)} %pad_add_fusion.refs_2_, bf16[256,512]{1,0:T(8,128)(2,1)S(1)} %collective-permute-done.1.refs_3_, ...), custom_call_target="tpu_custom_call" | custom-call | bytes 200000 | tf_op jit(solution)/shard_map/pallas_call | solution.py:323
  25.7 2.4 %collective-permute-done.5.refs_4_ = bf16[256,1024]{1,0:T(8,128)(2,1)S(1)} collective-permute-done((bf16[256,1024]{1,0:T(8,128)(2,1)S(1)}, bf16[256,1024]{1,0:T(8,128)(2,1)S(1)}, u32[]{:S(2)}, u32[]{:S(2)}) %collective-permute-start.5) | collective-permute-done | bytes 524320 | tf_op jit(solution)/shard_map/ppermute | solution.py:82
  28.1 2.3 %collective-permute-start.9 = (bf16[256,1024]{1,0:T(8,128)(2,1)S(1)}, bf16[256,1024]{1,0:T(8,128)(2,1)S(1)}, u32[]{:S(2)}, u32[]{:S(2)}) collective-permute-start(bf16[256,1024]{1,0:T(8,128)(2,1)S(1)} %collective-permute-done.5.refs_4_), channel_id=1, source_target_pairs={{0,4},{4,0},{8,12},{12,8},{16,20},{20,16},{24,28},{28,24},{32,36},... | collective-permute-start | bytes 1572872 | tf_op jit(solution)/shard_map/ppermute | solution.py:74
  30.4 1.8 %shard_map.103 = (bf16[256,1024]{1,0:T(8,128)(2,1)S(1)}, bf16[256,1024]{1,0:T(8,128)(2,1)S(1)}) custom-call(s32[2]{0:T(128)S(1)} %pad_add_fusion.1.refs_0_, bf16[256,1024]{1,0:T(8,128)(2,1)S(1)} %get-tuple-element.51.refs_1_.refs_9_.refs_7_, bf16[4096,1024]{1,0:T(8,128)(2,1)S(1)} %copy-done.1), custom_call_target="tpu_custom_call" | custom-call | bytes 100000 | tf_op jit(solution)/shard_map/pallas_call | solution.py:334
  32.3 1.6 %shard_map.104 = (bf16[1024,512]{1,0:T(8,128)(2,1)S(1)}, bf16[4,512,1024]{2,1,0:T(8,128)(2,1)S(1)}, bf16[512,512]{1,0:T(8,128)(2,1)S(1)}) custom-call(s32[2]{0:T(128)S(1)} %pad_add_fusion.1.refs_0_, bf16[256,1024]{1,0:T(8,128)(2,1)S(1)} %copy-done.2, bf16[256,1024]{1,0:T(8,128)(2,1)S(1)} %collective-permute-done.2.refs_2_, ...), custom_call_target="tpu_custom_call" | custom-call | bytes 200000 | tf_op jit(solution)/shard_map/pallas_call | solution.py:339
  34.1 2.1 %shard_map.105 = (bf16[1024,512]{1,0:T(8,128)(2,1)S(1)}, bf16[1024,512]{1,0:T(8,128)(2,1)S(1)}) custom-call(s32[2]{0:T(128)S(1)} %pad_add_fusion.1.refs_0_, bf16[4,512,1024]{2,1,0:T(8,128)(2,1)S(1)} %get-tuple-element.58.refs_1_, bf16[512,512]{1,0:T(8,128)(2,1)S(1)} %get-tuple-element.59.refs_2_), custom_call_target="tpu_custom_call" | custom-call | bytes 200000 | tf_op jit(solution)/shard_map/pallas_call | solution.py:349
  37.7 4.6 %collective-permute-start.17 = (bf16[1024,512]{1,0:T(8,128)(2,1)S(1)}, bf16[1024,512]{1,0:T(8,128)(2,1)S(1)}, u32[]{:S(2)}, u32[]{:S(2)}) collective-permute-start(bf16[1024,512]{1,0:T(8,128)(2,1)S(1)} %get-tuple-element.71), channel_id=1, source_target_pairs={{0,96},{4,28},{8,104},{12,4},{16,112},{20,12},{24,120},{28,20},{32... | collective-permute-start | bytes 3145736 | tf_op jit(solution)/shard_map/ppermute | solution.py:74
  42.3 2.9 %shard_map.106.refs_8_ = bf16[256,1024]{1,0:T(8,128)(2,1)S(1)} custom-call(s32[2]{0:T(128)S(1)} %pad_add_fusion.1.refs_0_, bf16[256,1024]{1,0:T(8,128)(2,1)S(1)} %copy-done.2, bf16[256,1024]{1,0:T(8,128)(2,1)S(1)} %collective-permute-done.2.refs_2_, bf16[256,1024]{1,0:T(8,128)(2,1)S(1)} %collective-permute-done.4.refs_3_, ...), custom_call_target="tpu_custom_call" | custom-call | bytes 150000 | tf_op jit(solution)/shard_map/pallas_call | solution.py:357
  45.2 6.2 %shard_map.107 = (bf16[256,1024]{1,0:T(8,128)(2,1)}, f32[256,512]{1,0:T(8,128)S(1)}, f32[256,512]{1,0:T(8,128)S(1)}, bf16[256,512]{1,0:T(8,128)(2,1)S(1)}, bf16[256,512]{1,0:T(8,128)(2,1)S(1)}) custom-call(bf16[2,1024,128]{2,1,0:T(8,128)(2,1)S(1)} %get-tuple-element.47.refs_0_, f32[4,256,256]{2,1,0:T(8,128)S(1)} %get-tuple-element.48.refs_1_, ...), custom_call_target="tpu_custom_call" | custom-call | bytes 325000 | tf_op jit(solution)/shard_map/pallas_call | solution.py:363
  52.2 1.9 %shard_map.108 = (bf16[256,1024]{1,0:T(8,128)(2,1)S(1)}, f32[256,1024]{1,0:T(8,128)S(1)}) custom-call(s32[2]{0:T(128)S(1)} %pad_add_fusion.1.refs_0_, bf16[256,1024]{1,0:T(8,128)(2,1)S(1)} %get-tuple-element.51.refs_1_.refs_9_.refs_7_, bf16[4096,1024]{1,0:T(8,128)(2,1)S(1)} %copy-done.1, bf16[256,1024]{1,0:T(8,128)(2,1)S(1)} %collective-permute-done.11.refs_3_, ...), custom_call_target="tpu_custom_call" | custom-call | bytes 100000 | tf_op jit(solution)/shard_map/pallas_call | solution.py:368
  54.7 1.5 %shard_map.110.refs_1_ = f32[1024,512]{1,0:T(8,128)S(1)} custom-call(s32[2]{0:T(128)S(1)} %pad_add_fusion.1.refs_0_, bf16[4,512,1024]{2,1,0:T(8,128)(2,1)S(1)} %get-tuple-element.58.refs_1_, bf16[512,512]{1,0:T(8,128)(2,1)S(1)} %get-tuple-element.59.refs_2_, bf16[256,512]{1,0:T(8,128)(2,1)S(1)} %shard_map.109.refs_3_.refs_5_), custom_call_target="tpu_custom_call" | custom-call | bytes 50000 | tf_op jit(solution)/shard_map/pallas_call | solution.py:377
  56.2 5.3 %collective-permute-start.19 = (bf16[256,512]{1,0:T(8,128)(2,1)S(1)}, bf16[256,512]{1,0:T(8,128)(2,1)S(1)}, u32[]{:S(2)}, u32[]{:S(2)}) collective-permute-start(bf16[256,512]{1,0:T(8,128)(2,1)S(1)} %shard_map.109.refs_3_.refs_5_), channel_id=1, source_target_pairs={{8,0},{12,4},{16,8},{20,12},{24,16},{28,20},{32,24},{36,28},{40,32... | collective-permute-start | bytes 786440 | tf_op jit(solution)/shard_map/ppermute | solution.py:74
  62.8 1.4 %collective-permute-start.20 = (bf16[256,512]{1,0:T(8,128)(2,1)S(1)}, bf16[256,512]{1,0:T(8,128)(2,1)S(1)}, u32[]{:S(2)}, u32[]{:S(2)}) collective-permute-start(bf16[256,512]{1,0:T(8,128)(2,1)S(1)} %get-tuple-element.72.refs_3_), channel_id=1, source_target_pairs={{0,16},{4,68},{8,24},{12,76},{16,0},{20,84},{24,8},{28,92},{32,48}... | collective-permute-start | bytes 786440 | tf_op jit(solution)/shard_map/ppermute | solution.py:74
  64.5 2.4 %collective-permute-start.22 = (bf16[256,512]{1,0:T(8,128)(2,1)S(1)}, bf16[256,512]{1,0:T(8,128)(2,1)S(1)}, u32[]{:S(2)}, u32[]{:S(2)}) collective-permute-start(bf16[256,512]{1,0:T(8,128)(2,1)S(1)} %get-tuple-element.81), channel_id=1, source_target_pairs={{0,24},{4,100},{8,0},{12,108},{16,8},{20,116},{24,16},{28,124},{32... | collective-permute-start | bytes 786440 | tf_op jit(solution)/shard_map/ppermute | solution.py:74
  67.8 1.9 %collective-permute-done.20.refs_4_.refs_2_ = bf16[256,512]{1,0:T(8,128)(2,1)S(1)} collective-permute-done((bf16[256,512]{1,0:T(8,128)(2,1)S(1)}, bf16[256,512]{1,0:T(8,128)(2,1)S(1)}, u32[]{:S(2)}, u32[]{:S(2)}) %collective-permute-start.20) | collective-permute-done | bytes 262176 | tf_op jit(solution)/shard_map/ppermute | solution.py:74
  70.5 2.3 %collective-permute-done.21.refs_3_ = bf16[256,512]{1,0:T(8,128)(2,1)S(1)} collective-permute-done((bf16[256,512]{1,0:T(8,128)(2,1)S(1)}, bf16[256,512]{1,0:T(8,128)(2,1)S(1)}, u32[]{:S(2)}, u32[]{:S(2)}) %collective-permute-start.21) | collective-permute-done | bytes 262176 | tf_op jit(solution)/shard_map/ppermute | solution.py:74
  72.7 2.8 %collective-permute-done.22.refs_4_ = bf16[256,512]{1,0:T(8,128)(2,1)S(1)} collective-permute-done((bf16[256,512]{1,0:T(8,128)(2,1)S(1)}, bf16[256,512]{1,0:T(8,128)(2,1)S(1)}, u32[]{:S(2)}, u32[]{:S(2)}) %collective-permute-start.22) | collective-permute-done | bytes 262176 | tf_op jit(solution)/shard_map/ppermute | solution.py:74
  76.2 1.5 %collective-permute-start.23 = (bf16[128,512]{1,0:T(8,128)(2,1)S(1)}, bf16[128,512]{1,0:T(8,128)(2,1)S(1)}, u32[]{:S(2)}, u32[]{:S(2)}) collective-permute-start(bf16[128,512]{1,0:T(8,128)(2,1)S(1)} %get-tuple-element.84), channel_id=1, source_target_pairs={{0,4},{4,0},{8,12},{12,8},{16,20},{20,16},{24,28},{28,24},{32,36},... | collective-permute-start | bytes 393224 | tf_op jit(solution)/shard_map/ppermute | solution.py:74
  (51 shorter events, 15.6 us)
Async XLA Ops:
  0.6 19.2 %collective-permute-start.2 = (bf16[256,1024]{1,0:T(8,128)(2,1)}, bf16[256,1024]{1,0:T(8,128)(2,1)S(1)}, u32[]{:S(2)}, u32[]{:S(2)}) collective-permute-start(bf16[256,1024]{1,0:T(8,128)(2,1)} %refs_1_.5), channel_id=1, source_target_pairs={{0,1},{1,2},{2,3},{3,0},{4,7},{5,4},{6,5},{7,6},{8,9},{9,10},{10,1... | collective-permute-start | bytes 1572872 | tf_op jit(solution)/shard_map/ppermute | solution.py:82
  6.3 13.5 %collective-permute-start.1 = (bf16[256,512]{1,0:T(8,128)(2,1)S(1)}, bf16[256,512]{1,0:T(8,128)(2,1)S(1)}, u32[]{:S(2)}, u32[]{:S(2)}) collective-permute-start(bf16[256,512]{1,0:T(8,128)(2,1)S(1)} %pad_add_fusion.refs_2_), channel_id=1, source_target_pairs={{0,8},{4,12},{8,16},{12,20},{16,24},{20,28},{24,32},{28,36},{32,40... | collective-permute-start | bytes 786440 | tf_op jit(solution)/shard_map/ppermute | solution.py:74
  7.6 12.2 %collective-permute-start = (bf16[256,512]{1,0:T(8,128)(2,1)S(1)}, bf16[256,512]{1,0:T(8,128)(2,1)S(1)}, u32[]{:S(2)}, u32[]{:S(2)}) collective-permute-start(bf16[256,512]{1,0:T(8,128)(2,1)S(1)} %pad_add_fusion.refs_2_), channel_id=1, source_target_pairs={{0,4},{4,16},{8,12},{12,24},{16,20},{20,32},{24,28},{28,40},{32,36... | collective-permute-start | bytes 786440 | tf_op jit(solution)/shard_map/ppermute | solution.py:74
  9.3 16.0 %collective-permute-start.4 = (bf16[256,1024]{1,0:T(8,128)(2,1)}, bf16[256,1024]{1,0:T(8,128)(2,1)S(1)}, u32[]{:S(2)}, u32[]{:S(2)}) collective-permute-start(bf16[256,1024]{1,0:T(8,128)(2,1)} %refs_1_.5), channel_id=1, source_target_pairs={{0,3},{1,0},{2,1},{3,2},{4,5},{5,6},{6,7},{7,4},{8,11},{9,8},{10,9... | collective-permute-start | bytes 1572872 | tf_op jit(solution)/shard_map/ppermute | solution.py:82
  19.8 8.3 %collective-permute-start.5 = (bf16[256,1024]{1,0:T(8,128)(2,1)S(1)}, bf16[256,1024]{1,0:T(8,128)(2,1)S(1)}, u32[]{:S(2)}, u32[]{:S(2)}) collective-permute-start(bf16[256,1024]{1,0:T(8,128)(2,1)S(1)} %collective-permute-done.2.refs_2_), channel_id=1, source_target_pairs={{0,1},{1,2},{2,3},{3,0},{4,7},{5,4},{6,5},{7,6},{8,9},{9,10},{10,1... | collective-permute-start | bytes 1572872 | tf_op jit(solution)/shard_map/ppermute | solution.py:82
  19.8 1.6 %collective-permute-start.3 = (bf16[256,512]{1,0:T(8,128)(2,1)S(1)}, bf16[256,512]{1,0:T(8,128)(2,1)S(1)}, u32[]{:S(2)}, u32[]{:S(2)}) collective-permute-start(bf16[256,512]{1,0:T(8,128)(2,1)S(1)} %collective-permute-done.1.refs_3_), channel_id=1, source_target_pairs={{0,4},{4,0},{8,12},{12,8},{16,20},{20,16},{24,28},{28,24},{32,36},... | collective-permute-start | bytes 786440 | tf_op jit(solution)/shard_map/ppermute | solution.py:74
  20.0 12.2 %collective-permute-start.6 = (bf16[256,1024]{1,0:T(8,128)(2,1)S(1)}, bf16[256,1024]{1,0:T(8,128)(2,1)S(1)}, u32[]{:S(2)}, u32[]{:S(2)}) collective-permute-start(bf16[256,1024]{1,0:T(8,128)(2,1)S(1)} %copy-done.2), channel_id=1, source_target_pairs={{0,4},{4,0},{8,12},{12,8},{16,20},{20,16},{24,28},{28,24},{32,36},... | collective-permute-start | bytes 1572872 | tf_op jit(solution)/shard_map/ppermute | solution.py:74
  25.0 7.3 %collective-permute-start.10 = (bf16[256,1024]{1,0:T(8,128)(2,1)S(1)}, bf16[256,1024]{1,0:T(8,128)(2,1)S(1)}, u32[]{:S(2)}, u32[]{:S(2)}) collective-permute-start(bf16[256,1024]{1,0:T(8,128)(2,1)S(1)} %get-tuple-element.51.refs_1_.refs_9_.refs_7_), channel_id=1, source_target_pairs={{0,4},{4,0},{8,12},{12,8},{16,20},{20,16},{24,28},{28,24},{32,36},... | collective-permute-start | bytes 1572872 | tf_op jit(solution)/shard_map/ppermute | solution.py:74
  25.2 7.0 %collective-permute-start.7 = (bf16[256,1024]{1,0:T(8,128)(2,1)S(1)}, bf16[256,1024]{1,0:T(8,128)(2,1)S(1)}, u32[]{:S(2)}, u32[]{:S(2)}) collective-permute-start(bf16[256,1024]{1,0:T(8,128)(2,1)S(1)} %collective-permute-done.2.refs_2_), channel_id=1, source_target_pairs={{0,4},{4,0},{8,12},{12,8},{16,20},{20,16},{24,28},{28,24},{32,36},... | collective-permute-start | bytes 1572872 | tf_op jit(solution)/shard_map/ppermute | solution.py:74
  25.6 6.7 %collective-permute-start.8 = (bf16[256,1024]{1,0:T(8,128)(2,1)S(1)}, bf16[256,1024]{1,0:T(8,128)(2,1)S(1)}, u32[]{:S(2)}, u32[]{:S(2)}) collective-permute-start(bf16[256,1024]{1,0:T(8,128)(2,1)S(1)} %collective-permute-done.4.refs_3_), channel_id=1, source_target_pairs={{0,4},{4,0},{8,12},{12,8},{16,20},{20,16},{24,28},{28,24},{32,36},... | collective-permute-start | bytes 1572872 | tf_op jit(solution)/shard_map/ppermute | solution.py:74
  28.1 4.2 %collective-permute-start.9 = (bf16[256,1024]{1,0:T(8,128)(2,1)S(1)}, bf16[256,1024]{1,0:T(8,128)(2,1)S(1)}, u32[]{:S(2)}, u32[]{:S(2)}) collective-permute-start(bf16[256,1024]{1,0:T(8,128)(2,1)S(1)} %collective-permute-done.5.refs_4_), channel_id=1, source_target_pairs={{0,4},{4,0},{8,12},{12,8},{16,20},{20,16},{24,28},{28,24},{32,36},... | collective-permute-start | bytes 1572872 | tf_op jit(solution)/shard_map/ppermute | solution.py:74
  33.9 20.1 %collective-permute-start.14 = (bf16[1024,512]{1,0:T(8,128)(2,1)S(1)}, bf16[1024,512]{1,0:T(8,128)(2,1)S(1)}, u32[]{:S(2)}, u32[]{:S(2)}) collective-permute-start(bf16[1024,512]{1,0:T(8,128)(2,1)S(1)} %get-tuple-element.69), channel_id=1, source_target_pairs={{0,64},{4,20},{8,72},{12,28},{16,80},{20,4},{24,88},{28,12},{32,96... | collective-permute-start | bytes 3145736 | tf_op jit(solution)/shard_map/ppermute | solution.py:74
  36.2 15.2 %collective-permute-start.11 = (bf16[256,1024]{1,0:T(8,128)(2,1)S(1)}, bf16[256,1024]{1,0:T(8,128)(2,1)S(1)}, u32[]{:S(2)}, u32[]{:S(2)}) collective-permute-start(bf16[256,1024]{1,0:T(8,128)(2,1)S(1)} %get-tuple-element.61.refs_11_), channel_id=1, source_target_pairs={{0,1},{1,2},{2,3},{3,0},{4,7},{5,4},{6,5},{7,6},{8,9},{9,10},{10,1... | collective-permute-start | bytes 1572872 | tf_op jit(solution)/shard_map/ppermute | solution.py:82
  36.4 15.8 %collective-permute-start.12 = (bf16[256,1024]{1,0:T(8,128)(2,1)S(1)}, bf16[256,1024]{1,0:T(8,128)(2,1)S(1)}, u32[]{:S(2)}, u32[]{:S(2)}) collective-permute-start(bf16[256,1024]{1,0:T(8,128)(2,1)S(1)} %get-tuple-element.64), channel_id=1, source_target_pairs={{0,3},{1,0},{2,1},{3,2},{4,5},{5,6},{6,7},{7,4},{8,11},{9,8},{10,9... | collective-permute-start | bytes 1572872 | tf_op jit(solution)/shard_map/ppermute | solution.py:82
  37.7 23.9 %collective-permute-start.17 = (bf16[1024,512]{1,0:T(8,128)(2,1)S(1)}, bf16[1024,512]{1,0:T(8,128)(2,1)S(1)}, u32[]{:S(2)}, u32[]{:S(2)}) collective-permute-start(bf16[1024,512]{1,0:T(8,128)(2,1)S(1)} %get-tuple-element.71), channel_id=1, source_target_pairs={{0,96},{4,28},{8,104},{12,4},{16,112},{20,12},{24,120},{28,20},{32... | collective-permute-start | bytes 3145736 | tf_op jit(solution)/shard_map/ppermute | solution.py:74
  42.2 19.6 %collective-permute-start.16 = (bf16[1024,512]{1,0:T(8,128)(2,1)S(1)}, bf16[1024,512]{1,0:T(8,128)(2,1)S(1)}, u32[]{:S(2)}, u32[]{:S(2)}) collective-permute-start(bf16[1024,512]{1,0:T(8,128)(2,1)S(1)} %get-tuple-element.60.refs_6_), channel_id=1, source_target_pairs={{0,32},{4,12},{8,40},{12,20},{16,48},{20,28},{24,56},{28,4},{32,64... | collective-permute-start | bytes 3145736 | tf_op jit(solution)/shard_map/ppermute | solution.py:74
  51.4 2.6 %collective-permute-start.13 = (bf16[256,512]{1,0:T(8,128)(2,1)S(1)}, bf16[256,512]{1,0:T(8,128)(2,1)S(1)}, u32[]{:S(2)}, u32[]{:S(2)}) collective-permute-start(bf16[256,512]{1,0:T(8,128)(2,1)S(1)} %get-tuple-element.68), channel_id=1, source_target_pairs={{0,4},{4,0},{8,12},{12,8},{16,20},{20,16},{24,28},{28,24},{32,36},... | collective-permute-start | bytes 786440 | tf_op jit(solution)/shard_map/ppermute | solution.py:74
  54.1 10.4 %collective-permute-start.15 = (bf16[256,1024]{1,0:T(8,128)(2,1)S(1)}, bf16[256,1024]{1,0:T(8,128)(2,1)S(1)}, u32[]{:S(2)}, u32[]{:S(2)}) collective-permute-start(bf16[256,1024]{1,0:T(8,128)(2,1)S(1)} %get-tuple-element.70.refs_2_), channel_id=1, source_target_pairs={{0,1},{1,2},{2,3},{3,0},{4,7},{5,4},{6,5},{7,6},{8,9},{9,10},{10,1... | collective-permute-start | bytes 1572872 | tf_op jit(solution)/shard_map/ppermute | solution.py:82
  54.7 13.1 %collective-permute-start.18 = (bf16[256,512]{1,0:T(8,128)(2,1)S(1)}, bf16[256,512]{1,0:T(8,128)(2,1)S(1)}, u32[]{:S(2)}, u32[]{:S(2)}) collective-permute-start(bf16[256,512]{1,0:T(8,128)(2,1)S(1)} %get-tuple-element.75), channel_id=1, source_target_pairs={{4,0},{16,4},{12,8},{24,12},{20,16},{32,20},{28,24},{40,28},{36,32... | collective-permute-start | bytes 786440 | tf_op jit(solution)/shard_map/ppermute | solution.py:74
  56.2 11.6 %collective-permute-start.19 = (bf16[256,512]{1,0:T(8,128)(2,1)S(1)}, bf16[256,512]{1,0:T(8,128)(2,1)S(1)}, u32[]{:S(2)}, u32[]{:S(2)}) collective-permute-start(bf16[256,512]{1,0:T(8,128)(2,1)S(1)} %shard_map.109.refs_3_.refs_5_), channel_id=1, source_target_pairs={{8,0},{12,4},{16,8},{20,12},{24,16},{28,20},{32,24},{36,28},{40,32... | collective-permute-start | bytes 786440 | tf_op jit(solution)/shard_map/ppermute | solution.py:74
  62.8 6.9 %collective-permute-start.20 = (bf16[256,512]{1,0:T(8,128)(2,1)S(1)}, bf16[256,512]{1,0:T(8,128)(2,1)S(1)}, u32[]{:S(2)}, u32[]{:S(2)}) collective-permute-start(bf16[256,512]{1,0:T(8,128)(2,1)S(1)} %get-tuple-element.72.refs_3_), channel_id=1, source_target_pairs={{0,16},{4,68},{8,24},{12,76},{16,0},{20,84},{24,8},{28,92},{32,48}... | collective-permute-start | bytes 786440 | tf_op jit(solution)/shard_map/ppermute | solution.py:74
  64.2 8.5 %collective-permute-start.21 = (bf16[256,512]{1,0:T(8,128)(2,1)S(1)}, bf16[256,512]{1,0:T(8,128)(2,1)S(1)}, u32[]{:S(2)}, u32[]{:S(2)}) collective-permute-start(bf16[256,512]{1,0:T(8,128)(2,1)S(1)} %get-tuple-element.80), channel_id=1, source_target_pairs={{0,8},{4,36},{8,16},{12,44},{16,24},{20,52},{24,0},{28,60},{32,40}... | collective-permute-start | bytes 786440 | tf_op jit(solution)/shard_map/ppermute | solution.py:74
  64.5 11.0 %collective-permute-start.22 = (bf16[256,512]{1,0:T(8,128)(2,1)S(1)}, bf16[256,512]{1,0:T(8,128)(2,1)S(1)}, u32[]{:S(2)}, u32[]{:S(2)}) collective-permute-start(bf16[256,512]{1,0:T(8,128)(2,1)S(1)} %get-tuple-element.81), channel_id=1, source_target_pairs={{0,24},{4,100},{8,0},{12,108},{16,8},{20,116},{24,16},{28,124},{32... | collective-permute-start | bytes 786440 | tf_op jit(solution)/shard_map/ppermute | solution.py:74
  76.2 2.4 %collective-permute-start.23 = (bf16[128,512]{1,0:T(8,128)(2,1)S(1)}, bf16[128,512]{1,0:T(8,128)(2,1)S(1)}, u32[]{:S(2)}, u32[]{:S(2)}) collective-permute-start(bf16[128,512]{1,0:T(8,128)(2,1)S(1)} %get-tuple-element.84), channel_id=1, source_target_pairs={{0,4},{4,0},{8,12},{12,8},{16,20},{20,16},{24,28},{28,24},{32,36},... | collective-permute-start | bytes 393224 | tf_op jit(solution)/shard_map/ppermute | solution.py:74
  (5 other events, 23.4 us)
